TPU v7x, 32 devices: a whole 2x2x4 slice. The times are simulated.
32 devices in a mesh: tm: 16 (over z, y, x), inp: 2 (over core).
Axes of the slice: x: 2, y: 2, z: 4, core: 2. Of those that a mesh axis runs over, the one named last changes fastest.
Arguments:
- voltages: bfloat16 [2, 65536, 1024], P(None, 'tm', 'inp'), may hold values from -127 to 127, as said below
- taps: int32 [12, 1024], replicated, may hold values from -64 to 64
Outputs:
- visibility: bfloat16 [512, 1024, 1024], P(('tm', 'inp'))
Inputs may be any that keep to these rules, and one draw needn't show every extreme that they name: `voltages`: every sample is a whole number.
All inputs are finite; a program needn't handle non-finite values.
Results may differ from a plain program's by a relative error of at most 0.0048.
Values may be sent and summed in bfloat16 or wider, within the bound.
No kernel may reach another device: no remote copies, remote signals or barrier semaphores. Data moves between devices by JAX's collectives and lax.ppermute only.
A program may use at most 576 MiB of HBM per device.

v0:
```python
import math

import jax
import jax.numpy as jnp
from jax import lax
from jax.sharding import PartitionSpec as P

KEEP = 512


def passed_along(value, axis, steps):
    count = lax.axis_size(axis)
    first, last = (max(0, -steps), min(count, count - steps))
    return lax.ppermute(value, axis, [(source, source + steps) for source in range(first, last)])


def dft_table(fine_count, keep_count):
    branch = jnp.arange(fine_count, dtype=jnp.int32)[:, None]
    channel = jnp.arange(keep_count, dtype=jnp.int32)[None, :] - keep_count // 2
    phase_index = jnp.mod(branch * channel, fine_count).astype(jnp.float32)
    angles = 2.0 * math.pi / fine_count * phase_index
    norm_scale = 1.0 / math.sqrt(fine_count)
    cosine = jnp.cos(angles) * norm_scale
    sine_part = jnp.sin(angles) * norm_scale
    dft_matrix = jnp.stack(
        [jnp.stack([cosine, -sine_part], 1), jnp.stack([sine_part, cosine], 1)], 0
    )
    return dft_matrix.astype(jnp.bfloat16)


def finish(products, chan_count, all_inputs, spec_total):
    visibility = products.reshape(chan_count, 2, all_inputs, all_inputs) * (1.0 / spec_total)
    upper_mask = jnp.arange(all_inputs)[:, None] <= jnp.arange(all_inputs)[None, :]
    return jnp.where(upper_mask[None], visibility[:, 0], visibility[:, 1]).astype(jnp.bfloat16)


def per_device(voltages, taps):
    history_len = taps.shape[0] - 1
    fine_count = taps.shape[1]
    frames = voltages.shape[1] // fine_count
    input_width = voltages.shape[2]
    keep_count = KEEP
    coefficient = taps.astype(jnp.float32)
    dft_matrix = dft_table(fine_count, keep_count)
    n_time = lax.axis_size("tm")
    n_group = lax.axis_size("inp")
    chan_count = keep_count // (n_time * n_group)
    all_inputs = n_group * input_width
    spec_total = n_time * frames
    own_frames = voltages.reshape(2, frames, fine_count, input_width)
    pieces = [own_frames]
    remaining = history_len
    shift_count = (history_len + frames - 1) // frames
    for offset in range(1, shift_count + 1):
        take_count = min(remaining, frames)
        received = passed_along(own_frames[:, frames - take_count :], "tm", offset)
        pieces.insert(0, received)
        remaining = remaining - take_count
    extended = jnp.concatenate(pieces, axis=1)
    filtered = coefficient[0][None, None, :, None] * extended[
        :, history_len : history_len + frames
    ].astype(jnp.float32)
    for k in range(1, history_len + 1):
        filtered = filtered + coefficient[k][None, None, :, None] * extended[
            :, history_len - k : history_len - k + frames
        ].astype(jnp.float32)
    filtered = (filtered * (1.0 / 8192.0)).astype(jnp.bfloat16)
    spectra = jnp.einsum(
        "rfna,rnsj->jsfa", filtered, dft_matrix, preferred_element_type=jnp.float32
    ).astype(jnp.bfloat16)
    flat_spectra = spectra.reshape(keep_count, 2, frames * input_width)
    exchanged = lax.all_to_all(flat_spectra, ("tm", "inp"), split_axis=0, concat_axis=2, tiled=True)
    channel_grid = exchanged.reshape(chan_count, 2, n_time, n_group, frames, input_width)
    einsum_form = "crtgfa,csrthfb->csgahb"
    rotated = jnp.stack([-channel_grid[:, 1], channel_grid[:, 0]], axis=1)
    turned = jnp.stack([channel_grid, rotated], axis=1)
    products = jnp.einsum(einsum_form, channel_grid, turned, preferred_element_type=jnp.float32)
    return finish(products, chan_count, all_inputs, spec_total)


def solution(mesh):
    placed = (P(None, "tm", "inp"), P())
    return jax.shard_map(
        per_device,
        mesh=mesh,
        in_specs=placed,
        out_specs=P(("tm", "inp"), None, None),
        check_vma=False,
    )
```

profile of v0, /device:TPU:0, one launch (start us, length us, event | category | flops | bytes accessed | tf_op | source)
XLA Modules:
  0.0 1050.1 jit_solution(5953344357083101981)
XLA Ops:
  0.0 11.5 %copy.26 = bf16[2,4,1024,512]{2,3,0,1:T(8,128)(2,1)} copy(bf16[2,4,1024,512]{3,2,1,0:T(8,128)(2,1)} %bitcast.91) | data formatting | bytes 16777216 | tf_op jit(solution)/shard_map/reshape | solution.py:50
  11.5 5.5 collective-permute-start.1
  17.0 3.9 collective-permute-start
  21.0 6.9 slice.130
  27.8 5.9 collective-permute-start.2
  33.8 8.8 negate_convert_fusion
  44.3 290.7 %collective-permute-done.2 = bf16[2,3,1024,512]{2,3,0,1:T(8,128)(2,1)} collective-permute-done((bf16[2,3,1024,512]{2,3,0,1:T(8,128)(2,1)}, bf16[2,3,1024,512]{2,3,0,1:T(8,128)(2,1)}, u32[]{:S(2)}, u32[]{:S(2)}) %collective-permute-start.2) | collective-permute-done | bytes 6291488 | tf_op jit(solution)/shard_map/ppermute | solution.py:14
  335.0 6.8 constant_dynamic-update-slice_fusion.3
  341.8 34.5 %collective-permute-done.1 = bf16[2,4,1024,512]{2,3,0,1:T(8,128)(2,1)S(1)} collective-permute-done((bf16[2,4,1024,512]{2,3,0,1:T(8,128)(2,1)}, bf16[2,4,1024,512]{2,3,0,1:T(8,128)(2,1)S(1)}, u32[]{:S(2)}, u32[]{:S(2)}) %collective-permute-start.1) | collective-permute-done | bytes 8388640 | tf_op jit(solution)/shard_map/ppermute | solution.py:14
  376.3 7.5 constant_dynamic-update-slice_fusion.1
  388.1 7.8 constant_dynamic-update-slice_fusion
  395.9 38.7 %bitcast_convert_fusion = bf16[2,512,4,512]{1,3,2,0:T(8,128)(2,1)} fusion(bf16[2,7,1024,512]{2,3,0,1:T(8,128)(2,1)} %get-tuple-element.6, f32[1024]{0:T(1024)S(1)} %bitcast.94, f32[1024]{0:T(1024)S(1)} %bitcast.95, f32[1024]{0:T(1024)S(1)} %bitcast.96, bf16[2,4,1024,512]{2,3,0,1:T(8,128)(2,1)} %copy-done.2, f32[1024]{0:T(1024)S(1)} %bitcast.97, ...), kind=kOutput, calls=%fused_computation.17 | convolution fusion | flops 8793358336 | bytes 83935232 | tf_op jit(solution)/shard_map/rfna,rnsj->jsfa/dot_general | solution.py:68
  434.6 11.3 %copy.31 = bf16[512,2,2048]{2,1,0:T(2,128)(2,1)} copy(bf16[512,2,2048]{0,2,1:T(8,128)(2,1)} %bitcast.92) | data formatting | bytes 8388608 | tf_op jit(solution)/shard_map/reshape | solution.py:71
  445.8 148.7 %all-to-all-start = ((bf16[512,2,2048]{2,1,0:T(2,128)(2,1)}), bf16[512,2,2048]{2,1,0:T(2,128)(2,1)}, u32[]{:S(2)}, u32[]{:S(2)}) async-start(bf16[512,2,2048]{2,1,0:T(2,128)(2,1)} %copy.31), calls=%async_computation | async-start | bytes 8388608 | tf_op jit(solution)/shard_map/all_to_all | solution.py:72
  595.9 92.5 %all-to-all-done = bf16[512,2,2048]{2,1,0:T(2,128)(2,1)} async-done(((bf16[512,2,2048]{2,1,0:T(2,128)(2,1)}), bf16[512,2,2048]{2,1,0:T(2,128)(2,1)}, u32[]{:S(2)}, u32[]{:S(2)}) %all-to-all-start) | async-done | bytes 4194336 | tf_op jit(solution)/shard_map/all_to_all | solution.py:72
  688.4 6.1 copy.32
  694.4 7.8 reshape.176
  702.2 7.9 reshape.175
  710.1 3.4 fusion.24
  716.5 3.4 copy.37
  722.3 27.3 %fusion = bf16[16,2,2,512,2,512]{3,5,2,4,1,0:T(8,128)(2,1)} fusion(bf16[16,1,2,16,2,4,512]{6,3,2,5,4,1,0:T(8,128)(2,1)} %maximum_bitcast_fusion.4, bf16[16,1,2,16,2,4,512]{6,3,2,5,4,1,0:T(8,128)(2,1)S(1)} %copy.37, bf16[16,2,16,2,4,512,1,1]{5,4,0,3,2,1,7,6:T(4,128)(2,1)S(1)} %bitcast.90), kind=kOutput, calls=%fused_computation.1 | convolution fusion | flops 8673820672 | bytes 79691776 | tf_op jit(solution)/shard_map/crtgfa,csrthfb->csgahb/dot_general | solution.py:77
  749.6 162.0 %copy.39 = bf16[16,2,2,512,2,512]{5,4,3,2,1,0:T(2,128)(2,1)} copy(bf16[16,2,2,512,2,512]{3,5,2,4,1,0:T(8,128)(2,1)} %fusion) | data formatting | bytes 134217728 | tf_op jit(solution)/shard_map/mul | solution.py:32
  911.6 106.0 %mul.287 = bf16[16,2,1024,1024]{3,2,1,0:T(8,128)(2,1)} reshape(bf16[16,2,2,512,2,512]{5,4,3,2,1,0:T(2,128)(2,1)} %copy.39) | data formatting | bytes 134217728 | tf_op jit(solution)/shard_map/mul | solution.py:32
  1017.6 32.4 %fusion.2 = bf16[16,1024,1024]{2,1,0:T(8,128)(2,1)} fusion(bf16[16,2,1024,1024]{3,2,1,0:T(8,128)(2,1)} %mul.287, pred[1024,1024]{1,0:T(8,128)(4,1)S(1)} %copy-done.4), kind=kLoop, calls=%fused_computation.4 | loop fusion | flops 16777216 | bytes 101711872 | tf_op jit(solution)/shard_map/convert_element_type | solution.py:34
  (21 shorter events, 12.7 us)
Async XLA Ops:
  11.5 22.3 %copy-start.5 = (s32[12,1024]{1,0:T(8,128)S(1)}, s32[12,1024]{1,0:T(8,128)}, u32[]{:S(2)}) copy-start(s32[12,1024]{1,0:T(8,128)} %param.3) | copy-start | bytes 147460
  11.5 364.8 %collective-permute-start.1 = (bf16[2,4,1024,512]{2,3,0,1:T(8,128)(2,1)}, bf16[2,4,1024,512]{2,3,0,1:T(8,128)(2,1)S(1)}, u32[]{:S(2)}, u32[]{:S(2)}) collective-permute-start(bf16[2,4,1024,512]{2,3,0,1:T(8,128)(2,1)} %copy.26), channel_id=1, source_target_pairs={{0,4},{2,6},{4,8},{6,10},{8,12},{10,14},{12,16},{14,18},{16,20},{1... | collective-permute-start | bytes 25165832 | tf_op jit(solution)/shard_map/ppermute | solution.py:14
  17.0 367.8 %collective-permute-start = (bf16[2,4,1024,512]{2,3,0,1:T(8,128)(2,1)}, bf16[2,4,1024,512]{2,3,0,1:T(8,128)(2,1)S(1)}, u32[]{:S(2)}, u32[]{:S(2)}) collective-permute-start(bf16[2,4,1024,512]{2,3,0,1:T(8,128)(2,1)} %copy.26), channel_id=1, source_target_pairs={{0,2},{2,4},{4,6},{6,8},{8,10},{10,12},{12,14},{14,16},{16,18},{18... | collective-permute-start | bytes 25165832 | tf_op jit(solution)/shard_map/ppermute | solution.py:14
  27.8 307.1 %collective-permute-start.2 = (bf16[2,3,1024,512]{2,3,0,1:T(8,128)(2,1)}, bf16[2,3,1024,512]{2,3,0,1:T(8,128)(2,1)}, u32[]{:S(2)}, u32[]{:S(2)}) collective-permute-start(bf16[2,3,1024,512]{2,3,0,1:T(8,128)(2,1)} %slice.130), channel_id=1, source_target_pairs={{0,6},{2,8},{4,10},{6,12},{8,14},{10,16},{12,18},{14,20},{16,22},{... | collective-permute-start | bytes 18874376 | tf_op jit(solution)/shard_map/ppermute | solution.py:14
  376.3 8.6 copy-start.2
  384.8 3.3 copy-start.3
  445.8 242.5 %all-to-all-start = ((bf16[512,2,2048]{2,1,0:T(2,128)(2,1)}), bf16[512,2,2048]{2,1,0:T(2,128)(2,1)}, u32[]{:S(2)}, u32[]{:S(2)}) async-start(bf16[512,2,2048]{2,1,0:T(2,128)(2,1)} %copy.31), calls=%async_computation | async-start | bytes 8388608 | tf_op jit(solution)/shard_map/all_to_all | solution.py:72
  710.1 6.4 copy-start.1
  716.5 5.8 copy-start
  911.5 106.0 %copy-start.4 = (pred[1024,1024]{1,0:T(8,128)(4,1)S(1)}, pred[1024,1024]{1,0:T(8,128)(4,1)}, u32[]{:S(2)}) copy-start(pred[1024,1024]{1,0:T(8,128)(4,1)} %iota_compare_fusion) | copy-start | bytes 3145732
where the time goes:
time: 1060 us; the launch traced here: 1050 us
  waiting for transfers between devices  418 us (39%)
  local copies, waits for them, and re-layouts  354 us (33%)
  starting transfers between devices  164 us (15%)
  matrix products  66 us (6%)
  other arithmetic  47.8 us (5%)
    ppermute x3, waiting for transfers between devices, passed_along(): lax.ppermute(value, axis, [(source, source + steps) for source in range(f...  325 us
    mul x2, local copies, waits for them, and re-layouts, finish(): products.reshape(chan_count, 2, all_inputs, all_inputs) * (1.0 / spec_total)  268 us
    all_to_all x1, starting transfers between devices, per_device(): lax.all_to_all(flat_spectra, ('tm', 'inp'), split_axis=0, concat_axis=2,...  149 us
    all_to_all x1, waiting for transfers between devices, per_device(): lax.all_to_all(flat_spectra, ('tm', 'inp'), split_axis=0, concat_axis=2,...  92.5 us
    dot_general x1, matrix products, per_device(): jnp.einsum('rfna,rnsj->jsfa', filtered, dft_matrix, preferred_element_typ...  38.7 us
    convert_element_type x1, other arithmetic, finish(): jnp.where(upper_mask[None], visibility[:, 0], visibility[:, 1])  32.4 us
    dot_general x1, matrix products, per_device(): jnp.einsum(einsum_form, channel_grid, turned, preferred_element_type=jnp....  27.3 us
  transfers between devices with their start and end apart: 4, of which 3 were waited for; matrix products, arithmetic and copies ran while one was open for 3% of the time, Pallas kernels for 0%

commit v1 on v0

v1 whole, which is shorter than its diff:
```python
import functools
import math

import jax
import jax.numpy as jnp
import numpy as np
from jax import lax
from jax.experimental import pallas as pl
from jax.experimental.pallas import tpu as pltpu
from jax.sharding import PartitionSpec as P

KEEP = 512
RADIX = 4
MIB = 1 << 20


def dft_tables(fine, keep):
    base = fine // RADIX
    branch = np.arange(base)[None, :]
    channel = np.arange(keep)[:, None]
    phase = np.mod(branch * (channel - keep // 2), fine)
    angle = 2.0 * np.pi / fine * phase
    norm = 1.0 / math.sqrt(fine)
    both = np.stack([np.cos(angle) * norm, -np.sin(angle) * norm])
    both = both.reshape(2, keep // RADIX, RADIX, base).transpose(2, 0, 1, 3)
    return both.reshape(RADIX, 2 * (keep // RADIX), base).astype(np.float32)


def pack_kernel(peers, half, place, *refs):
    ins, outs = refs[:peers], refs[peers:]
    for k in range(peers):
        real = ins[k][0].astype(jnp.float32)
        imag = ins[k][1].astype(jnp.float32)
        low = lax.broadcasted_iota(jnp.int32, real.shape, 1) < half
        outs[k][...] = jnp.where(low, real, pltpu.roll(imag, half, 1)).astype(jnp.bfloat16)
        outs[peers + k][...] = jnp.where(low, pltpu.roll(real, half, 1), imag).astype(jnp.bfloat16)


def pack(voltages, place, peers):
    rows, width = voltages.shape[1:]
    lanes = width // peers
    step = min(rows, 512)
    spec = [
        pl.BlockSpec((2, step, lanes), functools.partial(lambda k, i, p: (0, i, jnp.bitwise_xor(p[0], k)), k))
        for k in range(peers)
    ]
    out_spec = [pl.BlockSpec((step, lanes), lambda i, p: (i, 0))] * (2 * peers)
    return pl.pallas_call(
        functools.partial(pack_kernel, peers, lanes // 2),
        grid_spec=pltpu.PrefetchScalarGridSpec(
            num_scalar_prefetch=1, grid=(rows // step,), in_specs=spec, out_specs=out_spec
        ),
        out_shape=[jax.ShapeDtypeStruct((rows, lanes), jnp.bfloat16)] * (2 * peers),
        compiler_params=pltpu.CompilerParams(vmem_limit_bytes=40 * MIB),
        name="pack",
    )(place, *([voltages] * peers))


def spectra_kernel(dims, place, *refs):
    peers, frames, taps_n, base, per_res, dests, chan, tail_step, step = dims
    pieces = refs[:peers]
    taps, table, out, xs, ys, zs, heads, tails = refs[peers:]
    own = peers * frames
    past = taps_n - 1
    total = own + past
    lanes = xs.shape[-1]
    half = lanes // 2
    at = pl.program_id(0)

    for k in range(peers):
        first = jnp.bitwise_xor(place[0], k) * frames
        for f in range(frames):
            xs[first + f] = pieces[k][f].astype(jnp.float32)

    flip = jnp.where(lax.broadcasted_iota(jnp.int32, (16, lanes), 1) < half, 1.0, -1.0)

    @pl.when(at == 0)
    def _():
        for c in range(RADIX):
            zs[c, (total + 1) // 2 - 1] = jnp.zeros(zs.shape[2:], zs.dtype)

    def filter_rows(b, carry):
        row = pl.multiple_of(b * 16, 16)
        for q in range(RADIX):
            for s in range(2):
                here = pl.ds(pl.multiple_of(row + 8 * s, 8), 8)
                weight = taps[q, pl.ds(pl.multiple_of(at * step + row + 8 * s, 8), 8), :]
                weights = [jnp.broadcast_to(weight[:, k : k + 1], (8, lanes)) for k in range(taps_n)]
                x = [xs[f, q, here, :] for f in range(own)]
                for f in range(total):
                    parts = [weights[k] * x[f - k] for k in range(taps_n) if 0 <= f - k < own]
                    while len(parts) > 1:
                        parts = [sum(parts[i : i + 2]) for i in range(0, len(parts), 2)]
                    ys[q, f, pl.ds(8 * s, 8), :] = parts[0]
        place_rows = pl.ds(pl.multiple_of(at * step + row, 16), 16)
        for f in range(total):
            y0, y1, y2, y3 = (ys[q, f] for q in range(RADIX))
            even, odd = y0 + y2, y1 + y3
            diff = y0 - y2
            turned = pltpu.roll(y1 - y3, half, 1) * flip
            side = pl.ds((f % 2) * lanes, lanes)
            for c, value in enumerate((even + odd, diff + turned, even - odd, diff - turned)):
                zs[c, f // 2, place_rows, side] = value.astype(jnp.bfloat16)
        return carry

    lax.fori_loop(0, step // 16, filter_rows, 0)

    @pl.when(at == pl.num_programs(0) - 1)
    def _():
        sign = jnp.where(lax.broadcasted_iota(jnp.int32, (per_res, lanes), 1) < half, -1.0, 1.0)

        def transform(pair, c):
            both = jnp.dot(table[c], zs[c, pair], preferred_element_type=jnp.float32)
            return [
                both[:per_res, u * lanes : (u + 1) * lanes]
                + pltpu.roll(both[per_res:, u * lanes : (u + 1) * lanes], half, 1) * sign
                for u in range(2)
            ]

        def head_pair(pair, carry):
            for c in range(RADIX):
                for u, value in enumerate(transform(pair, c)):
                    heads[pl.ds(c * own + pair * 2 + u, per_res, stride=RADIX * own), :] = value
            return carry

        lax.fori_loop(0, own // 2, head_pair, 0)
        for pair in range(own // 2, (total + 1) // 2):
            for c in range(RADIX):
                for u, value in enumerate(transform(pair, c)):
                    f = pair * 2 + u - own
                    if f < past:
                        tails[pl.ds(c * past + f, per_res, stride=tail_step), :] = value
        head_rows = chan * own
        tail_rows = chan // RADIX * tail_step

        def emit(d, carry):
            out[d, pl.ds(0, head_rows), :] = heads[
                pl.ds(pl.multiple_of(d * head_rows, 16), head_rows), :
            ].astype(jnp.bfloat16)
            out[d, pl.ds(head_rows, tail_rows), :] = tails[
                pl.ds(pl.multiple_of(d * tail_rows, 16), tail_rows), :
            ].astype(jnp.bfloat16)
            return carry

        lax.fori_loop(0, dests, emit, 0)


def tail_stride(chan, past):
    stride = RADIX * past
    if chan // RADIX * stride % 16:
        stride = -(-stride // 16) * 16
    return stride


def spectra(pieces, place, taps, table, frames, dests, chan):
    peers = len(pieces)
    lanes = pieces[0].shape[-1]
    fine, taps_n = taps.shape[1], taps.shape[0]
    base = fine // RADIX
    keep = chan * dests
    per_res = keep // RADIX
    own, past = peers * frames, taps_n - 1
    pairs = (own + past + 1) // 2
    stride = tail_stride(chan, past)
    step = min(base, 64)
    dims = (peers, frames, taps_n, base, per_res, dests, chan, stride, step)
    rows = chan * own + chan // RADIX * stride
    weights = (taps.astype(jnp.float32) * (1.0 / 8192.0)).T.reshape(RADIX, base, taps_n)
    blocks = [piece.reshape(frames, RADIX, base, lanes) for piece in pieces]
    whole = lambda shape: pl.BlockSpec(shape, lambda i, p: (0,) * len(shape))
    return pl.pallas_call(
        functools.partial(spectra_kernel, dims),
        grid_spec=pltpu.PrefetchScalarGridSpec(
            num_scalar_prefetch=1,
            grid=(base // step,),
            in_specs=[pl.BlockSpec((frames, RADIX, step, lanes), lambda i, p: (0, 0, i, 0))] * peers
            + [whole(weights.shape), whole(table.shape)],
            out_specs=whole((dests, rows, lanes)),
            scratch_shapes=[
                pltpu.VMEM((own, RADIX, step, lanes), jnp.float32),
                pltpu.VMEM((RADIX, own + past, 16, lanes), jnp.float32),
                pltpu.VMEM((RADIX, pairs, base, 2 * lanes), jnp.bfloat16),
                pltpu.VMEM((keep * own, lanes), jnp.float32),
                pltpu.VMEM((per_res * stride, lanes), jnp.float32),
            ],
        ),
        out_shape=jax.ShapeDtypeStruct((dests, rows, lanes), jnp.bfloat16),
        compiler_params=pltpu.CompilerParams(vmem_limit_bytes=56 * MIB),
        name="spectra",
    )(place, *blocks, weights, table)


def gram_kernel(dims, first, second, out, tails, stacked, turned):
    planes, peers, cores, own, past, chan, stride, scale = dims
    lanes = first.shape[-1]
    half = lanes // 2
    ch = pl.program_id(0)
    head_rows = chan * own
    tail_rows = chan // RADIX * stride
    sources = planes * peers * cores
    inputs = peers * cores * lanes
    depth = planes * own

    @pl.when(ch == 0)
    def _():
        def widen(d, carry):
            for h, ref in enumerate((first, second)):
                tails[h, d, pl.ds(0, tail_rows), :] = ref[d, pl.ds(head_rows, tail_rows), :].astype(jnp.float32)
                tails[h, d, pl.ds(tail_rows, 16), :] = jnp.zeros((16, lanes), jnp.float32)
            return carry

        lax.fori_loop(0, sources, widen, 0)

    low = lax.broadcasted_iota(jnp.int32, (own, lanes), 1) < half
    early = lax.broadcasted_iota(jnp.int32, (own, lanes), 0) < past
    tail_at = ch // RADIX * stride + ch % RADIX * past
    head_at = pl.multiple_of(ch * own, 16)
    for z in range(planes):
        for q in range(peers):
            for c in range(cores):
                source = (z * peers + q) * cores + c
                value = []
                for h, ref in enumerate((first, second)):
                    v = ref[source, pl.ds(head_at, own), :].astype(jnp.float32)
                    if z:
                        late = tails[h, source - peers * cores, pl.ds(tail_at, own), :]
                        v = v + jnp.where(early, late, 0.0)
                    value.append(v)
                a, b = value
                real = jnp.where(low, a, pltpu.roll(b, half, 1)).astype(jnp.bfloat16)
                imag = jnp.where(low, pltpu.roll(a, half, 1), b)
                column = pl.ds((c * peers + q) * lanes, lanes)
                stacked[pl.ds(z * own, own), column] = real
                stacked[pl.ds(depth + z * own, own), column] = imag.astype(jnp.bfloat16)
                turned[pl.ds(z * own, own), column] = (-imag).astype(jnp.bfloat16)
                turned[pl.ds(depth + z * own, own), column] = real

    block = min(256, inputs)
    diagonal = (
        lax.broadcasted_iota(jnp.int32, (block, block), 0) <= lax.broadcasted_iota(jnp.int32, (block, block), 1)
    )
    for i in range(inputs // block):
        left = stacked[:, i * block : (i + 1) * block].T

        def product(ref, lo, hi):
            return jnp.dot(left, ref[:, lo:hi], preferred_element_type=jnp.float32) * scale

        rows = pl.ds(i * block, block)
        lo, hi = i * block, (i + 1) * block
        if lo:
            out[0, rows, 0:lo] = product(turned, 0, lo).astype(jnp.bfloat16)
        mixed = jnp.where(diagonal, product(stacked, lo, hi), product(turned, lo, hi))
        out[0, rows, lo:hi] = mixed.astype(jnp.bfloat16)
        if hi < inputs:
            out[0, rows, hi:inputs] = product(stacked, hi, inputs).astype(jnp.bfloat16)


def gram(first, second, planes, peers, cores, own, past, chan, scale):
    sources, rows, lanes = first.shape
    inputs = peers * cores * lanes
    stride = tail_stride(chan, past)
    tail_rows = chan // RADIX * stride
    depth = planes * own
    whole = pl.BlockSpec(first.shape, lambda i: (0, 0, 0))
    dims = (planes, peers, cores, own, past, chan, stride, scale)
    return pl.pallas_call(
        functools.partial(gram_kernel, dims),
        grid=(chan,),
        in_specs=[whole, whole],
        out_specs=pl.BlockSpec((1, inputs, inputs), lambda i: (i, 0, 0)),
        scratch_shapes=[
            pltpu.VMEM((2, sources, tail_rows + 16, lanes), jnp.float32),
            pltpu.VMEM((2 * depth, inputs), jnp.bfloat16),
            pltpu.VMEM((2 * depth, inputs), jnp.bfloat16),
        ],
        out_shape=jax.ShapeDtypeStruct((chan, inputs, inputs), jnp.bfloat16),
        compiler_params=pltpu.CompilerParams(vmem_limit_bytes=56 * MIB),
        name="gram",
    )(first, second)


def per_device(voltages, taps):
    past, fine = taps.shape[0] - 1, taps.shape[1]
    frames = voltages.shape[1] // fine
    n_time, n_group = lax.axis_size("tm"), lax.axis_size("inp")
    dests = n_time * n_group
    chan = KEEP // dests
    peers = 1
    while peers * frames < past:
        peers *= 2
    planes = n_time // peers
    own = peers * frames
    place = jnp.bitwise_and(lax.axis_index("tm"), peers - 1).astype(jnp.int32)[None]
    table = jnp.asarray(dft_tables(fine, KEEP).astype(jnp.bfloat16))

    packed = pack(voltages, place, peers)
    halves = [packed[:peers], packed[peers:]]
    turned = []
    for h in range(2):
        pieces = halves[h]
        if h:
            pieces, turned[0] = lax.optimization_barrier((pieces, turned[0]))
        moved = [pieces[0]]
        for k in range(1, peers):
            moved.append(lax.ppermute(pieces[k], "tm", [(t, t ^ k) for t in range(n_time)]))
        turned.append(moved)
    received = []
    for h in range(2):
        mine = spectra(turned[h], place, taps, table, frames, dests, chan)
        received.append(lax.all_to_all(mine, ("tm", "inp"), split_axis=0, concat_axis=0, tiled=True))
    return gram(*received, planes, peers, n_group, own, past, chan, 1.0 / (n_time * frames))


def solution(mesh):
    return jax.shard_map(
        per_device,
        mesh=mesh,
        in_specs=(P(None, "tm", "inp"), P()),
        out_specs=P(("tm", "inp"), None, None),
        check_vma=False,
    )
```

time: 1060 us -> 306 us (0.29)
  local copies, waits for them, and re-layouts: 354 us -> 3.95 us
  waiting for transfers between devices: 418 us -> 129 us
  starting transfers between devices: 164 us -> 13 us
  blocking collectives: 0 us -> 86.2 us
  Pallas kernels: 0 us -> 73.6 us
  matrix products: 66 us -> 0 us
  other arithmetic: 47.8 us -> 0.01 us
    mul x2 -> x0, local copies, waits for them, and re-layouts: 268 us -> none  [finish(): products.reshape(chan_count, 2, all_inputs, all_inputs) * (1.0 / spec_total)]
    ppermute x3 -> x6, waiting for transfers between devices: 325 us -> 129 us  [per_device(): lax.ppermute(pieces[k], 'tm', [(t, t ^ k) for t in range(n_time)])]
    all_to_all x1, starting transfers between devices: 149 us -> 5.03 us  [per_device(): lax.all_to_all(mine, ('tm', 'inp'), split_axis=0, concat_axis=0, tiled=True)]
    all_to_all x1, waiting for transfers between devices: 92.5 us -> 0.01 us  [per_device(): lax.all_to_all(mine, ('tm', 'inp'), split_axis=0, concat_axis=0, tiled=True)]
    all_to_all x0 -> x1, blocking collectives: none -> 86.2 us  [per_device(): lax.all_to_all(mine, ('tm', 'inp'), split_axis=0, concat_axis=0, tiled=True)]
    pallas_call x0 -> x4, Pallas kernels: none -> 73.6 us  [the longest x2 41.9 us: spectra(): pl.pallas_call(functools.partial(spectra_kernel, dims), grid_spec=pltpu.P...]
    dot_general x2 -> x0, matrix products: 66 us -> none  [the longest x1 38.7 us: per_device(): jnp.einsum('rfna,rnsj->jsfa', filtered, dft_matrix, preferred_element_typ...]
    convert_element_type x2 -> x0, other arithmetic: 32.4 us -> none  [the longest x1 32.4 us: finish(): jnp.where(upper_mask[None], visibility[:, 0], visibility[:, 1])]
  transfers between devices with their start and end apart: 4 -> 7, of which waited for: 3 -> 4; matrix products, arithmetic and copies ran while one was open for 3% -> 0% of each run, Pallas kernels for 0% -> 7%
where the time goes in v1:
time: 306 us
  waiting for transfers between devices  129 us (42%)
  blocking collectives  86.2 us (28%)
  Pallas kernels  73.6 us (24%)
  starting transfers between devices  13 us (4%)
  local copies, waits for them, and re-layouts  3.95 us (1%)
    ppermute x6, waiting for transfers between devices, per_device(): lax.ppermute(pieces[k], 'tm', [(t, t ^ k) for t in range(n_time)])  129 us
    all_to_all x1, blocking collectives, per_device(): lax.all_to_all(mine, ('tm', 'inp'), split_axis=0, concat_axis=0, tiled=True)  86.2 us
    pallas_call x2, Pallas kernels, spectra(): pl.pallas_call(functools.partial(spectra_kernel, dims), grid_spec=pltpu.P...  41.9 us
    pallas_call x1, Pallas kernels, gram(): pl.pallas_call(functools.partial(gram_kernel, dims), grid=(chan,), in_spe...  23.4 us
    pallas_call x1, Pallas kernels, pack(): pl.pallas_call(functools.partial(pack_kernel, peers, lanes // 2), grid_sp...  8.31 us
    ppermute x6, starting transfers between devices, per_device(): lax.ppermute(pieces[k], 'tm', [(t, t ^ k) for t in range(n_time)])  8.01 us
  transfers between devices with their start and end apart: 7, of which 4 were waited for; matrix products, arithmetic and copies ran while one was open for 0% of the time, Pallas kernels for 7%

profile of v1, /device:TPU:0, one launch (start us, length us, event | category | flops | bytes accessed | tf_op | source)
XLA Modules:
  0.0 306.1 jit_solution(2908612240566618660)
XLA Ops:
  0.0 8.3 %pack.1 = (bf16[4096,128]{1,0:T(8,128)(2,1)S(1)}, bf16[4096,128]{1,0:T(8,128)(2,1)}, bf16[4096,128]{1,0:T(8,128)(2,1)}, bf16[4096,128]{1,0:T(8,128)(2,1)}, bf16[...) custom-call(s32[1]{0:T(128)} %bitcast.place, ...), custom_call_target="tpu_custom_call" | custom-call | tf_op jit(solution)/shard_map/pack/pallas_call | solution.py:48
  8.3 1.0 copy-done
  9.3 1.0 copy-done.1
  10.3 2.9 collective-permute-start
  13.2 1.5 collective-permute-start.1
  14.7 0.0 collective-permute-start.2
  14.7 0.0 copy-done.5
  14.7 1.0 copy.4
  15.8 21.7 %collective-permute-done = bf16[4096,128]{1,0:T(8,128)(2,1)} collective-permute-done((bf16[4096,128]{1,0:T(8,128)(2,1)}, bf16[4096,128]{1,0:T(8,128)(2,1)}, u32[]{:S(2)}, u32[]{:S(2)}) %collective-permute-start) | collective-permute-done | bytes 1048608 | tf_op jit(solution)/shard_map/ppermute | solution.py:305
  37.5 23.1 %collective-permute-done.1 = bf16[4096,128]{1,0:T(8,128)(2,1)} collective-permute-done((bf16[4096,128]{1,0:T(8,128)(2,1)}, bf16[4096,128]{1,0:T(8,128)(2,1)}, u32[]{:S(2)}, u32[]{:S(2)}) %collective-permute-start.1) | collective-permute-done | bytes 1048608 | tf_op jit(solution)/shard_map/ppermute | solution.py:305
  60.6 0.0 collective-permute-done.2
  60.6 21.0 %spectra.2 = bf16[32,432,128]{2,1,0:T(8,128)(2,1)} custom-call(s32[1]{0:T(128)} %bitcast.place, bf16[4,4,256,128]{3,2,1,0:T(8,128)(2,1)} %bitcast.13, bf16[4,4,256,128]{3,2,1,0:T(8,128)(2,1)} %bitcast.2.refs_1_, bf16[4,4,256,128]{3,2,1,0:T(8,128)(2,1)} %bitcast.3.refs_2_, bf16[4,4,256,128]{3,2,1,0:T(8,128)(2,1)} %bitcast.4.refs_3_, f32[4,256,12]{2,1,0:T(8,128)} %bitcast.14, ...), custom_call_target="tpu_custom_call" | custom-call | tf_op jit(solution)/shard_map/spectra/pallas_call | solution.py:171
  81.6 5.0 %all-to-all-start = ((bf16[32,432,128]{2,1,0:T(8,128)(2,1)}), bf16[32,432,128]{2,1,0:T(8,128)(2,1)}, u32[]{:S(2)}, u32[]{:S(2)}) async-start(bf16[32,432,128]{2,1,0:T(8,128)(2,1)} %spectra.2), calls=%async_computation | async-start | bytes 7077888 | tf_op jit(solution)/shard_map/all_to_all | solution.py:310
  86.6 1.8 collective-permute-start.3
  88.4 1.5 collective-permute-start.4
  89.8 0.3 collective-permute-start.5
  90.2 55.3 %collective-permute-done.3 = bf16[4096,128]{1,0:T(8,128)(2,1)S(1)} collective-permute-done((bf16[4096,128]{1,0:T(8,128)(2,1)S(1)}, bf16[4096,128]{1,0:T(8,128)(2,1)S(1)}, u32[]{:S(2)}, u32[]{:S(2)}) %collective-permute-start.3) | collective-permute-done | bytes 1048608 | tf_op jit(solution)/shard_map/ppermute | solution.py:305
  145.5 0.0 collective-permute-done.4
  145.5 29.0 %collective-permute-done.5 = bf16[4096,128]{1,0:T(8,128)(2,1)S(1)} collective-permute-done((bf16[4096,128]{1,0:T(8,128)(2,1)S(1)}, bf16[4096,128]{1,0:T(8,128)(2,1)S(1)}, u32[]{:S(2)}, u32[]{:S(2)}) %collective-permute-start.5) | collective-permute-done | bytes 1048608 | tf_op jit(solution)/shard_map/ppermute | solution.py:305
  174.5 1.0 copy-done.4
  175.5 21.0 %spectra.3 = bf16[32,432,128]{2,1,0:T(8,128)(2,1)} custom-call(s32[1]{0:T(128)} %bitcast.place, bf16[4,4,256,128]{3,2,1,0:T(8,128)(2,1)} %bitcast.12, bf16[4,4,256,128]{3,2,1,0:T(8,128)(2,1)} %bitcast.16, bf16[4,4,256,128]{3,2,1,0:T(8,128)(2,1)} %bitcast.17, bf16[4,4,256,128]{3,2,1,0:T(8,128)(2,1)} %bitcast.18, f32[4,256,12]{2,1,0:T(8,128)} %bitcast.15, ...), custom_call_target="tpu_custom_call" | custom-call | tf_op jit(solution)/shard_map/spectra/pallas_call | solution.py:171
  196.5 0.0 all-to-all-done.first
  196.5 86.2 %all_to_all.10.second = bf16[32,432,128]{2,1,0:T(8,128)(2,1)} all-to-all(bf16[32,432,128]{2,1,0:T(8,128)(2,1)} %spectra.3), channel_id=1, replica_groups=mesh['tm'=16,'inp'=2] {'tm','inp'}, dimensions={0} | all-to-all | bytes 7077888 | tf_op jit(solution)/shard_map/all_to_all | solution.py:310
  282.7 23.4 %gram.1 = bf16[16,1024,1024]{2,1,0:T(8,128)(2,1)} custom-call(bf16[32,432,128]{2,1,0:T(8,128)(2,1)} %all-to-all-done.first, bf16[32,432,128]{2,1,0:T(8,128)(2,1)} %all_to_all.10.second), custom_call_target="tpu_custom_call" | custom-call | tf_op jit(solution)/shard_map/gram/pallas_call | solution.py:266
  (9 shorter events, 0.0 us)
Async XLA Ops:
  0.0 14.7 %copy-start.5 = (s32[12,1024]{1,0:T(8,128)S(1)}, s32[12,1024]{1,0:T(8,128)}, u32[]{:S(2)}) copy-start(s32[12,1024]{1,0:T(8,128)} %param.4) | copy-start | bytes 147460
  8.3 1.0 copy-start
  9.3 1.0 copy-start.1
  10.3 27.2 %collective-permute-start = (bf16[4096,128]{1,0:T(8,128)(2,1)}, bf16[4096,128]{1,0:T(8,128)(2,1)}, u32[]{:S(2)}, u32[]{:S(2)}) collective-permute-start(bf16[4096,128]{1,0:T(8,128)(2,1)} %get-tuple-element.26), channel_id=1, source_target_pairs={{0,2},{2,0},{4,6},{6,4},{8,10},{10,8},{12,14},{14,12},{16,18},{18,... | collective-permute-start | bytes 3145736 | tf_op jit(solution)/shard_map/ppermute | solution.py:305
  13.2 47.4 %collective-permute-start.1 = (bf16[4096,128]{1,0:T(8,128)(2,1)}, bf16[4096,128]{1,0:T(8,128)(2,1)}, u32[]{:S(2)}, u32[]{:S(2)}) collective-permute-start(bf16[4096,128]{1,0:T(8,128)(2,1)} %get-tuple-element.27), channel_id=1, source_target_pairs={{0,4},{2,6},{4,0},{6,2},{8,12},{10,14},{12,8},{14,10},{16,20},{18,... | collective-permute-start | bytes 3145736 | tf_op jit(solution)/shard_map/ppermute | solution.py:305
  14.7 45.9 %collective-permute-start.2 = (bf16[4096,128]{1,0:T(8,128)(2,1)}, bf16[4096,128]{1,0:T(8,128)(2,1)}, u32[]{:S(2)}, u32[]{:S(2)}) collective-permute-start(bf16[4096,128]{1,0:T(8,128)(2,1)} %get-tuple-element.28), channel_id=1, source_target_pairs={{0,6},{2,4},{4,2},{6,0},{8,14},{10,12},{12,10},{14,8},{16,22},{18,... | collective-permute-start | bytes 3145736 | tf_op jit(solution)/shard_map/ppermute | solution.py:305
  81.6 114.9 %all-to-all-start = ((bf16[32,432,128]{2,1,0:T(8,128)(2,1)}), bf16[32,432,128]{2,1,0:T(8,128)(2,1)}, u32[]{:S(2)}, u32[]{:S(2)}) async-start(bf16[32,432,128]{2,1,0:T(8,128)(2,1)} %spectra.2), calls=%async_computation | async-start | bytes 7077888 | tf_op jit(solution)/shard_map/all_to_all | solution.py:310
  86.6 58.9 %collective-permute-start.3 = (bf16[4096,128]{1,0:T(8,128)(2,1)S(1)}, bf16[4096,128]{1,0:T(8,128)(2,1)S(1)}, u32[]{:S(2)}, u32[]{:S(2)}) collective-permute-start(bf16[4096,128]{1,0:T(8,128)(2,1)S(1)} %get-tuple-element.34), channel_id=1, source_target_pairs={{0,2},{2,0},{4,6},{6,4},{8,10},{10,8},{12,14},{14,12},{16,18},{18,... | collective-permute-start | bytes 3145736 | tf_op jit(solution)/shard_map/ppermute | solution.py:305
  88.4 57.1 %collective-permute-start.4 = (bf16[4096,128]{1,0:T(8,128)(2,1)S(1)}, bf16[4096,128]{1,0:T(8,128)(2,1)S(1)}, u32[]{:S(2)}, u32[]{:S(2)}) collective-permute-start(bf16[4096,128]{1,0:T(8,128)(2,1)S(1)} %get-tuple-element.35), channel_id=1, source_target_pairs={{0,4},{2,6},{4,0},{6,2},{8,12},{10,14},{12,8},{14,10},{16,20},{18,... | collective-permute-start | bytes 3145736 | tf_op jit(solution)/shard_map/ppermute | solution.py:305
  89.8 84.7 %collective-permute-start.5 = (bf16[4096,128]{1,0:T(8,128)(2,1)S(1)}, bf16[4096,128]{1,0:T(8,128)(2,1)S(1)}, u32[]{:S(2)}, u32[]{:S(2)}) collective-permute-start(bf16[4096,128]{1,0:T(8,128)(2,1)S(1)} %get-tuple-element.36), channel_id=1, source_target_pairs={{0,6},{2,4},{4,2},{6,0},{8,14},{10,12},{12,10},{14,8},{16,22},{18,... | collective-permute-start | bytes 3145736 | tf_op jit(solution)/shard_map/ppermute | solution.py:305
  145.5 29.0 %copy-start.2 = (bf16[4096,128]{1,0:T(8,128)(2,1)}, bf16[4096,128]{1,0:T(8,128)(2,1)S(1)}, u32[]{:S(2)}) copy-start(bf16[4096,128]{1,0:T(8,128)(2,1)S(1)} %collective-permute-done.3) | copy-start | bytes 3145732
  145.5 29.0 %copy-start.3 = (bf16[4096,128]{1,0:T(8,128)(2,1)}, bf16[4096,128]{1,0:T(8,128)(2,1)S(1)}, u32[]{:S(2)}) copy-start(bf16[4096,128]{1,0:T(8,128)(2,1)S(1)} %collective-permute-done.4) | copy-start | bytes 3145732
  174.5 1.0 copy-start.4

commit v2 on v0

v2 whole, which is shorter than its diff:
```python
import functools
import math

import jax
import jax.numpy as jnp
import numpy as np
from jax import lax
from jax.experimental import pallas as pl
from jax.experimental.pallas import tpu as pltpu
from jax.sharding import PartitionSpec as P

KEEP = 512
RADIX = 4
LANES = 128
PEERS = 4
SUB = LANES // PEERS
MIB = 1 << 20


def dft_tables(fine, keep):
    base = fine // RADIX
    branch = np.arange(base)[None, :]
    channel = np.arange(keep)[:, None]
    phase = np.mod(branch * (channel - keep // 2), fine)
    angle = 2.0 * np.pi / fine * phase
    norm = 1.0 / math.sqrt(fine)
    cosine = (np.cos(angle) * norm).reshape(keep // RADIX, RADIX, base)
    sine = (-np.sin(angle) * norm).reshape(keep // RADIX, RADIX, base)
    plain = np.stack([np.concatenate([cosine[:, c], sine[:, c]]) for c in (0, 2)])
    odd = [
        np.block([[cosine[:, c], sign * sine[:, c]], [sine[:, c], -sign * cosine[:, c]]])
        for c, sign in ((1, 1.0), (3, -1.0))
    ]
    return plain.astype(np.float32), np.concatenate(odd).astype(np.float32)


def lane(shape):
    return lax.broadcasted_iota(jnp.int32, shape, len(shape) - 1)


def blocks_transposed(x):
    low = lane(x[0].shape) < 2 * SUB
    even = lane(x[0].shape) % (2 * SUB) < SUB
    mid = [None] * 4
    for i in range(2):
        a, b = x[i], x[i + 2]
        mid[i] = jnp.where(low, a, pltpu.roll(b, 2 * SUB, 1))
        mid[i + 2] = jnp.where(low, pltpu.roll(a, 2 * SUB, 1), b)
    out = []
    for i in (0, 2):
        a, b = mid[i], mid[i + 1]
        out.append(jnp.where(even, a, pltpu.roll(b, SUB, 1)))
        out.append(jnp.where(even, pltpu.roll(a, LANES - SUB, 1), b))
    return out


def pack_kernel(place, source, *refs):
    outs, select = refs[:PEERS], refs[PEERS]

    @pl.when(pl.program_id(0) == 0)
    def _():
        shape = select.shape
        row, column = (lax.broadcasted_iota(jnp.int32, shape, axis) for axis in range(2))
        peer = jnp.bitwise_xor(column // LANES, place[0])
        wanted = (column % LANES) // SUB * LANES + peer * SUB + column % SUB
        select[...] = jnp.where(row == wanted, 1.0, 0.0).astype(jnp.bfloat16)

    x = jnp.concatenate([source[r, 0, upper] for upper in range(2) for r in range(2)], 1)
    moved = jnp.dot(x, select[...], preferred_element_type=jnp.float32).astype(jnp.bfloat16)
    for k in range(PEERS):
        outs[k][...] = moved[:, k * LANES : (k + 1) * LANES]


def pack(voltages, place, chunk, fine):
    frames = voltages.shape[1] // fine
    rows = fine // 2
    shaped = voltages.reshape(2, frames, 2, rows, voltages.shape[2])
    return pl.pallas_call(
        pack_kernel,
        grid_spec=pltpu.PrefetchScalarGridSpec(
            num_scalar_prefetch=1,
            grid=(frames,),
            in_specs=[pl.BlockSpec((2, 1, 2, rows, LANES), lambda i, p: (0, i, 0, 0, chunk))],
            out_specs=[pl.BlockSpec((rows, LANES), lambda i, p: (i, 0))] * PEERS,
            scratch_shapes=[pltpu.VMEM((PEERS * LANES, PEERS * LANES), jnp.bfloat16)],
        ),
        out_shape=[jax.ShapeDtypeStruct((frames * rows, LANES), jnp.bfloat16)] * PEERS,
        compiler_params=pltpu.CompilerParams(vmem_limit_bytes=40 * MIB),
        name="pack",
    )(place, shaped)


def spectra_kernel(dims, place, *refs):
    frames, taps_n, base, per_res, dests, chan, head_rows, tail_rows, step = dims
    pieces = refs[:PEERS]
    taps, plain, odd = refs[PEERS : PEERS + 3]
    out, xs, ys, zs, heads, tails = refs[-6:]
    own = PEERS * frames
    past = taps_n - 1
    total = own + past
    half = LANES // 2
    head_pairs, tail_pairs = own // 2, (past + 1) // 2
    pitch = heads.shape[0] // (per_res * RADIX)
    at = pl.program_id(0)

    for k in range(PEERS):
        first = jnp.bitwise_xor(place[0], k) * frames
        for f in range(frames):
            xs[first + f] = pieces[k][f].astype(jnp.float32)

    low = lane((8, LANES)) < half
    low16 = lane((16, LANES)) < half
    flip = jnp.where(low16, 1.0, -1.0)

    if total % 2:

        @pl.when(at == 0)
        def _():
            ys[:, total] = jnp.zeros(ys.shape[:1] + ys.shape[2:], ys.dtype)

    def filter_rows(b, carry):
        row = pl.multiple_of(b * 16, 16)
        for q in range(2):
            for s in range(2):
                here = pl.ds(pl.multiple_of(row + 8 * s, 8), 8)
                weight = taps[q, pl.ds(pl.multiple_of(at * step + row + 8 * s, 8), 8), :]
                wide = [jnp.broadcast_to(weight[:, k : k + 1], (8, LANES)) for k in range(2 * taps_n)]
                weights = [jnp.where(low, wide[k], wide[k + taps_n]) for k in range(taps_n)]
                x = [xs[f, q, here, :] for f in range(own)]
                for f in range(total):
                    parts = [weights[k] * x[f - k] for k in range(taps_n) if 0 <= f - k < own]
                    while len(parts) > 1:
                        parts = [sum(parts[i : i + 2]) for i in range(0, len(parts), 2)]
                    ys[q, f, pl.ds(8 * s, 8), :] = parts[0]
        for pair in range(head_pairs + tail_pairs):

            def sum_and_difference(q):
                first, second = ys[q, 2 * pair], ys[q, 2 * pair + 1]
                kept = jnp.where(low16, first, second)
                other = pltpu.roll(jnp.where(low16, second, first), half, 1)
                return kept + other, (kept - other) * flip

            a_sum, a_diff = sum_and_difference(0)
            b_sum, b_diff = sum_and_difference(1)
            side = pl.ds((pair % 2) * LANES, LANES)
            for part, value in enumerate((a_sum + b_sum, a_sum - b_sum, a_diff, b_diff)):
                rows = pl.ds(pl.multiple_of(part * base + at * step + row, 16), 16)
                zs[pair // 2, rows, side] = value.astype(jnp.bfloat16)
        return carry

    lax.fori_loop(0, step // 16, filter_rows, 0)

    @pl.when(at == pl.num_programs(0) - 1)
    def _():
        even = lane((per_res, LANES)) % (2 * SUB) < SUB

        def keep(quad, c, both):
            for u in range(2):
                sine = both[per_res:, u * LANES : (u + 1) * LANES]
                turned = jnp.where(even, -pltpu.roll(sine, LANES - SUB, 1), pltpu.roll(sine, SUB, 1))
                value = both[:per_res, u * LANES : (u + 1) * LANES] + turned
                pair = quad * 2 + u
                if pair < head_pairs:
                    heads[pl.ds(c * pitch + pair, per_res, stride=RADIX * pitch), :] = value
                elif pair < head_pairs + tail_pairs:
                    tails[pl.ds(c * tail_pairs + pair - head_pairs, per_res, stride=RADIX * tail_pairs), :] = value

        for quad in range((head_pairs + tail_pairs + 1) // 2):
            for i in range(2):
                rows = zs[quad, i * base : (i + 1) * base]
                keep(quad, 2 * i, jnp.dot(plain[i], rows, preferred_element_type=jnp.float32))
            both = jnp.dot(odd[...], zs[quad, 2 * base :], preferred_element_type=jnp.float32)
            keep(quad, 1, both[: 2 * per_res])
            keep(quad, 3, both[2 * per_res :])

        def emit(d, carry):
            for e in range(0, chan, 16 // head_pairs):
                rows = [heads[pl.ds((d * chan + e + i) * pitch, head_pairs), :] for i in range(16 // head_pairs)]
                out[d, pl.ds(e * head_pairs, 16), :] = jnp.concatenate(rows, 0).astype(jnp.bfloat16)
            out[d, pl.ds(head_rows, tail_rows), :] = tails[
                pl.ds(pl.multiple_of(d * chan * tail_pairs, 8), tail_rows), :
            ].astype(jnp.bfloat16)
            return carry

        lax.fori_loop(0, dests, emit, 0)


def block_rows(chan, own, past):
    head = chan * (own // 2)
    tail = -(-chan * ((past + 1) // 2) // 16) * 16
    return head, tail


def spectra(pieces, place, taps, tables, frames, dests, chan, part=0, parts=1, into=None):
    fine, taps_n = taps.shape[1], taps.shape[0]
    base = fine // RADIX
    keep = chan * dests
    per_res = keep // RADIX
    own, past = PEERS * frames, taps_n - 1
    head_pairs, tail_pairs = own // 2, (past + 1) // 2
    pitch = head_pairs + PITCH
    quads = (head_pairs + tail_pairs + 1) // 2
    step = min(base, 128)
    head_rows, tail_rows = block_rows(chan, own, past)
    dims = (frames, taps_n, base, per_res, dests, chan, head_rows, tail_rows, step)
    weights = (taps.astype(jnp.float32) * (1.0 / 8192.0)).reshape(taps_n, 2, 2, base)
    weights = weights.transpose(2, 3, 1, 0).reshape(2, base, 2 * taps_n)
    blocks = [piece.reshape(frames, 2, base, LANES) for piece in pieces]
    whole = lambda shape: pl.BlockSpec(shape, lambda i, p: (0,) * len(shape))
    return pl.pallas_call(
        functools.partial(spectra_kernel, dims),
        grid_spec=pltpu.PrefetchScalarGridSpec(
            num_scalar_prefetch=1,
            grid=(base // step,),
            in_specs=[pl.BlockSpec((frames, 2, step, LANES), lambda i, p: (0, 0, i, 0))] * PEERS
            + [whole(weights.shape)]
            + [whole(table.shape) for table in tables]
            + [pl.BlockSpec(memory_space=pl.ANY)] * (into is not None),
            out_specs=pl.BlockSpec((dests, head_rows + tail_rows, LANES), lambda i, p: (0, part, 0)),
            scratch_shapes=[
                pltpu.VMEM((own, 2, step, LANES), jnp.float32),
                pltpu.VMEM((2, 2 * (head_pairs + tail_pairs), 16, LANES), jnp.float32),
                pltpu.VMEM((quads, RADIX * base, 2 * LANES), jnp.bfloat16),
                pltpu.VMEM((keep * pitch, LANES), jnp.float32),
                pltpu.VMEM((keep * tail_pairs + 16, LANES), jnp.float32),
            ],
        ),
        out_shape=jax.ShapeDtypeStruct((dests, parts * (head_rows + tail_rows), LANES), jnp.bfloat16),
        input_output_aliases={} if into is None else {PEERS + 4: 0},
        compiler_params=pltpu.CompilerParams(vmem_limit_bytes=56 * MIB),
        name="spectra",
    )(place, *blocks, weights, *tables, *([] if into is None else [into]))


def sort_kernel(dims, source, out, tails):
    planes, cores, own, past, chan = dims
    head_pairs, tail_pairs = own // 2, (past + 1) // 2
    head_rows, tail_rows = block_rows(chan, own, past)
    depth = planes * own
    per_step = out.shape[0]
    at = pl.program_id(0)

    @pl.when(at == 0)
    def _():
        def widen(d, carry):
            tails[d, pl.ds(0, tail_rows), :] = source[d, pl.ds(head_rows, tail_rows), :].astype(jnp.float32)
            tails[d, pl.ds(tail_rows, 8), :] = jnp.zeros((8, LANES), jnp.float32)
            return carry

        lax.fori_loop(0, (planes - 1) * PEERS * cores, widen, 0)

    early = lax.broadcasted_iota(jnp.int32, (head_pairs, LANES), 0) < tail_pairs
    head_at = pl.ds(pl.multiple_of(at * per_step * head_pairs, 16), per_step * head_pairs)
    for z in range(planes):
        for c in range(cores):
            both = [source[(z * PEERS + q) * cores + c, head_at, :].astype(jnp.float32) for q in range(PEERS)]
            for e in range(per_step):
                value = [v[e * head_pairs : (e + 1) * head_pairs] for v in both]
                if z:
                    tail_at = pl.ds((at * per_step + e) * tail_pairs, head_pairs)
                    for q in range(PEERS):
                        late = tails[((z - 1) * PEERS + q) * cores + c, tail_at, :]
                        value[q] = value[q] + jnp.where(early, late, 0.0)
                value = blocks_transposed(value)
                for part in range(2):
                    rows = jnp.concatenate([value[part], value[2 + part]], 0).astype(jnp.bfloat16)
                    out[e, pl.ds(part * depth + z * own, own), pl.ds(c * LANES, LANES)] = rows


def sort(received, part, planes, cores, own, past, chan):
    head_rows, tail_rows = block_rows(chan, own, past)
    per_step = 2
    shape = (chan, 2 * planes * own, cores * LANES)
    return pl.pallas_call(
        functools.partial(sort_kernel, (planes, cores, own, past, chan)),
        grid=(chan // per_step,),
        in_specs=[pl.BlockSpec((received.shape[0], head_rows + tail_rows, LANES), lambda i: (0, part, 0))],
        out_specs=pl.BlockSpec((per_step, *shape[1:]), lambda i: (i, 0, 0)),
        scratch_shapes=[pltpu.VMEM((received.shape[0], tail_rows + 8, LANES), jnp.float32)],
        out_shape=jax.ShapeDtypeStruct(shape, jnp.bfloat16),
        compiler_params=pltpu.CompilerParams(vmem_limit_bytes=40 * MIB),
        name="sort",
    )(received)


def gram_kernel(dims, *refs):
    here, chunks, cores, scale, last = dims
    ins = refs[:here]
    out, stacked, turned, rows_out, cols_out, sems = refs[here + last :]
    per_step = ins[0].shape[0]
    depth = ins[0].shape[1] // 2
    width = here * LANES
    at, steps = pl.program_id(0), pl.num_programs(0)
    slot = at % 2
    exact = math.frexp(scale)[0] == 0.5

    def copies(step):
        half = step % 2
        moves = []
        for e in range(per_step):
            ch = step * per_step + e
            for c in range(cores):
                base = c * chunks * LANES
                if last:
                    old = width - LANES
                    moves.append((rows_out.at[half, e, c], out.at[ch, pl.ds(base + old, LANES), :]))
                    for d in range(cores):
                        moves.append(
                            (
                                cols_out.at[half, e, pl.ds(c * old, old), pl.ds(d * LANES, LANES)],
                                out.at[ch, pl.ds(base, old), pl.ds(d * chunks * LANES + old, LANES)],
                            )
                        )
                else:
                    for d in range(cores):
                        moves.append(
                            (
                                rows_out.at[half, e, pl.ds(c * width, width), pl.ds(d * width, width)],
                                out.at[ch, pl.ds(base, width), pl.ds(d * chunks * LANES, width)],
                            )
                        )
        return [pltpu.make_async_copy(a, b, sems.at[half, k]) for k, (a, b) in enumerate(moves)]

    @pl.when(at >= 2)
    def _():
        for copy in copies(at - 2):
            copy.wait()

    for e in range(per_step):
        for c in range(cores):
            for h in range(here):
                block = ins[h][e, :, c * LANES : (c + 1) * LANES]
                column = pl.ds((c * here + h) * LANES, LANES)
                stacked[e, :, column] = block
                turned[e, 0:depth, column] = -block[depth:]
                turned[e, depth:, column] = block[:depth]

    def left(e, lo, hi):
        value = stacked[e, :, lo:hi].T
        return value * jnp.bfloat16(scale) if exact else value

    def product(rows, value):
        value = jnp.dot(rows, value, preferred_element_type=jnp.float32)
        return value if exact else value * scale

    def narrow(value):
        return value.astype(jnp.bfloat16)

    def diagonal(size):
        shape = (size, size)
        return lax.broadcasted_iota(jnp.int32, shape, 0) <= lax.broadcasted_iota(jnp.int32, shape, 1)

    inputs = cores * width
    if last:
        old = width - LANES
        mask = diagonal(LANES)
        for e in range(per_step):
            for c in range(cores):
                rows = left(e, c * width, c * width + old)
                columns = [
                    (stacked if c <= d else turned)[e, :, d * width + old : (d + 1) * width] for d in range(cores)
                ]
                cols_out[slot, e, pl.ds(c * old, old), :] = narrow(product(rows, jnp.concatenate(columns, 1)))
                lo, hi = c * width + old, (c + 1) * width
                rows = left(e, lo, hi)
                rows_out[slot, e, c, :, 0:lo] = narrow(product(rows, turned[e, :, 0:lo]))
                mixed = jnp.where(mask, product(rows, stacked[e, :, lo:hi]), product(rows, turned[e, :, lo:hi]))
                rows_out[slot, e, c, :, lo:hi] = narrow(mixed)
                if hi < inputs:
                    rows_out[slot, e, c, :, hi:inputs] = narrow(product(rows, stacked[e, :, hi:inputs]))
    else:
        block = 2 * LANES
        mask = diagonal(block)
        for e in range(per_step):
            for i in range(inputs // block):
                lo, hi = i * block, (i + 1) * block
                rows, place = left(e, lo, hi), pl.ds(lo, block)
                if lo:
                    rows_out[slot, e, place, 0:lo] = narrow(product(rows, turned[e, :, 0:lo]))
                mixed = jnp.where(mask, product(rows, stacked[e, :, lo:hi]), product(rows, turned[e, :, lo:hi]))
                rows_out[slot, e, place, lo:hi] = narrow(mixed)
                if hi < inputs:
                    rows_out[slot, e, place, hi:inputs] = narrow(product(rows, stacked[e, :, hi:inputs]))

    for copy in copies(at):
        copy.start()

    @pl.when(at == steps - 1)
    def _():
        if steps > 1:
            for copy in copies(at - 1):
                copy.wait()
        for copy in copies(at):
            copy.wait()


def gram(sorted_chunks, chunks, cores, scale, before=None):
    chan, depth, wide = sorted_chunks[0].shape
    here = len(sorted_chunks)
    last = before is not None
    per_step = 2
    inputs = cores * here * LANES
    old = (here - 1) * LANES
    count = per_step * (cores + cores * cores if last else cores * cores)
    rows_shape = (2, per_step, cores, LANES, inputs) if last else (2, per_step, inputs, inputs)
    cols_shape = (2, per_step, cores * old, cores * LANES) if last else (16, LANES)
    total = cores * chunks * LANES
    return pl.pallas_call(
        functools.partial(gram_kernel, (here, chunks, cores, scale, last)),
        grid=(chan // per_step,),
        in_specs=[pl.BlockSpec((per_step, depth, wide), lambda i: (i, 0, 0))] * here
        + [pl.BlockSpec(memory_space=pl.ANY)] * last,
        out_specs=pl.BlockSpec(memory_space=pl.ANY),
        scratch_shapes=[
            pltpu.VMEM((per_step, depth, inputs), jnp.bfloat16),
            pltpu.VMEM((per_step, depth, inputs), jnp.bfloat16),
            pltpu.VMEM(rows_shape, jnp.bfloat16),
            pltpu.VMEM(cols_shape, jnp.bfloat16),
            pltpu.SemaphoreType.DMA((2, count)),
        ],
        out_shape=jax.ShapeDtypeStruct((chan, total, total), jnp.bfloat16),
        input_output_aliases={here: 0} if last else {},
        compiler_params=pltpu.CompilerParams(vmem_limit_bytes=56 * MIB),
        name="gram_last" if last else "gram_first",
    )(*sorted_chunks, *([before] if last else []))


PITCH = 1
GROUPS = [[0], [1], [2], [3]]
FIRST = False
TIES = [4, 4, 4]


def per_device(voltages, taps):
    past, fine = taps.shape[0] - 1, taps.shape[1]
    frames = voltages.shape[1] // fine
    chunks = voltages.shape[2] // LANES
    n_time, n_group = lax.axis_size("tm"), lax.axis_size("inp")
    dests = n_time * n_group
    chan = KEEP // dests
    own = PEERS * frames
    place = jnp.bitwise_and(lax.axis_index("tm"), PEERS - 1).astype(jnp.int32)[None]
    tables = [jnp.asarray(table.astype(jnp.bfloat16)) for table in dft_tables(fine, KEEP)]

    planes, scale = n_time // PEERS, 1.0 / (n_time * frames)

    def sent(h, after):
        here = lax.optimization_barrier((place, after))[0] if after else place
        pieces = pack(voltages, here, h, fine)
        others = [lax.ppermute(pieces[k], "tm", [(t, t ^ k) for t in range(n_time)]) for k in range(1, PEERS)]
        return [pieces[0], *others]

    groups = GROUPS if chunks == 4 else [[h] for h in range(chunks)]
    moved = [sent(0, [])]
    packed = moved[0][0]
    received, ordered = [], [None] * chunks
    for g, group in enumerate(groups):
        mine = None
        for part, h in enumerate(group):
            if g >= 2 and not part:
                moved[h][0], received[g - 2] = lax.optimization_barrier((moved[h][0], received[g - 2]))
            if h == 0:
                moved.append(sent(1, [packed, moved[0][1]] if FIRST else [packed]))
            mine = spectra(moved[h], place, taps, tables, frames, dests, chan, part, len(group), mine)
            if h == 0 and len(groups[1]) > 1:
                moved.append(sent(2, [moved[1][1]]))
            elif h + 2 < chunks and len(moved) < h + 3:
                moved.append(sent(h + 2, [mine]))
        h += 1
        if h < chunks:
            k = TIES[g]
            mine, moved[h][1:k] = lax.optimization_barrier((mine, moved[h][1:k]))
        if received:
            mine, received[-1] = lax.optimization_barrier((mine, received[-1]))
        received.append(lax.all_to_all(mine, ("tm", "inp"), split_axis=0, concat_axis=0, tiled=True))
    for array, group in zip(received, groups):
        for part, h in enumerate(group):
            ordered[h] = sort(array, part, planes, n_group, own, past, chan)
    first = gram(ordered[:-1], chunks, n_group, scale)
    return gram(ordered, chunks, n_group, scale, first)


def solution(mesh):
    return jax.shard_map(
        per_device,
        mesh=mesh,
        in_specs=(P(None, "tm", "inp"), P()),
        out_specs=P(("tm", "inp"), None, None),
        check_vma=False,
    )
```

time: 1060 us -> 273 us (0.26)
  local copies, waits for them, and re-layouts: 354 us -> 19.8 us
  waiting for transfers between devices: 418 us -> 123 us
  starting transfers between devices: 164 us -> 35.7 us
  Pallas kernels: 0 us -> 92.6 us
  matrix products: 66 us -> 0 us
  other arithmetic: 47.8 us -> 0.01 us
    mul x2 -> x0, local copies, waits for them, and re-layouts: 268 us -> none  [finish(): products.reshape(chan_count, 2, all_inputs, all_inputs) * (1.0 / spec_total)]
    ppermute x3 -> x12, waiting for transfers between devices: 325 us -> 72.5 us  [sent(): lax.ppermute(pieces[k], 'tm', [(t, t ^ k) for t in range(n_time)])]
    all_to_all x1 -> x4, starting transfers between devices: 149 us -> 17.8 us  [per_device(): lax.all_to_all(mine, ('tm', 'inp'), split_axis=0, concat_axis=0, tiled=True)]
    pallas_call x0 -> x14, Pallas kernels: none -> 92.6 us  [the longest x4 47.9 us: spectra(): pl.pallas_call(functools.partial(spectra_kernel, dims), grid_spec=pltpu.P...]
    dot_general x2 -> x0, matrix products: 66 us -> none  [the longest x1 38.7 us: per_device(): jnp.einsum('rfna,rnsj->jsfa', filtered, dft_matrix, preferred_element_typ...]
    all_to_all x1 -> x4, waiting for transfers between devices: 92.5 us -> 50.8 us  [per_device(): lax.all_to_all(mine, ('tm', 'inp'), split_axis=0, concat_axis=0, tiled=True)]
    convert_element_type x2 -> x0, other arithmetic: 32.4 us -> none  [the longest x1 32.4 us: finish(): jnp.where(upper_mask[None], visibility[:, 0], visibility[:, 1])]
    reshape x3, local copies, waits for them, and re-layouts: 30.6 us -> 0.94 us  [the longest x1 0.88 us: spectra(): weights = weights.transpose(2, 3, 1, 0).reshape(2, base, 2 * taps_n)]
  transfers between devices with their start and end apart: 4 -> 16, of which waited for: 3 -> 11; matrix products, arithmetic and copies ran while one was open for 3% -> 0% of each run, Pallas kernels for 0% -> 28%
where the time goes in v2:
time: 273 us; the launch traced here: 272 us
  waiting for transfers between devices  123 us (45%)
  Pallas kernels  92.6 us (34%)
  starting transfers between devices  35.7 us (13%)
  local copies, waits for them, and re-layouts  19.8 us (7%)
    ppermute x12, waiting for transfers between devices, sent(): lax.ppermute(pieces[k], 'tm', [(t, t ^ k) for t in range(n_time)])  72.5 us
    all_to_all x4, waiting for transfers between devices, per_device(): lax.all_to_all(mine, ('tm', 'inp'), split_axis=0, concat_axis=0, tiled=True)  50.8 us
    pallas_call x4, Pallas kernels, spectra(): pl.pallas_call(functools.partial(spectra_kernel, dims), grid_spec=pltpu.P...  47.9 us
    pallas_call x2, Pallas kernels, gram(): pl.pallas_call(functools.partial(gram_kernel, (here, chunks, cores, scale...  24.2 us
    unnamed x40, local copies, waits for them, and re-layouts  18.8 us
    ppermute x12, starting transfers between devices, sent(): lax.ppermute(pieces[k], 'tm', [(t, t ^ k) for t in range(n_time)])  17.9 us
    all_to_all x4, starting transfers between devices, per_device(): lax.all_to_all(mine, ('tm', 'inp'), split_axis=0, concat_axis=0, tiled=True)  17.8 us
    pallas_call x4, Pallas kernels, sort(): pl.pallas_call(functools.partial(sort_kernel, (planes, cores, own, past,...  11.4 us
  transfers between devices with their start and end apart: 16, of which 11 were waited for; matrix products, arithmetic and copies ran while one was open for 0% of the time, Pallas kernels for 28%

profile of v2, /device:TPU:0, one launch (start us, length us, event | category | flops | bytes accessed | tf_op | source)
XLA Modules:
  0.0 271.8 jit_solution(11984487326787413480)
XLA Ops:
  0.0 3.4 %copy-done = bf16[2,4096,512]{2,1,0:T(8,128)(2,1)S(1)} copy-done((bf16[2,4096,512]{2,1,0:T(8,128)(2,1)S(1)}, bf16[2,4096,512]{2,1,0:T(8,128)(2,1)}, u32[]{:S(2)}) %copy-start) | copy-done | bytes 8388632
  17.5 4.7 %collective-permute-done = bf16[2048,128]{1,0:T(8,128)(2,1)S(1)} collective-permute-done((bf16[2048,128]{1,0:T(8,128)(2,1)S(1)}, bf16[2048,128]{1,0:T(8,128)(2,1)S(1)}, u32[]{:S(2)}, u32[]{:S(2)}) %collective-permute-start) | collective-permute-done | bytes 524320 | tf_op jit(solution)/shard_map/ppermute | solution.py:450
  26.1 9.5 %collective-permute-done.1 = bf16[2048,128]{1,0:T(8,128)(2,1)} collective-permute-done((bf16[2048,128]{1,0:T(8,128)(2,1)S(1)}, bf16[2048,128]{1,0:T(8,128)(2,1)}, u32[]{:S(2)}, u32[]{:S(2)}) %collective-permute-start.1) | collective-permute-done | bytes 524320 | tf_op jit(solution)/shard_map/ppermute | solution.py:450
  35.6 12.0 %spectra.4 = bf16[32,224,128]{2,1,0:T(8,128)(2,1)} custom-call(s32[1]{0:T(128)} %bitcast.place, bf16[4,2,256,128]{3,2,1,0:T(8,128)(2,1)} %bitcast.27, bf16[4,2,256,128]{3,2,1,0:T(8,128)(2,1)} %bitcast.33, bf16[4,2,256,128]{3,2,1,0:T(8,128)(2,1)} %bitcast.4.refs_2_, bf16[4,2,256,128]{3,2,1,0:T(8,128)(2,1)} %bitcast.5.refs_3_, f32[2,256,24]{2,1,0:T(8,128)} %copy.8.refs_4_, ...), custom_call_target="tpu_custom_call" | custom-call | tf_op jit(solution)/shard_map/spectra/pallas_call | solution.py:210
  47.6 9.0 %collective-permute-done.4 = bf16[2048,128]{1,0:T(8,128)(2,1)} collective-permute-done((bf16[2048,128]{1,0:T(8,128)(2,1)S(1)}, bf16[2048,128]{1,0:T(8,128)(2,1)}, u32[]{:S(2)}, u32[]{:S(2)}) %collective-permute-start.4) | collective-permute-done | bytes 524320 | tf_op jit(solution)/shard_map/ppermute | solution.py:450
  56.6 4.9 %all-to-all-start = ((bf16[32,224,128]{2,1,0:T(8,128)(2,1)}), bf16[32,224,128]{2,1,0:T(8,128)(2,1)S(1)}, u32[]{:S(2)}, u32[]{:S(2)}) async-start(bf16[32,224,128]{2,1,0:T(8,128)(2,1)} %spectra.4), calls=%async_computation | async-start | bytes 3670016 | tf_op jit(solution)/shard_map/all_to_all | solution.py:475
  61.6 3.4 %copy-done.1 = bf16[2,4096,512]{2,1,0:T(8,128)(2,1)S(1)} copy-done((bf16[2,4096,512]{2,1,0:T(8,128)(2,1)S(1)}, bf16[2,4096,512]{2,1,0:T(8,128)(2,1)}, u32[]{:S(2)}) %copy-start.1) | copy-done | bytes 8388632
  71.5 12.0 %spectra.5 = bf16[32,224,128]{2,1,0:T(8,128)(2,1)} custom-call(s32[1]{0:T(128)} %bitcast.place, bf16[4,2,256,128]{3,2,1,0:T(8,128)(2,1)} %bitcast.25, bf16[4,2,256,128]{3,2,1,0:T(8,128)(2,1)} %bitcast.29, bf16[4,2,256,128]{3,2,1,0:T(8,128)(2,1)} %bitcast.10.refs_2_, bf16[4,2,256,128]{3,2,1,0:T(8,128)(2,1)} %bitcast.11.refs_3_, f32[2,256,24]{2,1,0:T(8,128)} %copy.8.refs_4_, ...), custom_call_target="tpu_custom_call" | custom-call | tf_op jit(solution)/shard_map/spectra/pallas_call | solution.py:210
  83.5 9.6 %collective-permute-done.6 = bf16[2048,128]{1,0:T(8,128)(2,1)S(1)} collective-permute-done((bf16[2048,128]{1,0:T(8,128)(2,1)S(1)}, bf16[2048,128]{1,0:T(8,128)(2,1)S(1)}, u32[]{:S(2)}, u32[]{:S(2)}) %collective-permute-start.6) | collective-permute-done | bytes 524320 | tf_op jit(solution)/shard_map/ppermute | solution.py:450
  93.1 6.4 %collective-permute-done.7 = bf16[2048,128]{1,0:T(8,128)(2,1)S(1)} collective-permute-done((bf16[2048,128]{1,0:T(8,128)(2,1)S(1)}, bf16[2048,128]{1,0:T(8,128)(2,1)S(1)}, u32[]{:S(2)}, u32[]{:S(2)}) %collective-permute-start.7) | collective-permute-done | bytes 524320 | tf_op jit(solution)/shard_map/ppermute | solution.py:450
  99.5 8.7 %collective-permute-done.8 = bf16[2048,128]{1,0:T(8,128)(2,1)S(1)} collective-permute-done((bf16[2048,128]{1,0:T(8,128)(2,1)S(1)}, bf16[2048,128]{1,0:T(8,128)(2,1)S(1)}, u32[]{:S(2)}, u32[]{:S(2)}) %collective-permute-start.8) | collective-permute-done | bytes 524320 | tf_op jit(solution)/shard_map/ppermute | solution.py:450
  109.0 4.3 %all-to-all-start.1 = ((bf16[32,224,128]{2,1,0:T(8,128)(2,1)}), bf16[32,224,128]{2,1,0:T(8,128)(2,1)}, u32[]{:S(2)}, u32[]{:S(2)}) async-start(bf16[32,224,128]{2,1,0:T(8,128)(2,1)} %spectra.5), calls=%async_computation.1 | async-start | bytes 3670016 | tf_op jit(solution)/shard_map/all_to_all | solution.py:475
  113.4 3.4 %copy-done.2 = bf16[2,4096,512]{2,1,0:T(8,128)(2,1)S(1)} copy-done((bf16[2,4096,512]{2,1,0:T(8,128)(2,1)S(1)}, bf16[2,4096,512]{2,1,0:T(8,128)(2,1)}, u32[]{:S(2)}) %copy-start.2) | copy-done | bytes 8388632
  123.3 11.9 %spectra.6 = bf16[32,224,128]{2,1,0:T(8,128)(2,1)} custom-call(s32[1]{0:T(128)} %bitcast.place, bf16[4,2,256,128]{3,2,1,0:T(8,128)(2,1)} %bitcast.26, bf16[4,2,256,128]{3,2,1,0:T(8,128)(2,1)} %bitcast.30, bf16[4,2,256,128]{3,2,1,0:T(8,128)(2,1)} %bitcast.31, bf16[4,2,256,128]{3,2,1,0:T(8,128)(2,1)} %bitcast.32, f32[2,256,24]{2,1,0:T(8,128)} %copy.8.refs_4_, ...), custom_call_target="tpu_custom_call" | custom-call | tf_op jit(solution)/shard_map/spectra/pallas_call | solution.py:210
  135.3 9.5 %collective-permute-done.9 = bf16[2048,128]{1,0:T(8,128)(2,1)S(1)} collective-permute-done((bf16[2048,128]{1,0:T(8,128)(2,1)S(1)}, bf16[2048,128]{1,0:T(8,128)(2,1)S(1)}, u32[]{:S(2)}, u32[]{:S(2)}) %collective-permute-start.9) | collective-permute-done | bytes 524320 | tf_op jit(solution)/shard_map/ppermute | solution.py:450
  144.8 6.5 %collective-permute-done.10 = bf16[2048,128]{1,0:T(8,128)(2,1)S(1)} collective-permute-done((bf16[2048,128]{1,0:T(8,128)(2,1)S(1)}, bf16[2048,128]{1,0:T(8,128)(2,1)S(1)}, u32[]{:S(2)}, u32[]{:S(2)}) %collective-permute-start.10) | collective-permute-done | bytes 524320 | tf_op jit(solution)/shard_map/ppermute | solution.py:450
  151.3 8.6 %collective-permute-done.11 = bf16[2048,128]{1,0:T(8,128)(2,1)S(1)} collective-permute-done((bf16[2048,128]{1,0:T(8,128)(2,1)S(1)}, bf16[2048,128]{1,0:T(8,128)(2,1)S(1)}, u32[]{:S(2)}, u32[]{:S(2)}) %collective-permute-start.11) | collective-permute-done | bytes 524320 | tf_op jit(solution)/shard_map/ppermute | solution.py:450
  160.7 4.4 %all-to-all-start.2 = ((bf16[32,224,128]{2,1,0:T(8,128)(2,1)}), bf16[32,224,128]{2,1,0:T(8,128)(2,1)}, u32[]{:S(2)}, u32[]{:S(2)}) async-start(bf16[32,224,128]{2,1,0:T(8,128)(2,1)} %spectra.6), calls=%async_computation.2 | async-start | bytes 3670016 | tf_op jit(solution)/shard_map/all_to_all | solution.py:475
  165.1 12.0 %spectra.7 = bf16[32,224,128]{2,1,0:T(8,128)(2,1)} custom-call(s32[1]{0:T(128)} %bitcast.place, bf16[4,2,256,128]{3,2,1,0:T(8,128)(2,1)} %bitcast.28, bf16[4,2,256,128]{3,2,1,0:T(8,128)(2,1)} %bitcast.34, bf16[4,2,256,128]{3,2,1,0:T(8,128)(2,1)} %bitcast.35, bf16[4,2,256,128]{3,2,1,0:T(8,128)(2,1)} %bitcast.36, f32[2,256,24]{2,1,0:T(8,128)} %copy.8.refs_4_, ...), custom_call_target="tpu_custom_call" | custom-call | tf_op jit(solution)/shard_map/spectra/pallas_call | solution.py:210
  177.1 31.2 %all-to-all-done.2.source = bf16[32,224,128]{2,1,0:T(8,128)(2,1)} async-done(((bf16[32,224,128]{2,1,0:T(8,128)(2,1)}), bf16[32,224,128]{2,1,0:T(8,128)(2,1)}, u32[]{:S(2)}, u32[]{:S(2)}) %all-to-all-start.2) | async-done | bytes 1835040 | tf_op jit(solution)/shard_map/all_to_all | solution.py:475
  208.3 4.1 %all-to-all-start.3 = ((bf16[32,224,128]{2,1,0:T(8,128)(2,1)}), bf16[32,224,128]{2,1,0:T(8,128)(2,1)}, u32[]{:S(2)}, u32[]{:S(2)}) async-start(bf16[32,224,128]{2,1,0:T(8,128)(2,1)} %spectra.7), calls=%async_computation.3 | async-start | bytes 3670016 | tf_op jit(solution)/shard_map/all_to_all | solution.py:475
  223.7 12.4 %gram_first.1.refs_4_ = bf16[16,1024,1024]{2,1,0:T(8,128)(2,1)} custom-call(bf16[16,128,256]{2,1,0:T(8,128)(2,1)} %copy-done.3, bf16[16,128,256]{2,1,0:T(8,128)(2,1)} %copy-done.4, bf16[16,128,256]{2,1,0:T(8,128)(2,1)} %copy-done.5), custom_call_target="tpu_custom_call" | custom-call | tf_op jit(solution)/shard_map/gram_first/pallas_call | solution.py:408
  236.0 19.6 %all-to-all-done.3.source = bf16[32,224,128]{2,1,0:T(8,128)(2,1)} async-done(((bf16[32,224,128]{2,1,0:T(8,128)(2,1)}), bf16[32,224,128]{2,1,0:T(8,128)(2,1)}, u32[]{:S(2)}, u32[]{:S(2)}) %all-to-all-start.3) | async-done | bytes 1835040 | tf_op jit(solution)/shard_map/all_to_all | solution.py:475
  259.8 11.8 %gram_last.1 = bf16[16,1024,1024]{2,1,0:T(8,128)(2,1)} custom-call(bf16[16,128,256]{2,1,0:T(8,128)(2,1)} %copy-done.3, bf16[16,128,256]{2,1,0:T(8,128)(2,1)} %copy-done.4, bf16[16,128,256]{2,1,0:T(8,128)(2,1)} %copy-done.5, bf16[16,128,256]{2,1,0:T(8,128)(2,1)} %copy-done.6, bf16[16,1024,1024]{2,1,0:T(8,128)(2,1)} %gram_first.1.refs_4_), custom_call_target="tpu_custom_call", output_to_operand_aliasing={{}: (4, {})} | custom-call | tf_op jit(solution)/shard_map/gram_last/pallas_call | solution.py:408
  (66 shorter events, 48.2 us)
Async XLA Ops:
  6.5 15.7 %collective-permute-start = (bf16[2048,128]{1,0:T(8,128)(2,1)S(1)}, bf16[2048,128]{1,0:T(8,128)(2,1)S(1)}, u32[]{:S(2)}, u32[]{:S(2)}) collective-permute-start(bf16[2048,128]{1,0:T(8,128)(2,1)S(1)} %get-tuple-element.47), channel_id=1, source_target_pairs={{0,2},{2,0},{4,6},{6,4},{8,10},{10,8},{12,14},{14,12},{16,18},{18,... | collective-permute-start | bytes 1572872 | tf_op jit(solution)/shard_map/ppermute | solution.py:450
  9.4 26.2 %collective-permute-start.1 = (bf16[2048,128]{1,0:T(8,128)(2,1)S(1)}, bf16[2048,128]{1,0:T(8,128)(2,1)}, u32[]{:S(2)}, u32[]{:S(2)}) collective-permute-start(bf16[2048,128]{1,0:T(8,128)(2,1)S(1)} %get-tuple-element.48), channel_id=1, source_target_pairs={{0,4},{2,6},{4,0},{6,2},{8,12},{10,14},{12,8},{14,10},{16,20},{18,... | collective-permute-start | bytes 1572872 | tf_op jit(solution)/shard_map/ppermute | solution.py:450
  10.9 24.7 %collective-permute-start.2 = (bf16[2048,128]{1,0:T(8,128)(2,1)S(1)}, bf16[2048,128]{1,0:T(8,128)(2,1)}, u32[]{:S(2)}, u32[]{:S(2)}) collective-permute-start(bf16[2048,128]{1,0:T(8,128)(2,1)S(1)} %get-tuple-element.49), channel_id=1, source_target_pairs={{0,6},{2,4},{4,2},{6,0},{8,14},{10,12},{12,10},{14,8},{16,22},{18,... | collective-permute-start | bytes 1572872 | tf_op jit(solution)/shard_map/ppermute | solution.py:450
  10.9 14.3 %copy-start.19 = (s32[12,1024]{1,0:T(8,128)S(1)}, s32[12,1024]{1,0:T(8,128)}, u32[]{:S(2)}) copy-start(s32[12,1024]{1,0:T(8,128)} %param.5) | copy-start | bytes 147460
  14.0 33.6 %collective-permute-start.3 = (bf16[2048,128]{1,0:T(8,128)(2,1)S(1)}, bf16[2048,128]{1,0:T(8,128)(2,1)S(1)}, u32[]{:S(2)}, u32[]{:S(2)}) collective-permute-start(bf16[2048,128]{1,0:T(8,128)(2,1)S(1)} %get-tuple-element.54), channel_id=1, source_target_pairs={{0,2},{2,0},{4,6},{6,4},{8,10},{10,8},{12,14},{14,12},{16,18},{18,... | collective-permute-start | bytes 1572872 | tf_op jit(solution)/shard_map/ppermute | solution.py:450
  16.0 40.6 %collective-permute-start.4 = (bf16[2048,128]{1,0:T(8,128)(2,1)S(1)}, bf16[2048,128]{1,0:T(8,128)(2,1)}, u32[]{:S(2)}, u32[]{:S(2)}) collective-permute-start(bf16[2048,128]{1,0:T(8,128)(2,1)S(1)} %get-tuple-element.55), channel_id=1, source_target_pairs={{0,4},{2,6},{4,0},{6,2},{8,12},{10,14},{12,8},{14,10},{16,20},{18,... | collective-permute-start | bytes 1572872 | tf_op jit(solution)/shard_map/ppermute | solution.py:450
  22.2 34.4 %collective-permute-start.5 = (bf16[2048,128]{1,0:T(8,128)(2,1)S(1)}, bf16[2048,128]{1,0:T(8,128)(2,1)}, u32[]{:S(2)}, u32[]{:S(2)}) collective-permute-start(bf16[2048,128]{1,0:T(8,128)(2,1)S(1)} %get-tuple-element.56), channel_id=1, source_target_pairs={{0,6},{2,4},{4,2},{6,0},{8,14},{10,12},{12,10},{14,8},{16,22},{18,... | collective-permute-start | bytes 1572872 | tf_op jit(solution)/shard_map/ppermute | solution.py:450
  47.6 9.0 %copy-start.11 = (bf16[2048,128]{1,0:T(8,128)(2,1)}, bf16[2048,128]{1,0:T(8,128)(2,1)S(1)}, u32[]{:S(2)}) copy-start(bf16[2048,128]{1,0:T(8,128)(2,1)S(1)} %collective-permute-done.3) | copy-start | bytes 1572868
  56.6 51.6 %all-to-all-start = ((bf16[32,224,128]{2,1,0:T(8,128)(2,1)}), bf16[32,224,128]{2,1,0:T(8,128)(2,1)S(1)}, u32[]{:S(2)}, u32[]{:S(2)}) async-start(bf16[32,224,128]{2,1,0:T(8,128)(2,1)} %spectra.4), calls=%async_computation | async-start | bytes 3670016 | tf_op jit(solution)/shard_map/all_to_all | solution.py:475
  61.5 3.4 %copy-start.1 = (bf16[2,4096,512]{2,1,0:T(8,128)(2,1)S(1)}, bf16[2,4096,512]{2,1,0:T(8,128)(2,1)}, u32[]{:S(2)}) copy-start(bf16[2,4096,512]{2,1,0:T(8,128)(2,1)} %param.4) | copy-start | bytes 25165828
  68.0 25.1 %collective-permute-start.6 = (bf16[2048,128]{1,0:T(8,128)(2,1)S(1)}, bf16[2048,128]{1,0:T(8,128)(2,1)S(1)}, u32[]{:S(2)}, u32[]{:S(2)}) collective-permute-start(bf16[2048,128]{1,0:T(8,128)(2,1)S(1)} %get-tuple-element.60), channel_id=1, source_target_pairs={{0,2},{2,0},{4,6},{6,4},{8,10},{10,8},{12,14},{14,12},{16,18},{18,... | collective-permute-start | bytes 1572872 | tf_op jit(solution)/shard_map/ppermute | solution.py:450
  69.8 29.7 %collective-permute-start.7 = (bf16[2048,128]{1,0:T(8,128)(2,1)S(1)}, bf16[2048,128]{1,0:T(8,128)(2,1)S(1)}, u32[]{:S(2)}, u32[]{:S(2)}) collective-permute-start(bf16[2048,128]{1,0:T(8,128)(2,1)S(1)} %get-tuple-element.61), channel_id=1, source_target_pairs={{0,4},{2,6},{4,0},{6,2},{8,12},{10,14},{12,8},{14,10},{16,20},{18,... | collective-permute-start | bytes 1572872 | tf_op jit(solution)/shard_map/ppermute | solution.py:450
  71.3 36.9 %collective-permute-start.8 = (bf16[2048,128]{1,0:T(8,128)(2,1)S(1)}, bf16[2048,128]{1,0:T(8,128)(2,1)S(1)}, u32[]{:S(2)}, u32[]{:S(2)}) collective-permute-start(bf16[2048,128]{1,0:T(8,128)(2,1)S(1)} %get-tuple-element.62), channel_id=1, source_target_pairs={{0,6},{2,4},{4,2},{6,0},{8,14},{10,12},{12,10},{14,8},{16,22},{18,... | collective-permute-start | bytes 1572872 | tf_op jit(solution)/shard_map/ppermute | solution.py:450
  93.1 15.1 %copy-start.12 = (bf16[2048,128]{1,0:T(8,128)(2,1)}, bf16[2048,128]{1,0:T(8,128)(2,1)S(1)}, u32[]{:S(2)}) copy-start(bf16[2048,128]{1,0:T(8,128)(2,1)S(1)} %collective-permute-done.6) | copy-start | bytes 1572868
  99.5 8.7 %copy-start.13 = (bf16[2048,128]{1,0:T(8,128)(2,1)}, bf16[2048,128]{1,0:T(8,128)(2,1)S(1)}, u32[]{:S(2)}) copy-start(bf16[2048,128]{1,0:T(8,128)(2,1)S(1)} %collective-permute-done.7) | copy-start | bytes 1572868
  109.0 50.9 %all-to-all-start.1 = ((bf16[32,224,128]{2,1,0:T(8,128)(2,1)}), bf16[32,224,128]{2,1,0:T(8,128)(2,1)}, u32[]{:S(2)}, u32[]{:S(2)}) async-start(bf16[32,224,128]{2,1,0:T(8,128)(2,1)} %spectra.5), calls=%async_computation.1 | async-start | bytes 3670016 | tf_op jit(solution)/shard_map/all_to_all | solution.py:475
  113.4 3.4 %copy-start.2 = (bf16[2,4096,512]{2,1,0:T(8,128)(2,1)S(1)}, bf16[2,4096,512]{2,1,0:T(8,128)(2,1)}, u32[]{:S(2)}) copy-start(bf16[2,4096,512]{2,1,0:T(8,128)(2,1)} %param.4) | copy-start | bytes 25165828
  119.9 25.0 %collective-permute-start.9 = (bf16[2048,128]{1,0:T(8,128)(2,1)S(1)}, bf16[2048,128]{1,0:T(8,128)(2,1)S(1)}, u32[]{:S(2)}, u32[]{:S(2)}) collective-permute-start(bf16[2048,128]{1,0:T(8,128)(2,1)S(1)} %get-tuple-element.73), channel_id=1, source_target_pairs={{0,2},{2,0},{4,6},{6,4},{8,10},{10,8},{12,14},{14,12},{16,18},{18,... | collective-permute-start | bytes 1572872 | tf_op jit(solution)/shard_map/ppermute | solution.py:450
  121.6 29.8 %collective-permute-start.10 = (bf16[2048,128]{1,0:T(8,128)(2,1)S(1)}, bf16[2048,128]{1,0:T(8,128)(2,1)S(1)}, u32[]{:S(2)}, u32[]{:S(2)}) collective-permute-start(bf16[2048,128]{1,0:T(8,128)(2,1)S(1)} %get-tuple-element.74), channel_id=1, source_target_pairs={{0,4},{2,6},{4,0},{6,2},{8,12},{10,14},{12,8},{14,10},{16,20},{18,... | collective-permute-start | bytes 1572872 | tf_op jit(solution)/shard_map/ppermute | solution.py:450
  123.0 36.9 %collective-permute-start.11 = (bf16[2048,128]{1,0:T(8,128)(2,1)S(1)}, bf16[2048,128]{1,0:T(8,128)(2,1)S(1)}, u32[]{:S(2)}, u32[]{:S(2)}) collective-permute-start(bf16[2048,128]{1,0:T(8,128)(2,1)S(1)} %get-tuple-element.75), channel_id=1, source_target_pairs={{0,6},{2,4},{4,2},{6,0},{8,14},{10,12},{12,10},{14,8},{16,22},{18,... | collective-permute-start | bytes 1572872 | tf_op jit(solution)/shard_map/ppermute | solution.py:450
  144.8 15.1 %copy-start.16 = (bf16[2048,128]{1,0:T(8,128)(2,1)}, bf16[2048,128]{1,0:T(8,128)(2,1)S(1)}, u32[]{:S(2)}) copy-start(bf16[2048,128]{1,0:T(8,128)(2,1)S(1)} %collective-permute-done.9) | copy-start | bytes 1572868
  151.3 8.6 %copy-start.17 = (bf16[2048,128]{1,0:T(8,128)(2,1)}, bf16[2048,128]{1,0:T(8,128)(2,1)S(1)}, u32[]{:S(2)}) copy-start(bf16[2048,128]{1,0:T(8,128)(2,1)S(1)} %collective-permute-done.10) | copy-start | bytes 1572868
  160.7 47.6 %all-to-all-start.2 = ((bf16[32,224,128]{2,1,0:T(8,128)(2,1)}), bf16[32,224,128]{2,1,0:T(8,128)(2,1)}, u32[]{:S(2)}, u32[]{:S(2)}) async-start(bf16[32,224,128]{2,1,0:T(8,128)(2,1)} %spectra.6), calls=%async_computation.2 | async-start | bytes 3670016 | tf_op jit(solution)/shard_map/all_to_all | solution.py:475
  208.3 47.4 %all-to-all-start.3 = ((bf16[32,224,128]{2,1,0:T(8,128)(2,1)}), bf16[32,224,128]{2,1,0:T(8,128)(2,1)}, u32[]{:S(2)}, u32[]{:S(2)}) async-start(bf16[32,224,128]{2,1,0:T(8,128)(2,1)} %spectra.7), calls=%async_computation.3 | async-start | bytes 3670016 | tf_op jit(solution)/shard_map/all_to_all | solution.py:475
  (12 other events, 15.2 us)

commit v3 on v2

--- a/solution.py
+++ b/solution.py
@@ -54,36 +54,42 @@
     return out
 
 
-def pack_kernel(place, source, *refs):
-    outs, select = refs[:PEERS], refs[PEERS]
-
-    @pl.when(pl.program_id(0) == 0)
-    def _():
-        shape = select.shape
-        row, column = (lax.broadcasted_iota(jnp.int32, shape, axis) for axis in range(2))
-        peer = jnp.bitwise_xor(column // LANES, place[0])
-        wanted = (column % LANES) // SUB * LANES + peer * SUB + column % SUB
-        select[...] = jnp.where(row == wanted, 1.0, 0.0).astype(jnp.bfloat16)
-
-    x = jnp.concatenate([source[r, 0, upper] for upper in range(2) for r in range(2)], 1)
-    moved = jnp.dot(x, select[...], preferred_element_type=jnp.float32).astype(jnp.bfloat16)
-    for k in range(PEERS):
-        outs[k][...] = moved[:, k * LANES : (k + 1) * LANES]
+def pack_kernel(chunk, place, source, *refs):
+    outs, (select, held, sems) = refs[:PEERS], refs[PEERS:]
+    frames, rows = held.shape[1], held.shape[3]
+    copies = [
+        pltpu.make_async_copy(source.at[:, f, :, :, pl.ds(chunk * LANES, LANES)], held.at[:, f], sems.at[f])
+        for f in range(frames)
+    ]
+    for copy in copies:
+        copy.start()
+    shape = select.shape
+    row, column = (lax.broadcasted_iota(jnp.int32, shape, axis) for axis in range(2))
+    peer = jnp.bitwise_xor(column // LANES, place[0])
+    wanted = (column % LANES) // SUB * LANES + peer * SUB + column % SUB
+    select[...] = jnp.where(row == wanted, 1.0, 0.0).astype(jnp.bfloat16)
+    for f in range(frames):
+        copies[f].wait()
+        x = jnp.concatenate([held[r, f, upper] for upper in range(2) for r in range(2)], 1)
+        moved = jnp.dot(x, select[...], preferred_element_type=jnp.float32).astype(jnp.bfloat16)
+        for k in range(PEERS):
+            outs[k][pl.ds(f * rows, rows), :] = moved[:, k * LANES : (k + 1) * LANES]
 
 
 def pack(voltages, place, chunk, fine):
     frames = voltages.shape[1] // fine
     rows = fine // 2
     shaped = voltages.reshape(2, frames, 2, rows, voltages.shape[2])
+    shaped = pltpu.with_memory_space_constraint(shaped, pltpu.HBM)
     return pl.pallas_call(
-        pack_kernel,
-        grid_spec=pltpu.PrefetchScalarGridSpec(
-            num_scalar_prefetch=1,
-            grid=(frames,),
-            in_specs=[pl.BlockSpec((2, 1, 2, rows, LANES), lambda i, p: (0, i, 0, 0, chunk))],
-            out_specs=[pl.BlockSpec((rows, LANES), lambda i, p: (i, 0))] * PEERS,
-            scratch_shapes=[pltpu.VMEM((PEERS * LANES, PEERS * LANES), jnp.bfloat16)],
-        ),
+        functools.partial(pack_kernel, chunk),
+        in_specs=[pl.BlockSpec(memory_space=pltpu.SMEM), pl.BlockSpec(memory_space=pltpu.HBM)],
+        out_specs=[pl.BlockSpec((frames * rows, LANES), lambda: (0, 0))] * PEERS,
+        scratch_shapes=[
+            pltpu.VMEM((PEERS * LANES, PEERS * LANES), jnp.bfloat16),
+            pltpu.VMEM((2, frames, 2, rows, LANES), jnp.bfloat16),
+            pltpu.SemaphoreType.DMA((frames,)),
+        ],
         out_shape=[jax.ShapeDtypeStruct((frames * rows, LANES), jnp.bfloat16)] * PEERS,
         compiler_params=pltpu.CompilerParams(vmem_limit_bytes=40 * MIB),
         name="pack",
@@ -269,7 +275,7 @@
 
 def sort(received, part, planes, cores, own, past, chan):
     head_rows, tail_rows = block_rows(chan, own, past)
-    per_step = 2
+    per_step = min(chan, SORT_STEP)
     shape = (chan, 2 * planes * own, cores * LANES)
     return pl.pallas_call(
         functools.partial(sort_kernel, (planes, cores, own, past, chan)),
@@ -294,10 +300,10 @@
     slot = at % 2
     exact = math.frexp(scale)[0] == 0.5
 
-    def copies(step):
+    def copies(step, channels=None):
         half = step % 2
         moves = []
-        for e in range(per_step):
+        for e in range(per_step) if channels is None else channels:
             ch = step * per_step + e
             for c in range(cores):
                 base = c * chunks * LANES
@@ -319,7 +325,8 @@
                                 out.at[ch, pl.ds(base, width), pl.ds(d * chunks * LANES, width)],
                             )
                         )
-        return [pltpu.make_async_copy(a, b, sems.at[half, k]) for k, (a, b) in enumerate(moves)]
+        skip = 0 if channels is None else channels[0] * len(moves)
+        return [pltpu.make_async_copy(a, b, sems.at[half, skip + k]) for k, (a, b) in enumerate(moves)]
 
     @pl.when(at >= 2)
     def _():
@@ -368,6 +375,8 @@
                 rows_out[slot, e, c, :, lo:hi] = narrow(mixed)
                 if hi < inputs:
                     rows_out[slot, e, c, :, hi:inputs] = narrow(product(rows, stacked[e, :, hi:inputs]))
+            for copy in copies(at, [e]):
+                copy.start()
     else:
         block = 2 * LANES
         mask = diagonal(block)
@@ -381,9 +390,8 @@
                 rows_out[slot, e, place, lo:hi] = narrow(mixed)
                 if hi < inputs:
                     rows_out[slot, e, place, hi:inputs] = narrow(product(rows, stacked[e, :, hi:inputs]))
-
-    for copy in copies(at):
-        copy.start()
+            for copy in copies(at, [e]):
+                copy.start()
 
     @pl.when(at == steps - 1)
     def _():
@@ -398,7 +406,7 @@
     chan, depth, wide = sorted_chunks[0].shape
     here = len(sorted_chunks)
     last = before is not None
-    per_step = 2
+    per_step = min(chan, PER_STEP)
     inputs = cores * here * LANES
     old = (here - 1) * LANES
     count = per_step * (cores + cores * cores if last else cores * cores)
@@ -426,8 +434,10 @@
 
 
 PITCH = 1
-GROUPS = [[0], [1], [2], [3]]
+PER_STEP = 4
+SORT_STEP = 2
 FIRST = False
+WAIT = True
 TIES = [4, 4, 4]
 
 
@@ -444,38 +454,33 @@
 
     planes, scale = n_time // PEERS, 1.0 / (n_time * frames)
 
-    def sent(h, after):
-        here = lax.optimization_barrier((place, after))[0] if after else place
-        pieces = pack(voltages, here, h, fine)
+    def sent(pieces, after):
+        if after:
+            pieces = lax.optimization_barrier((pieces, after))[0]
         others = [lax.ppermute(pieces[k], "tm", [(t, t ^ k) for t in range(n_time)]) for k in range(1, PEERS)]
         return [pieces[0], *others]
 
-    groups = GROUPS if chunks == 4 else [[h] for h in range(chunks)]
-    moved = [sent(0, [])]
-    packed = moved[0][0]
-    received, ordered = [], [None] * chunks
-    for g, group in enumerate(groups):
-        mine = None
-        for part, h in enumerate(group):
-            if g >= 2 and not part:
-                moved[h][0], received[g - 2] = lax.optimization_barrier((moved[h][0], received[g - 2]))
-            if h == 0:
-                moved.append(sent(1, [packed, moved[0][1]] if FIRST else [packed]))
-            mine = spectra(moved[h], place, taps, tables, frames, dests, chan, part, len(group), mine)
-            if h == 0 and len(groups[1]) > 1:
-                moved.append(sent(2, [moved[1][1]]))
-            elif h + 2 < chunks and len(moved) < h + 3:
-                moved.append(sent(h + 2, [mine]))
-        h += 1
-        if h < chunks:
-            k = TIES[g]
-            mine, moved[h][1:k] = lax.optimization_barrier((mine, moved[h][1:k]))
+    packed = [pack(voltages, place, 0, fine)]
+    later = lax.optimization_barrier((place, packed[0]))[0]
+    packed += [pack(voltages, later, h, fine) for h in range(1, chunks)]
+    moved = [sent(packed[0], [])]
+    moved.append(sent(packed[1], [moved[0][1]] if FIRST else []))
+    received = []
+    for h in range(chunks):
+        if h >= 2:
+            moved[h][0], received[h - 2] = lax.optimization_barrier((moved[h][0], received[h - 2]))
+        if h == 0:
+            moved[0][0], packed = lax.optimization_barrier((moved[0][0], packed))
+        mine = spectra(moved[h], place, taps, tables, frames, dests, chan)
+        if h + 2 < chunks:
+            moved.append(sent(packed[h + 2], [mine] if WAIT else []))
+        if h + 1 < chunks:
+            k = TIES[h]
+            mine, moved[h + 1][1:k] = lax.optimization_barrier((mine, moved[h + 1][1:k]))
         if received:
             mine, received[-1] = lax.optimization_barrier((mine, received[-1]))
         received.append(lax.all_to_all(mine, ("tm", "inp"), split_axis=0, concat_axis=0, tiled=True))
-    for array, group in zip(received, groups):
-        for part, h in enumerate(group):
-            ordered[h] = sort(array, part, planes, n_group, own, past, chan)
+    ordered = [sort(array, 0, planes, n_group, own, past, chan) for array in received]
     first = gram(ordered[:-1], chunks, n_group, scale)
     return gram(ordered, chunks, n_group, scale, first)
 

time: 273 us -> 265 us (0.971)
  local copies, waits for them, and re-layouts: 19.8 us -> 13.7 us
    unnamed x40 -> x34, local copies, waits for them, and re-layouts: 18.8 us -> 12.8 us
    pallas_call x2, Pallas kernels: 24.2 us -> 18.6 us  [gram(): pl.pallas_call(functools.partial(gram_kernel, (here, chunks, cores, scale...]
    pallas_call x4, Pallas kernels: 9.17 us -> 12.4 us  [pack(): pl.pallas_call(functools.partial(pack_kernel, chunk), in_specs=[pl.BlockS...]
  transfers between devices with their start and end apart: 16 -> 16, of which waited for: 11 -> 8; matrix products, arithmetic and copies ran while one was open for 0% -> 0% of each run, Pallas kernels for 28% -> 29%
where the time goes in v3:
time: 265 us; the launch traced here: 264 us
  waiting for transfers between devices  124 us (47%)
  Pallas kernels  90.2 us (34%)
  starting transfers between devices  36.3 us (14%)
  local copies, waits for them, and re-layouts  13.7 us (5%)
    ppermute x12, waiting for transfers between devices, sent(): lax.ppermute(pieces[k], 'tm', [(t, t ^ k) for t in range(n_time)])  70.6 us
    all_to_all x4, waiting for transfers between devices, per_device(): lax.all_to_all(mine, ('tm', 'inp'), split_axis=0, concat_axis=0, tiled=True)  53.2 us
    pallas_call x4, Pallas kernels, spectra(): pl.pallas_call(functools.partial(spectra_kernel, dims), grid_spec=pltpu.P...  47.8 us
    pallas_call x2, Pallas kernels, gram(): pl.pallas_call(functools.partial(gram_kernel, (here, chunks, cores, scale...  18.6 us
    all_to_all x4, starting transfers between devices, per_device(): lax.all_to_all(mine, ('tm', 'inp'), split_axis=0, concat_axis=0, tiled=True)  18.2 us
    ppermute x12, starting transfers between devices, sent(): lax.ppermute(pieces[k], 'tm', [(t, t ^ k) for t in range(n_time)])  18.1 us
    unnamed x34, local copies, waits for them, and re-layouts  12.8 us
    pallas_call x4, Pallas kernels, pack(): pl.pallas_call(functools.partial(pack_kernel, chunk), in_specs=[pl.BlockS...  12.4 us
  transfers between devices with their start and end apart: 16, of which 8 were waited for; matrix products, arithmetic and copies ran while one was open for 0% of the time, Pallas kernels for 29%

profile of v3, /device:TPU:0, one launch (start us, length us, event | category | flops | bytes accessed | tf_op | source)
XLA Modules:
  0.0 264.3 jit_solution(7452157513873087549)
XLA Ops:
  3.7 2.9 %collective-permute-start = (bf16[2048,128]{1,0:T(8,128)(2,1)S(1)}, bf16[2048,128]{1,0:T(8,128)(2,1)S(1)}, u32[]{:S(2)}, u32[]{:S(2)}) collective-permute-start(bf16[2048,128]{1,0:T(8,128)(2,1)S(1)} %get-tuple-element.62), channel_id=1, source_target_pairs={{0,2},{2,0},{4,6},{6,4},{8,10},{10,8},{12,14},{14,12},{16,18},{18,... | collective-permute-start | bytes 1572872 | tf_op jit(solution)/shard_map/ppermute | solution.py:460
  8.1 3.9 %pack.5 = (bf16[2048,128]{1,0:T(8,128)(2,1)S(1)}, bf16[2048,128]{1,0:T(8,128)(2,1)}, bf16[2048,128]{1,0:T(8,128)(2,1)}, bf16[2048,128]{1,0:T(8,128)(2,1)S(1)}) custom-call(s32[1]{0:T(128)} %bitcast.place, bf16[2,4,2,512,512]{4,3,2,1,0:T(8,128)(2,1)} %bitcast.26), custom_call_target="tpu_custom_call" | custom-call | tf_op jit(solution)/shard_map/pack/pallas_call | solution.py:84
  16.3 3.0 %collective-permute-done = bf16[2048,128]{1,0:T(8,128)(2,1)S(1)} collective-permute-done((bf16[2048,128]{1,0:T(8,128)(2,1)S(1)}, bf16[2048,128]{1,0:T(8,128)(2,1)S(1)}, u32[]{:S(2)}, u32[]{:S(2)}) %collective-permute-start) | collective-permute-done | bytes 524320 | tf_op jit(solution)/shard_map/ppermute | solution.py:460
  19.3 3.0 %collective-permute-start.5 = (bf16[2048,128]{1,0:T(8,128)(2,1)S(1)}, bf16[2048,128]{1,0:T(8,128)(2,1)}, u32[]{:S(2)}, u32[]{:S(2)}) collective-permute-start(bf16[2048,128]{1,0:T(8,128)(2,1)S(1)} %get-tuple-element.69), channel_id=1, source_target_pairs={{0,6},{2,4},{4,2},{6,0},{8,14},{10,12},{12,10},{14,8},{16,22},{18,... | collective-permute-start | bytes 1572872 | tf_op jit(solution)/shard_map/ppermute | solution.py:460
  33.1 12.0 %spectra.4 = bf16[32,224,128]{2,1,0:T(8,128)(2,1)} custom-call(s32[1]{0:T(128)} %bitcast.place, bf16[4,2,256,128]{3,2,1,0:T(8,128)(2,1)} %bitcast.24, bf16[4,2,256,128]{3,2,1,0:T(8,128)(2,1)} %bitcast.29, bf16[4,2,256,128]{3,2,1,0:T(8,128)(2,1)} %bitcast.4.refs_2_, bf16[4,2,256,128]{3,2,1,0:T(8,128)(2,1)} %bitcast.5.refs_3_, f32[2,256,24]{2,1,0:T(8,128)} %copy.8.refs_4_, ...), custom_call_target="tpu_custom_call" | custom-call | tf_op jit(solution)/shard_map/spectra/pallas_call | solution.py:216
  45.0 8.7 %collective-permute-done.4 = bf16[2048,128]{1,0:T(8,128)(2,1)} collective-permute-done((bf16[2048,128]{1,0:T(8,128)(2,1)}, bf16[2048,128]{1,0:T(8,128)(2,1)}, u32[]{:S(2)}, u32[]{:S(2)}) %collective-permute-start.4) | collective-permute-done | bytes 524320 | tf_op jit(solution)/shard_map/ppermute | solution.py:460
  53.8 4.9 %all-to-all-start = ((bf16[32,224,128]{2,1,0:T(8,128)(2,1)}), bf16[32,224,128]{2,1,0:T(8,128)(2,1)S(1)}, u32[]{:S(2)}, u32[]{:S(2)}) async-start(bf16[32,224,128]{2,1,0:T(8,128)(2,1)} %spectra.4), calls=%async_computation | async-start | bytes 3670016 | tf_op jit(solution)/shard_map/all_to_all | solution.py:482
  62.3 11.9 %spectra.5 = bf16[32,224,128]{2,1,0:T(8,128)(2,1)} custom-call(s32[1]{0:T(128)} %bitcast.place, bf16[4,2,256,128]{3,2,1,0:T(8,128)(2,1)} %bitcast.23, bf16[4,2,256,128]{3,2,1,0:T(8,128)(2,1)} %bitcast.9.refs_1_, bf16[4,2,256,128]{3,2,1,0:T(8,128)(2,1)} %bitcast.10.refs_2_, bf16[4,2,256,128]{3,2,1,0:T(8,128)(2,1)} %bitcast.11.refs_3_, ...), custom_call_target="tpu_custom_call" | custom-call | tf_op jit(solution)/shard_map/spectra/pallas_call | solution.py:216
  74.2 16.3 %collective-permute-done.6 = bf16[2048,128]{1,0:T(8,128)(2,1)S(1)} collective-permute-done((bf16[2048,128]{1,0:T(8,128)(2,1)}, bf16[2048,128]{1,0:T(8,128)(2,1)S(1)}, u32[]{:S(2)}, u32[]{:S(2)}) %collective-permute-start.6) | collective-permute-done | bytes 524320 | tf_op jit(solution)/shard_map/ppermute | solution.py:460
  92.1 13.3 %collective-permute-done.8 = bf16[2048,128]{1,0:T(8,128)(2,1)} collective-permute-done((bf16[2048,128]{1,0:T(8,128)(2,1)}, bf16[2048,128]{1,0:T(8,128)(2,1)}, u32[]{:S(2)}, u32[]{:S(2)}) %collective-permute-start.8) | collective-permute-done | bytes 524320 | tf_op jit(solution)/shard_map/ppermute | solution.py:460
  105.4 4.6 %all-to-all-start.1 = ((bf16[32,224,128]{2,1,0:T(8,128)(2,1)}), bf16[32,224,128]{2,1,0:T(8,128)(2,1)}, u32[]{:S(2)}, u32[]{:S(2)}) async-start(bf16[32,224,128]{2,1,0:T(8,128)(2,1)} %spectra.5), calls=%async_computation.1 | async-start | bytes 3670016 | tf_op jit(solution)/shard_map/all_to_all | solution.py:482
  113.6 11.9 %spectra.6 = bf16[32,224,128]{2,1,0:T(8,128)(2,1)} custom-call(s32[1]{0:T(128)} %bitcast.place, bf16[4,2,256,128]{3,2,1,0:T(8,128)(2,1)} %bitcast.22, bf16[4,2,256,128]{3,2,1,0:T(8,128)(2,1)} %bitcast.30, bf16[4,2,256,128]{3,2,1,0:T(8,128)(2,1)} %bitcast.31, bf16[4,2,256,128]{3,2,1,0:T(8,128)(2,1)} %bitcast.15.refs_3_, f32[2,256,24]{2,1,0:T(8,128)} %copy.8.refs_4_, ...), custom_call_target="tpu_custom_call" | custom-call | tf_op jit(solution)/shard_map/spectra/pallas_call | solution.py:216
  125.5 16.0 %collective-permute-done.9 = bf16[2048,128]{1,0:T(8,128)(2,1)S(1)} collective-permute-done((bf16[2048,128]{1,0:T(8,128)(2,1)S(1)}, bf16[2048,128]{1,0:T(8,128)(2,1)S(1)}, u32[]{:S(2)}, u32[]{:S(2)}) %collective-permute-start.9) | collective-permute-done | bytes 524320 | tf_op jit(solution)/shard_map/ppermute | solution.py:460
  143.1 13.3 %collective-permute-done.11 = bf16[2048,128]{1,0:T(8,128)(2,1)} collective-permute-done((bf16[2048,128]{1,0:T(8,128)(2,1)S(1)}, bf16[2048,128]{1,0:T(8,128)(2,1)}, u32[]{:S(2)}, u32[]{:S(2)}) %collective-permute-start.11) | collective-permute-done | bytes 524320 | tf_op jit(solution)/shard_map/ppermute | solution.py:460
  156.4 4.5 %all-to-all-start.2 = ((bf16[32,224,128]{2,1,0:T(8,128)(2,1)}), bf16[32,224,128]{2,1,0:T(8,128)(2,1)}, u32[]{:S(2)}, u32[]{:S(2)}) async-start(bf16[32,224,128]{2,1,0:T(8,128)(2,1)} %spectra.6), calls=%async_computation.2 | async-start | bytes 3670016 | tf_op jit(solution)/shard_map/all_to_all | solution.py:482
  160.9 12.0 %spectra.7 = bf16[32,224,128]{2,1,0:T(8,128)(2,1)} custom-call(s32[1]{0:T(128)} %bitcast.place, bf16[4,2,256,128]{3,2,1,0:T(8,128)(2,1)} %bitcast.21, bf16[4,2,256,128]{3,2,1,0:T(8,128)(2,1)} %bitcast.32, bf16[4,2,256,128]{3,2,1,0:T(8,128)(2,1)} %bitcast.33, bf16[4,2,256,128]{3,2,1,0:T(8,128)(2,1)} %bitcast.19.refs_3_, f32[2,256,24]{2,1,0:T(8,128)} %copy.8.refs_4_, ...), custom_call_target="tpu_custom_call" | custom-call | tf_op jit(solution)/shard_map/spectra/pallas_call | solution.py:216
  172.9 31.2 %all-to-all-done.2.source = bf16[32,224,128]{2,1,0:T(8,128)(2,1)} async-done(((bf16[32,224,128]{2,1,0:T(8,128)(2,1)}), bf16[32,224,128]{2,1,0:T(8,128)(2,1)}, u32[]{:S(2)}, u32[]{:S(2)}) %all-to-all-start.2) | async-done | bytes 1835040 | tf_op jit(solution)/shard_map/all_to_all | solution.py:482
  204.1 4.1 %all-to-all-start.3 = ((bf16[32,224,128]{2,1,0:T(8,128)(2,1)}), bf16[32,224,128]{2,1,0:T(8,128)(2,1)}, u32[]{:S(2)}, u32[]{:S(2)}) async-start(bf16[32,224,128]{2,1,0:T(8,128)(2,1)} %spectra.7), calls=%async_computation.3 | async-start | bytes 3670016 | tf_op jit(solution)/shard_map/all_to_all | solution.py:482
  211.1 3.2 %sort.5.refs_1_ = bf16[16,128,256]{2,1,0:T(8,128)(2,1)S(1)} custom-call(bf16[32,224,128]{2,1,0:T(8,128)(2,1)} %all-to-all-done.1.source), custom_call_target="tpu_custom_call" | custom-call | tf_op jit(solution)/shard_map/sort/pallas_call | solution.py:280
  215.3 3.2 %sort.6.refs_2_ = bf16[16,128,256]{2,1,0:T(8,128)(2,1)S(1)} custom-call(bf16[32,224,128]{2,1,0:T(8,128)(2,1)} %all-to-all-done.2.source), custom_call_target="tpu_custom_call" | custom-call | tf_op jit(solution)/shard_map/sort/pallas_call | solution.py:280
  219.5 10.0 %gram_first.1.refs_4_ = bf16[16,1024,1024]{2,1,0:T(8,128)(2,1)} custom-call(bf16[16,128,256]{2,1,0:T(8,128)(2,1)} %copy-done, bf16[16,128,256]{2,1,0:T(8,128)(2,1)} %copy-done.1, bf16[16,128,256]{2,1,0:T(8,128)(2,1)} %copy-done.2), custom_call_target="tpu_custom_call" | custom-call | tf_op jit(solution)/shard_map/gram_first/pallas_call | solution.py:416
  229.5 21.9 %all-to-all-done.3.source = bf16[32,224,128]{2,1,0:T(8,128)(2,1)} async-done(((bf16[32,224,128]{2,1,0:T(8,128)(2,1)}), bf16[32,224,128]{2,1,0:T(8,128)(2,1)}, u32[]{:S(2)}, u32[]{:S(2)}) %all-to-all-start.3) | async-done | bytes 1835040 | tf_op jit(solution)/shard_map/all_to_all | solution.py:482
  251.4 3.2 %sort.7.refs_3_ = bf16[16,128,256]{2,1,0:T(8,128)(2,1)S(1)} custom-call(bf16[32,224,128]{2,1,0:T(8,128)(2,1)} %all-to-all-done.3.source), custom_call_target="tpu_custom_call" | custom-call | tf_op jit(solution)/shard_map/sort/pallas_call | solution.py:280
  255.6 8.5 %gram_last.1 = bf16[16,1024,1024]{2,1,0:T(8,128)(2,1)} custom-call(bf16[16,128,256]{2,1,0:T(8,128)(2,1)} %copy-done, bf16[16,128,256]{2,1,0:T(8,128)(2,1)} %copy-done.1, bf16[16,128,256]{2,1,0:T(8,128)(2,1)} %copy-done.2, bf16[16,128,256]{2,1,0:T(8,128)(2,1)} %copy-done.3, bf16[16,1024,1024]{2,1,0:T(8,128)(2,1)} %gram_first.1.refs_4_), custom_call_target="tpu_custom_call", output_to_operand_aliasing={{}: (4, {})} | custom-call | tf_op jit(solution)/shard_map/gram_last/pallas_call | solution.py:416
  (60 shorter events, 36.1 us)
Async XLA Ops:
  3.7 15.7 %collective-permute-start = (bf16[2048,128]{1,0:T(8,128)(2,1)S(1)}, bf16[2048,128]{1,0:T(8,128)(2,1)S(1)}, u32[]{:S(2)}, u32[]{:S(2)}) collective-permute-start(bf16[2048,128]{1,0:T(8,128)(2,1)S(1)} %get-tuple-element.62), channel_id=1, source_target_pairs={{0,2},{2,0},{4,6},{6,4},{8,10},{10,8},{12,14},{14,12},{16,18},{18,... | collective-permute-start | bytes 1572872 | tf_op jit(solution)/shard_map/ppermute | solution.py:460
  6.6 26.5 %collective-permute-start.1 = (bf16[2048,128]{1,0:T(8,128)(2,1)S(1)}, bf16[2048,128]{1,0:T(8,128)(2,1)}, u32[]{:S(2)}, u32[]{:S(2)}) collective-permute-start(bf16[2048,128]{1,0:T(8,128)(2,1)S(1)} %get-tuple-element.63), channel_id=1, source_target_pairs={{0,4},{2,6},{4,0},{6,2},{8,12},{10,14},{12,8},{14,10},{16,20},{18,... | collective-permute-start | bytes 1572872 | tf_op jit(solution)/shard_map/ppermute | solution.py:460
  8.1 25.0 %collective-permute-start.2 = (bf16[2048,128]{1,0:T(8,128)(2,1)S(1)}, bf16[2048,128]{1,0:T(8,128)(2,1)}, u32[]{:S(2)}, u32[]{:S(2)}) collective-permute-start(bf16[2048,128]{1,0:T(8,128)(2,1)S(1)} %get-tuple-element.64), channel_id=1, source_target_pairs={{0,6},{2,4},{4,2},{6,0},{8,14},{10,12},{12,10},{14,8},{16,22},{18,... | collective-permute-start | bytes 1572872 | tf_op jit(solution)/shard_map/ppermute | solution.py:460
  12.0 0.8 copy-start.6
  12.8 32.2 %collective-permute-start.3 = (bf16[2048,128]{1,0:T(8,128)(2,1)}, bf16[2048,128]{1,0:T(8,128)(2,1)}, u32[]{:S(2)}, u32[]{:S(2)}) collective-permute-start(bf16[2048,128]{1,0:T(8,128)(2,1)} %get-tuple-element.67), channel_id=1, source_target_pairs={{0,2},{2,0},{4,6},{6,4},{8,10},{10,8},{12,14},{14,12},{16,18},{18,... | collective-permute-start | bytes 1572872 | tf_op jit(solution)/shard_map/ppermute | solution.py:460
  14.8 39.0 %collective-permute-start.4 = (bf16[2048,128]{1,0:T(8,128)(2,1)}, bf16[2048,128]{1,0:T(8,128)(2,1)}, u32[]{:S(2)}, u32[]{:S(2)}) collective-permute-start(bf16[2048,128]{1,0:T(8,128)(2,1)} %get-tuple-element.68), channel_id=1, source_target_pairs={{0,4},{2,6},{4,0},{6,2},{8,12},{10,14},{12,8},{14,10},{16,20},{18,... | collective-permute-start | bytes 1572872 | tf_op jit(solution)/shard_map/ppermute | solution.py:460
  19.3 3.0 %copy-start.11 = (bf16[2048,128]{1,0:T(8,128)(2,1)}, bf16[2048,128]{1,0:T(8,128)(2,1)S(1)}, u32[]{:S(2)}) copy-start(bf16[2048,128]{1,0:T(8,128)(2,1)S(1)} %collective-permute-done) | copy-start | bytes 1572868
  19.3 34.4 %collective-permute-start.5 = (bf16[2048,128]{1,0:T(8,128)(2,1)S(1)}, bf16[2048,128]{1,0:T(8,128)(2,1)}, u32[]{:S(2)}, u32[]{:S(2)}) collective-permute-start(bf16[2048,128]{1,0:T(8,128)(2,1)S(1)} %get-tuple-element.69), channel_id=1, source_target_pairs={{0,6},{2,4},{4,2},{6,0},{8,14},{10,12},{12,10},{14,8},{16,22},{18,... | collective-permute-start | bytes 1572872 | tf_op jit(solution)/shard_map/ppermute | solution.py:460
  26.0 6.1 %copy-start.16 = (s32[12,1024]{1,0:T(8,128)S(1)}, s32[12,1024]{1,0:T(8,128)}, u32[]{:S(2)}) copy-start(s32[12,1024]{1,0:T(8,128)} %param.5) | copy-start | bytes 147460
  53.8 51.6 %all-to-all-start = ((bf16[32,224,128]{2,1,0:T(8,128)(2,1)}), bf16[32,224,128]{2,1,0:T(8,128)(2,1)S(1)}, u32[]{:S(2)}, u32[]{:S(2)}) async-start(bf16[32,224,128]{2,1,0:T(8,128)(2,1)} %spectra.4), calls=%async_computation | async-start | bytes 3670016 | tf_op jit(solution)/shard_map/all_to_all | solution.py:482
  58.7 31.8 %collective-permute-start.6 = (bf16[2048,128]{1,0:T(8,128)(2,1)}, bf16[2048,128]{1,0:T(8,128)(2,1)S(1)}, u32[]{:S(2)}, u32[]{:S(2)}) collective-permute-start(bf16[2048,128]{1,0:T(8,128)(2,1)} %copy-done.10), channel_id=1, source_target_pairs={{0,2},{2,0},{4,6},{6,4},{8,10},{10,8},{12,14},{14,12},{16,18},{18,... | collective-permute-start | bytes 1572872 | tf_op jit(solution)/shard_map/ppermute | solution.py:460
  60.6 29.9 %collective-permute-start.7 = (bf16[2048,128]{1,0:T(8,128)(2,1)}, bf16[2048,128]{1,0:T(8,128)(2,1)S(1)}, u32[]{:S(2)}, u32[]{:S(2)}) collective-permute-start(bf16[2048,128]{1,0:T(8,128)(2,1)} %copy-done.9), channel_id=1, source_target_pairs={{0,4},{2,6},{4,0},{6,2},{8,12},{10,14},{12,8},{14,10},{16,20},{18,... | collective-permute-start | bytes 1572872 | tf_op jit(solution)/shard_map/ppermute | solution.py:460
  62.0 43.4 %collective-permute-start.8 = (bf16[2048,128]{1,0:T(8,128)(2,1)}, bf16[2048,128]{1,0:T(8,128)(2,1)}, u32[]{:S(2)}, u32[]{:S(2)}) collective-permute-start(bf16[2048,128]{1,0:T(8,128)(2,1)} %copy-done.8), channel_id=1, source_target_pairs={{0,6},{2,4},{4,2},{6,0},{8,14},{10,12},{12,10},{14,8},{16,22},{18,... | collective-permute-start | bytes 1572872 | tf_op jit(solution)/shard_map/ppermute | solution.py:460
  90.5 0.8 copy-start.12
  105.4 51.0 %all-to-all-start.1 = ((bf16[32,224,128]{2,1,0:T(8,128)(2,1)}), bf16[32,224,128]{2,1,0:T(8,128)(2,1)}, u32[]{:S(2)}, u32[]{:S(2)}) async-start(bf16[32,224,128]{2,1,0:T(8,128)(2,1)} %spectra.5), calls=%async_computation.1 | async-start | bytes 3670016 | tf_op jit(solution)/shard_map/all_to_all | solution.py:482
  110.0 31.5 %collective-permute-start.9 = (bf16[2048,128]{1,0:T(8,128)(2,1)S(1)}, bf16[2048,128]{1,0:T(8,128)(2,1)S(1)}, u32[]{:S(2)}, u32[]{:S(2)}) collective-permute-start(bf16[2048,128]{1,0:T(8,128)(2,1)S(1)} %get-tuple-element.103), channel_id=1, source_target_pairs={{0,2},{2,0},{4,6},{6,4},{8,10},{10,8},{12,14},{14,12},{16,18},{18,... | collective-permute-start | bytes 1572872 | tf_op jit(solution)/shard_map/ppermute | solution.py:460
  111.6 29.9 %collective-permute-start.10 = (bf16[2048,128]{1,0:T(8,128)(2,1)S(1)}, bf16[2048,128]{1,0:T(8,128)(2,1)S(1)}, u32[]{:S(2)}, u32[]{:S(2)}) collective-permute-start(bf16[2048,128]{1,0:T(8,128)(2,1)S(1)} %get-tuple-element.104), channel_id=1, source_target_pairs={{0,4},{2,6},{4,0},{6,2},{8,12},{10,14},{12,8},{14,10},{16,20},{18,... | collective-permute-start | bytes 1572872 | tf_op jit(solution)/shard_map/ppermute | solution.py:460
  113.1 43.3 %collective-permute-start.11 = (bf16[2048,128]{1,0:T(8,128)(2,1)S(1)}, bf16[2048,128]{1,0:T(8,128)(2,1)}, u32[]{:S(2)}, u32[]{:S(2)}) collective-permute-start(bf16[2048,128]{1,0:T(8,128)(2,1)S(1)} %get-tuple-element.105), channel_id=1, source_target_pairs={{0,6},{2,4},{4,2},{6,0},{8,14},{10,12},{12,10},{14,8},{16,22},{18,... | collective-permute-start | bytes 1572872 | tf_op jit(solution)/shard_map/ppermute | solution.py:460
  156.4 47.7 %all-to-all-start.2 = ((bf16[32,224,128]{2,1,0:T(8,128)(2,1)}), bf16[32,224,128]{2,1,0:T(8,128)(2,1)}, u32[]{:S(2)}, u32[]{:S(2)}) async-start(bf16[32,224,128]{2,1,0:T(8,128)(2,1)} %spectra.6), calls=%async_computation.2 | async-start | bytes 3670016 | tf_op jit(solution)/shard_map/all_to_all | solution.py:482
  204.1 47.4 %all-to-all-start.3 = ((bf16[32,224,128]{2,1,0:T(8,128)(2,1)}), bf16[32,224,128]{2,1,0:T(8,128)(2,1)}, u32[]{:S(2)}, u32[]{:S(2)}) async-start(bf16[32,224,128]{2,1,0:T(8,128)(2,1)} %spectra.7), calls=%async_computation.3 | async-start | bytes 3670016 | tf_op jit(solution)/shard_map/all_to_all | solution.py:482
  210.0 1.1 copy-start
  214.3 1.0 copy-start.1
  218.5 1.0 copy-start.2
  254.7 1.0 copy-start.3
  (9 other events, 7.2 us)

commit v4 on v3

--- a/solution.py
+++ b/solution.py
@@ -238,13 +238,11 @@
     )(place, *blocks, weights, *tables, *([] if into is None else [into]))
 
 
-def sort_kernel(dims, source, out, tails):
+def in_order(dims, source, tails, at, per_step, store):
     planes, cores, own, past, chan = dims
     head_pairs, tail_pairs = own // 2, (past + 1) // 2
     head_rows, tail_rows = block_rows(chan, own, past)
     depth = planes * own
-    per_step = out.shape[0]
-    at = pl.program_id(0)
 
     @pl.when(at == 0)
     def _():
@@ -270,7 +268,14 @@
                 value = blocks_transposed(value)
                 for part in range(2):
                     rows = jnp.concatenate([value[part], value[2 + part]], 0).astype(jnp.bfloat16)
-                    out[e, pl.ds(part * depth + z * own, own), pl.ds(c * LANES, LANES)] = rows
+                    store(e, pl.ds(part * depth + z * own, own), c, rows)
+
+
+def sort_kernel(dims, source, out, tails):
+    def store(e, rows, c, value):
+        out[e, rows, pl.ds(c * LANES, LANES)] = value
+
+    in_order(dims, source, tails, pl.program_id(0), out.shape[0], store)
 
 
 def sort(received, part, planes, cores, own, past, chan):
@@ -290,9 +295,9 @@
 
 
 def gram_kernel(dims, *refs):
-    here, chunks, cores, scale, last = dims
-    ins = refs[:here]
-    out, stacked, turned, rows_out, cols_out, sems = refs[here + last :]
+    here, chunks, cores, scale, last = dims[:5]
+    ins = refs[: here - last]
+    out, stacked, turned, rows_out, cols_out, sems = refs[here + last : here + last + 6]
     per_step = ins[0].shape[0]
     depth = ins[0].shape[1] // 2
     width = here * LANES
@@ -333,12 +338,22 @@
         for copy in copies(at - 2):
             copy.wait()
 
+    if last:
+
+        def store(e, rows, c, value):
+            stacked[e, rows, pl.ds((c * here + here - 1) * LANES, LANES)] = value
+
+        in_order(dims[5], refs[here - 1], refs[-1], at, per_step, store)
+
     for e in range(per_step):
         for c in range(cores):
             for h in range(here):
-                block = ins[h][e, :, c * LANES : (c + 1) * LANES]
                 column = pl.ds((c * here + h) * LANES, LANES)
-                stacked[e, :, column] = block
+                if h < len(ins):
+                    block = ins[h][e, :, c * LANES : (c + 1) * LANES]
+                    stacked[e, :, column] = block
+                else:
+                    block = stacked[e, :, column]
                 turned[e, 0:depth, column] = -block[depth:]
                 turned[e, depth:, column] = block[:depth]
 
@@ -402,10 +417,10 @@
             copy.wait()
 
 
-def gram(sorted_chunks, chunks, cores, scale, before=None):
+def gram(sorted_chunks, chunks, cores, scale, before=None, fresh=None, order=None):
     chan, depth, wide = sorted_chunks[0].shape
-    here = len(sorted_chunks)
     last = before is not None
+    here = len(sorted_chunks) + last
     per_step = min(chan, PER_STEP)
     inputs = cores * here * LANES
     old = (here - 1) * LANES
@@ -414,9 +429,10 @@
     cols_shape = (2, per_step, cores * old, cores * LANES) if last else (16, LANES)
     total = cores * chunks * LANES
     return pl.pallas_call(
-        functools.partial(gram_kernel, (here, chunks, cores, scale, last)),
+        functools.partial(gram_kernel, (here, chunks, cores, scale, last, order)),
         grid=(chan // per_step,),
-        in_specs=[pl.BlockSpec((per_step, depth, wide), lambda i: (i, 0, 0))] * here
+        in_specs=[pl.BlockSpec((per_step, depth, wide), lambda i: (i, 0, 0))] * (here - last)
+        + ([pl.BlockSpec(fresh.shape, lambda i: (0, 0, 0))] if last else [])
         + [pl.BlockSpec(memory_space=pl.ANY)] * last,
         out_specs=pl.BlockSpec(memory_space=pl.ANY),
         scratch_shapes=[
@@ -425,12 +441,13 @@
             pltpu.VMEM(rows_shape, jnp.bfloat16),
             pltpu.VMEM(cols_shape, jnp.bfloat16),
             pltpu.SemaphoreType.DMA((2, count)),
-        ],
+        ]
+        + ([pltpu.VMEM((fresh.shape[0], block_rows(chan, *order[2:4])[1] + 8, LANES), jnp.float32)] if last else []),
         out_shape=jax.ShapeDtypeStruct((chan, total, total), jnp.bfloat16),
         input_output_aliases={here: 0} if last else {},
         compiler_params=pltpu.CompilerParams(vmem_limit_bytes=56 * MIB),
         name="gram_last" if last else "gram_first",
-    )(*sorted_chunks, *([before] if last else []))
+    )(*sorted_chunks, *([fresh, before] if last else []))
 
 
 PITCH = 1
@@ -480,9 +497,9 @@
         if received:
             mine, received[-1] = lax.optimization_barrier((mine, received[-1]))
         received.append(lax.all_to_all(mine, ("tm", "inp"), split_axis=0, concat_axis=0, tiled=True))
-    ordered = [sort(array, 0, planes, n_group, own, past, chan) for array in received]
-    first = gram(ordered[:-1], chunks, n_group, scale)
-    return gram(ordered, chunks, n_group, scale, first)
+    ordered = [sort(array, 0, planes, n_group, own, past, chan) for array in received[:-1]]
+    first = gram(ordered, chunks, n_group, scale)
+    return gram(ordered, chunks, n_group, scale, first, received[-1], (planes, n_group, own, past, chan))
 
 
 def solution(mesh):

time: 265 us -> 262 us (0.989)
    pallas_call x4 -> x3, Pallas kernels: 11.4 us -> 8.18 us  [sort(): pl.pallas_call(functools.partial(sort_kernel, (planes, cores, own, past,...]
    unnamed x34 -> x32, local copies, waits for them, and re-layouts: 12.8 us -> 11.7 us
where the time goes in v4:
time: 262 us; the launch traced here: 261 us
  waiting for transfers between devices  124 us (47%)
  Pallas kernels  88.2 us (34%)
  starting transfers between devices  36.3 us (14%)
  local copies, waits for them, and re-layouts  12.6 us (5%)
    ppermute x12, waiting for transfers between devices, sent(): lax.ppermute(pieces[k], 'tm', [(t, t ^ k) for t in range(n_time)])  70.7 us
    all_to_all x4, waiting for transfers between devices, per_device(): lax.all_to_all(mine, ('tm', 'inp'), split_axis=0, concat_axis=0, tiled=True)  53.2 us
    pallas_call x4, Pallas kernels, spectra(): pl.pallas_call(functools.partial(spectra_kernel, dims), grid_spec=pltpu.P...  47.8 us
    pallas_call x2, Pallas kernels, gram(): pl.pallas_call(functools.partial(gram_kernel, (here, chunks, cores, scale...  19.8 us
    all_to_all x4, starting transfers between devices, per_device(): lax.all_to_all(mine, ('tm', 'inp'), split_axis=0, concat_axis=0, tiled=True)  18.2 us
    ppermute x12, starting transfers between devices, sent(): lax.ppermute(pieces[k], 'tm', [(t, t ^ k) for t in range(n_time)])  18.1 us
    pallas_call x4, Pallas kernels, pack(): pl.pallas_call(functools.partial(pack_kernel, chunk), in_specs=[pl.BlockS...  12.4 us
    unnamed x32, local copies, waits for them, and re-layouts  11.7 us
  transfers between devices with their start and end apart: 16, of which 8 were waited for; matrix products, arithmetic and copies ran while one was open for 0% of the time, Pallas kernels for 29%

profile of v4, /device:TPU:0, one launch (start us, length us, event | category | flops | bytes accessed | tf_op | source)
XLA Modules:
  0.0 261.4 jit_solution(291490071624546410)
XLA Ops:
  3.6 2.9 %collective-permute-start = (bf16[2048,128]{1,0:T(8,128)(2,1)S(1)}, bf16[2048,128]{1,0:T(8,128)(2,1)S(1)}, u32[]{:S(2)}, u32[]{:S(2)}) collective-permute-start(bf16[2048,128]{1,0:T(8,128)(2,1)S(1)} %get-tuple-element.62), channel_id=1, source_target_pairs={{0,2},{2,0},{4,6},{6,4},{8,10},{10,8},{12,14},{14,12},{16,18},{18,... | collective-permute-start | bytes 1572872 | tf_op jit(solution)/shard_map/ppermute | solution.py:477
  8.1 3.9 %pack.5 = (bf16[2048,128]{1,0:T(8,128)(2,1)S(1)}, bf16[2048,128]{1,0:T(8,128)(2,1)}, bf16[2048,128]{1,0:T(8,128)(2,1)}, bf16[2048,128]{1,0:T(8,128)(2,1)S(1)}) custom-call(s32[1]{0:T(128)} %bitcast.place, bf16[2,4,2,512,512]{4,3,2,1,0:T(8,128)(2,1)} %bitcast.26), custom_call_target="tpu_custom_call" | custom-call | tf_op jit(solution)/shard_map/pack/pallas_call | solution.py:84
  16.3 3.1 %collective-permute-done = bf16[2048,128]{1,0:T(8,128)(2,1)S(1)} collective-permute-done((bf16[2048,128]{1,0:T(8,128)(2,1)S(1)}, bf16[2048,128]{1,0:T(8,128)(2,1)S(1)}, u32[]{:S(2)}, u32[]{:S(2)}) %collective-permute-start) | collective-permute-done | bytes 524320 | tf_op jit(solution)/shard_map/ppermute | solution.py:477
  19.3 3.0 %collective-permute-start.5 = (bf16[2048,128]{1,0:T(8,128)(2,1)S(1)}, bf16[2048,128]{1,0:T(8,128)(2,1)}, u32[]{:S(2)}, u32[]{:S(2)}) collective-permute-start(bf16[2048,128]{1,0:T(8,128)(2,1)S(1)} %get-tuple-element.69), channel_id=1, source_target_pairs={{0,6},{2,4},{4,2},{6,0},{8,14},{10,12},{12,10},{14,8},{16,22},{18,... | collective-permute-start | bytes 1572872 | tf_op jit(solution)/shard_map/ppermute | solution.py:477
  26.0 2.9 %pack.6 = (bf16[2048,128]{1,0:T(8,128)(2,1)S(1)}, bf16[2048,128]{1,0:T(8,128)(2,1)S(1)}, bf16[2048,128]{1,0:T(8,128)(2,1)S(1)}, bf16[2048,128]{1,0:T(8,128)(2,1)S(1)}) custom-call(s32[1]{0:T(128)} %bitcast.place, bf16[2,4,2,512,512]{4,3,2,1,0:T(8,128)(2,1)} %bitcast.28), custom_call_target="tpu_custom_call" | custom-call | tf_op jit(solution)/shard_map/pack/pallas_call | solution.py:84
  33.0 12.0 %spectra.4 = bf16[32,224,128]{2,1,0:T(8,128)(2,1)} custom-call(s32[1]{0:T(128)} %bitcast.place, bf16[4,2,256,128]{3,2,1,0:T(8,128)(2,1)} %bitcast.24, bf16[4,2,256,128]{3,2,1,0:T(8,128)(2,1)} %bitcast.29, bf16[4,2,256,128]{3,2,1,0:T(8,128)(2,1)} %bitcast.4.refs_2_, bf16[4,2,256,128]{3,2,1,0:T(8,128)(2,1)} %bitcast.5.refs_3_, f32[2,256,24]{2,1,0:T(8,128)} %copy.8.refs_4_, ...), custom_call_target="tpu_custom_call" | custom-call | tf_op jit(solution)/shard_map/spectra/pallas_call | solution.py:216
  45.0 8.8 %collective-permute-done.4 = bf16[2048,128]{1,0:T(8,128)(2,1)} collective-permute-done((bf16[2048,128]{1,0:T(8,128)(2,1)}, bf16[2048,128]{1,0:T(8,128)(2,1)}, u32[]{:S(2)}, u32[]{:S(2)}) %collective-permute-start.4) | collective-permute-done | bytes 524320 | tf_op jit(solution)/shard_map/ppermute | solution.py:477
  53.8 4.9 %all-to-all-start = ((bf16[32,224,128]{2,1,0:T(8,128)(2,1)}), bf16[32,224,128]{2,1,0:T(8,128)(2,1)S(1)}, u32[]{:S(2)}, u32[]{:S(2)}) async-start(bf16[32,224,128]{2,1,0:T(8,128)(2,1)} %spectra.4), calls=%async_computation | async-start | bytes 3670016 | tf_op jit(solution)/shard_map/all_to_all | solution.py:499
  62.3 11.9 %spectra.5 = bf16[32,224,128]{2,1,0:T(8,128)(2,1)} custom-call(s32[1]{0:T(128)} %bitcast.place, bf16[4,2,256,128]{3,2,1,0:T(8,128)(2,1)} %bitcast.23, bf16[4,2,256,128]{3,2,1,0:T(8,128)(2,1)} %bitcast.9.refs_1_, bf16[4,2,256,128]{3,2,1,0:T(8,128)(2,1)} %bitcast.10.refs_2_, bf16[4,2,256,128]{3,2,1,0:T(8,128)(2,1)} %bitcast.11.refs_3_, ...), custom_call_target="tpu_custom_call" | custom-call | tf_op jit(solution)/shard_map/spectra/pallas_call | solution.py:216
  74.2 16.3 %collective-permute-done.6 = bf16[2048,128]{1,0:T(8,128)(2,1)S(1)} collective-permute-done((bf16[2048,128]{1,0:T(8,128)(2,1)}, bf16[2048,128]{1,0:T(8,128)(2,1)S(1)}, u32[]{:S(2)}, u32[]{:S(2)}) %collective-permute-start.6) | collective-permute-done | bytes 524320 | tf_op jit(solution)/shard_map/ppermute | solution.py:477
  92.1 13.3 %collective-permute-done.8 = bf16[2048,128]{1,0:T(8,128)(2,1)} collective-permute-done((bf16[2048,128]{1,0:T(8,128)(2,1)}, bf16[2048,128]{1,0:T(8,128)(2,1)}, u32[]{:S(2)}, u32[]{:S(2)}) %collective-permute-start.8) | collective-permute-done | bytes 524320 | tf_op jit(solution)/shard_map/ppermute | solution.py:477
  105.4 4.6 %all-to-all-start.1 = ((bf16[32,224,128]{2,1,0:T(8,128)(2,1)}), bf16[32,224,128]{2,1,0:T(8,128)(2,1)}, u32[]{:S(2)}, u32[]{:S(2)}) async-start(bf16[32,224,128]{2,1,0:T(8,128)(2,1)} %spectra.5), calls=%async_computation.1 | async-start | bytes 3670016 | tf_op jit(solution)/shard_map/all_to_all | solution.py:499
  113.6 11.9 %spectra.6 = bf16[32,224,128]{2,1,0:T(8,128)(2,1)} custom-call(s32[1]{0:T(128)} %bitcast.place, bf16[4,2,256,128]{3,2,1,0:T(8,128)(2,1)} %bitcast.22, bf16[4,2,256,128]{3,2,1,0:T(8,128)(2,1)} %bitcast.30, bf16[4,2,256,128]{3,2,1,0:T(8,128)(2,1)} %bitcast.31, bf16[4,2,256,128]{3,2,1,0:T(8,128)(2,1)} %bitcast.15.refs_3_, f32[2,256,24]{2,1,0:T(8,128)} %copy.8.refs_4_, ...), custom_call_target="tpu_custom_call" | custom-call | tf_op jit(solution)/shard_map/spectra/pallas_call | solution.py:216
  125.5 16.0 %collective-permute-done.9 = bf16[2048,128]{1,0:T(8,128)(2,1)S(1)} collective-permute-done((bf16[2048,128]{1,0:T(8,128)(2,1)S(1)}, bf16[2048,128]{1,0:T(8,128)(2,1)S(1)}, u32[]{:S(2)}, u32[]{:S(2)}) %collective-permute-start.9) | collective-permute-done | bytes 524320 | tf_op jit(solution)/shard_map/ppermute | solution.py:477
  143.1 13.3 %collective-permute-done.11 = bf16[2048,128]{1,0:T(8,128)(2,1)} collective-permute-done((bf16[2048,128]{1,0:T(8,128)(2,1)S(1)}, bf16[2048,128]{1,0:T(8,128)(2,1)}, u32[]{:S(2)}, u32[]{:S(2)}) %collective-permute-start.11) | collective-permute-done | bytes 524320 | tf_op jit(solution)/shard_map/ppermute | solution.py:477
  156.4 4.5 %all-to-all-start.2 = ((bf16[32,224,128]{2,1,0:T(8,128)(2,1)}), bf16[32,224,128]{2,1,0:T(8,128)(2,1)}, u32[]{:S(2)}, u32[]{:S(2)}) async-start(bf16[32,224,128]{2,1,0:T(8,128)(2,1)} %spectra.6), calls=%async_computation.2 | async-start | bytes 3670016 | tf_op jit(solution)/shard_map/all_to_all | solution.py:499
  160.9 12.0 %spectra.7 = bf16[32,224,128]{2,1,0:T(8,128)(2,1)} custom-call(s32[1]{0:T(128)} %bitcast.place, bf16[4,2,256,128]{3,2,1,0:T(8,128)(2,1)} %bitcast.21, bf16[4,2,256,128]{3,2,1,0:T(8,128)(2,1)} %bitcast.32, bf16[4,2,256,128]{3,2,1,0:T(8,128)(2,1)} %bitcast.33, bf16[4,2,256,128]{3,2,1,0:T(8,128)(2,1)} %bitcast.19.refs_3_, f32[2,256,24]{2,1,0:T(8,128)} %copy.8.refs_4_, ...), custom_call_target="tpu_custom_call" | custom-call | tf_op jit(solution)/shard_map/spectra/pallas_call | solution.py:216
  172.9 31.2 %all-to-all-done.2.source = bf16[32,224,128]{2,1,0:T(8,128)(2,1)} async-done(((bf16[32,224,128]{2,1,0:T(8,128)(2,1)}), bf16[32,224,128]{2,1,0:T(8,128)(2,1)}, u32[]{:S(2)}, u32[]{:S(2)}) %all-to-all-start.2) | async-done | bytes 1835040 | tf_op jit(solution)/shard_map/all_to_all | solution.py:499
  204.1 4.1 %all-to-all-start.3 = ((bf16[32,224,128]{2,1,0:T(8,128)(2,1)}), bf16[32,224,128]{2,1,0:T(8,128)(2,1)}, u32[]{:S(2)}, u32[]{:S(2)}) async-start(bf16[32,224,128]{2,1,0:T(8,128)(2,1)} %spectra.7), calls=%async_computation.3 | async-start | bytes 3670016 | tf_op jit(solution)/shard_map/all_to_all | solution.py:499
  211.1 3.2 %sort.4.refs_1_ = bf16[16,128,256]{2,1,0:T(8,128)(2,1)S(1)} custom-call(bf16[32,224,128]{2,1,0:T(8,128)(2,1)} %all-to-all-done.1.source), custom_call_target="tpu_custom_call" | custom-call | tf_op jit(solution)/shard_map/sort/pallas_call | solution.py:285
  215.3 3.2 %sort.5.refs_2_ = bf16[16,128,256]{2,1,0:T(8,128)(2,1)S(1)} custom-call(bf16[32,224,128]{2,1,0:T(8,128)(2,1)} %all-to-all-done.2.source), custom_call_target="tpu_custom_call" | custom-call | tf_op jit(solution)/shard_map/sort/pallas_call | solution.py:285
  219.5 10.0 %gram_first.1.refs_4_ = bf16[16,1024,1024]{2,1,0:T(8,128)(2,1)} custom-call(bf16[16,128,256]{2,1,0:T(8,128)(2,1)} %copy-done, bf16[16,128,256]{2,1,0:T(8,128)(2,1)} %copy-done.1, bf16[16,128,256]{2,1,0:T(8,128)(2,1)} %copy-done.2), custom_call_target="tpu_custom_call" | custom-call | tf_op jit(solution)/shard_map/gram_first/pallas_call | solution.py:431
  229.5 21.9 %all-to-all-done.3.refs_3_ = bf16[32,224,128]{2,1,0:T(8,128)(2,1)} async-done(((bf16[32,224,128]{2,1,0:T(8,128)(2,1)}), bf16[32,224,128]{2,1,0:T(8,128)(2,1)}, u32[]{:S(2)}, u32[]{:S(2)}) %all-to-all-start.3) | async-done | bytes 1835040 | tf_op jit(solution)/shard_map/all_to_all | solution.py:499
  251.4 9.8 %gram_last.1 = bf16[16,1024,1024]{2,1,0:T(8,128)(2,1)} custom-call(bf16[16,128,256]{2,1,0:T(8,128)(2,1)} %copy-done, bf16[16,128,256]{2,1,0:T(8,128)(2,1)} %copy-done.1, bf16[16,128,256]{2,1,0:T(8,128)(2,1)} %copy-done.2, bf16[32,224,128]{2,1,0:T(8,128)(2,1)} %all-to-all-done.3.refs_3_, ...), custom_call_target="tpu_custom_call", output_to_operand_aliasing={{}: (4, {})} | custom-call | tf_op jit(solution)/shard_map/gram_last/pallas_call | solution.py:431
  (57 shorter events, 32.2 us)
Async XLA Ops:
  3.6 15.7 %collective-permute-start = (bf16[2048,128]{1,0:T(8,128)(2,1)S(1)}, bf16[2048,128]{1,0:T(8,128)(2,1)S(1)}, u32[]{:S(2)}, u32[]{:S(2)}) collective-permute-start(bf16[2048,128]{1,0:T(8,128)(2,1)S(1)} %get-tuple-element.62), channel_id=1, source_target_pairs={{0,2},{2,0},{4,6},{6,4},{8,10},{10,8},{12,14},{14,12},{16,18},{18,... | collective-permute-start | bytes 1572872 | tf_op jit(solution)/shard_map/ppermute | solution.py:477
  6.6 26.5 %collective-permute-start.1 = (bf16[2048,128]{1,0:T(8,128)(2,1)S(1)}, bf16[2048,128]{1,0:T(8,128)(2,1)}, u32[]{:S(2)}, u32[]{:S(2)}) collective-permute-start(bf16[2048,128]{1,0:T(8,128)(2,1)S(1)} %get-tuple-element.63), channel_id=1, source_target_pairs={{0,4},{2,6},{4,0},{6,2},{8,12},{10,14},{12,8},{14,10},{16,20},{18,... | collective-permute-start | bytes 1572872 | tf_op jit(solution)/shard_map/ppermute | solution.py:477
  8.1 24.9 %collective-permute-start.2 = (bf16[2048,128]{1,0:T(8,128)(2,1)S(1)}, bf16[2048,128]{1,0:T(8,128)(2,1)}, u32[]{:S(2)}, u32[]{:S(2)}) collective-permute-start(bf16[2048,128]{1,0:T(8,128)(2,1)S(1)} %get-tuple-element.64), channel_id=1, source_target_pairs={{0,6},{2,4},{4,2},{6,0},{8,14},{10,12},{12,10},{14,8},{16,22},{18,... | collective-permute-start | bytes 1572872 | tf_op jit(solution)/shard_map/ppermute | solution.py:477
  12.0 0.8 copy-start.5
  12.8 32.2 %collective-permute-start.3 = (bf16[2048,128]{1,0:T(8,128)(2,1)}, bf16[2048,128]{1,0:T(8,128)(2,1)}, u32[]{:S(2)}, u32[]{:S(2)}) collective-permute-start(bf16[2048,128]{1,0:T(8,128)(2,1)} %get-tuple-element.67), channel_id=1, source_target_pairs={{0,2},{2,0},{4,6},{6,4},{8,10},{10,8},{12,14},{14,12},{16,18},{18,... | collective-permute-start | bytes 1572872 | tf_op jit(solution)/shard_map/ppermute | solution.py:477
  14.7 39.0 %collective-permute-start.4 = (bf16[2048,128]{1,0:T(8,128)(2,1)}, bf16[2048,128]{1,0:T(8,128)(2,1)}, u32[]{:S(2)}, u32[]{:S(2)}) collective-permute-start(bf16[2048,128]{1,0:T(8,128)(2,1)} %get-tuple-element.68), channel_id=1, source_target_pairs={{0,4},{2,6},{4,0},{6,2},{8,12},{10,14},{12,8},{14,10},{16,20},{18,... | collective-permute-start | bytes 1572872 | tf_op jit(solution)/shard_map/ppermute | solution.py:477
  19.3 3.0 %copy-start.10 = (bf16[2048,128]{1,0:T(8,128)(2,1)}, bf16[2048,128]{1,0:T(8,128)(2,1)S(1)}, u32[]{:S(2)}) copy-start(bf16[2048,128]{1,0:T(8,128)(2,1)S(1)} %collective-permute-done) | copy-start | bytes 1572868
  19.3 34.4 %collective-permute-start.5 = (bf16[2048,128]{1,0:T(8,128)(2,1)S(1)}, bf16[2048,128]{1,0:T(8,128)(2,1)}, u32[]{:S(2)}, u32[]{:S(2)}) collective-permute-start(bf16[2048,128]{1,0:T(8,128)(2,1)S(1)} %get-tuple-element.69), channel_id=1, source_target_pairs={{0,6},{2,4},{4,2},{6,0},{8,14},{10,12},{12,10},{14,8},{16,22},{18,... | collective-permute-start | bytes 1572872 | tf_op jit(solution)/shard_map/ppermute | solution.py:477
  25.2 0.8 copy-start.3
  26.0 6.1 %copy-start.15 = (s32[12,1024]{1,0:T(8,128)S(1)}, s32[12,1024]{1,0:T(8,128)}, u32[]{:S(2)}) copy-start(s32[12,1024]{1,0:T(8,128)} %param.5) | copy-start | bytes 147460
  53.8 51.6 %all-to-all-start = ((bf16[32,224,128]{2,1,0:T(8,128)(2,1)}), bf16[32,224,128]{2,1,0:T(8,128)(2,1)S(1)}, u32[]{:S(2)}, u32[]{:S(2)}) async-start(bf16[32,224,128]{2,1,0:T(8,128)(2,1)} %spectra.4), calls=%async_computation | async-start | bytes 3670016 | tf_op jit(solution)/shard_map/all_to_all | solution.py:499
  58.7 31.8 %collective-permute-start.6 = (bf16[2048,128]{1,0:T(8,128)(2,1)}, bf16[2048,128]{1,0:T(8,128)(2,1)S(1)}, u32[]{:S(2)}, u32[]{:S(2)}) collective-permute-start(bf16[2048,128]{1,0:T(8,128)(2,1)} %copy-done.9), channel_id=1, source_target_pairs={{0,2},{2,0},{4,6},{6,4},{8,10},{10,8},{12,14},{14,12},{16,18},{18,... | collective-permute-start | bytes 1572872 | tf_op jit(solution)/shard_map/ppermute | solution.py:477
  60.5 29.9 %collective-permute-start.7 = (bf16[2048,128]{1,0:T(8,128)(2,1)}, bf16[2048,128]{1,0:T(8,128)(2,1)S(1)}, u32[]{:S(2)}, u32[]{:S(2)}) collective-permute-start(bf16[2048,128]{1,0:T(8,128)(2,1)} %copy-done.8), channel_id=1, source_target_pairs={{0,4},{2,6},{4,0},{6,2},{8,12},{10,14},{12,8},{14,10},{16,20},{18,... | collective-permute-start | bytes 1572872 | tf_op jit(solution)/shard_map/ppermute | solution.py:477
  62.0 43.4 %collective-permute-start.8 = (bf16[2048,128]{1,0:T(8,128)(2,1)}, bf16[2048,128]{1,0:T(8,128)(2,1)}, u32[]{:S(2)}, u32[]{:S(2)}) collective-permute-start(bf16[2048,128]{1,0:T(8,128)(2,1)} %copy-done.7), channel_id=1, source_target_pairs={{0,6},{2,4},{4,2},{6,0},{8,14},{10,12},{12,10},{14,8},{16,22},{18,... | collective-permute-start | bytes 1572872 | tf_op jit(solution)/shard_map/ppermute | solution.py:477
  90.5 0.8 copy-start.11
  105.4 51.0 %all-to-all-start.1 = ((bf16[32,224,128]{2,1,0:T(8,128)(2,1)}), bf16[32,224,128]{2,1,0:T(8,128)(2,1)}, u32[]{:S(2)}, u32[]{:S(2)}) async-start(bf16[32,224,128]{2,1,0:T(8,128)(2,1)} %spectra.5), calls=%async_computation.1 | async-start | bytes 3670016 | tf_op jit(solution)/shard_map/all_to_all | solution.py:499
  110.0 31.5 %collective-permute-start.9 = (bf16[2048,128]{1,0:T(8,128)(2,1)S(1)}, bf16[2048,128]{1,0:T(8,128)(2,1)S(1)}, u32[]{:S(2)}, u32[]{:S(2)}) collective-permute-start(bf16[2048,128]{1,0:T(8,128)(2,1)S(1)} %get-tuple-element.103), channel_id=1, source_target_pairs={{0,2},{2,0},{4,6},{6,4},{8,10},{10,8},{12,14},{14,12},{16,18},{18,... | collective-permute-start | bytes 1572872 | tf_op jit(solution)/shard_map/ppermute | solution.py:477
  111.6 29.9 %collective-permute-start.10 = (bf16[2048,128]{1,0:T(8,128)(2,1)S(1)}, bf16[2048,128]{1,0:T(8,128)(2,1)S(1)}, u32[]{:S(2)}, u32[]{:S(2)}) collective-permute-start(bf16[2048,128]{1,0:T(8,128)(2,1)S(1)} %get-tuple-element.104), channel_id=1, source_target_pairs={{0,4},{2,6},{4,0},{6,2},{8,12},{10,14},{12,8},{14,10},{16,20},{18,... | collective-permute-start | bytes 1572872 | tf_op jit(solution)/shard_map/ppermute | solution.py:477
  113.1 43.3 %collective-permute-start.11 = (bf16[2048,128]{1,0:T(8,128)(2,1)S(1)}, bf16[2048,128]{1,0:T(8,128)(2,1)}, u32[]{:S(2)}, u32[]{:S(2)}) collective-permute-start(bf16[2048,128]{1,0:T(8,128)(2,1)S(1)} %get-tuple-element.105), channel_id=1, source_target_pairs={{0,6},{2,4},{4,2},{6,0},{8,14},{10,12},{12,10},{14,8},{16,22},{18,... | collective-permute-start | bytes 1572872 | tf_op jit(solution)/shard_map/ppermute | solution.py:477
  156.4 47.7 %all-to-all-start.2 = ((bf16[32,224,128]{2,1,0:T(8,128)(2,1)}), bf16[32,224,128]{2,1,0:T(8,128)(2,1)}, u32[]{:S(2)}, u32[]{:S(2)}) async-start(bf16[32,224,128]{2,1,0:T(8,128)(2,1)} %spectra.6), calls=%async_computation.2 | async-start | bytes 3670016 | tf_op jit(solution)/shard_map/all_to_all | solution.py:499
  204.1 47.4 %all-to-all-start.3 = ((bf16[32,224,128]{2,1,0:T(8,128)(2,1)}), bf16[32,224,128]{2,1,0:T(8,128)(2,1)}, u32[]{:S(2)}, u32[]{:S(2)}) async-start(bf16[32,224,128]{2,1,0:T(8,128)(2,1)} %spectra.7), calls=%async_computation.3 | async-start | bytes 3670016 | tf_op jit(solution)/shard_map/all_to_all | solution.py:499
  210.0 1.1 copy-start
  214.3 1.0 copy-start.1
  218.5 1.0 copy-start.2
  (8 other events, 6.3 us)

commit v5 on v4

--- a/solution.py
+++ b/solution.py
@@ -15,6 +15,9 @@
 PEERS = 4
 SUB = LANES // PEERS
 MIB = 1 << 20
+PITCH = 1
+PER_STEP = 4
+SORT_STEP = 2
 
 
 def dft_tables(fine, keep):
@@ -227,8 +230,8 @@
                 pltpu.VMEM((own, 2, step, LANES), jnp.float32),
                 pltpu.VMEM((2, 2 * (head_pairs + tail_pairs), 16, LANES), jnp.float32),
                 pltpu.VMEM((quads, RADIX * base, 2 * LANES), jnp.bfloat16),
-                pltpu.VMEM((keep * pitch, LANES), jnp.float32),
-                pltpu.VMEM((keep * tail_pairs + 16, LANES), jnp.float32),
+                pltpu.VMEM((keep * pitch + 64, LANES), jnp.float32),
+                pltpu.VMEM((keep * tail_pairs + 64, LANES), jnp.float32),
             ],
         ),
         out_shape=jax.ShapeDtypeStruct((dests, parts * (head_rows + tail_rows), LANES), jnp.bfloat16),
@@ -450,14 +453,6 @@
     )(*sorted_chunks, *([fresh, before] if last else []))
 
 
-PITCH = 1
-PER_STEP = 4
-SORT_STEP = 2
-FIRST = False
-WAIT = True
-TIES = [4, 4, 4]
-
-
 def per_device(voltages, taps):
     past, fine = taps.shape[0] - 1, taps.shape[1]
     frames = voltages.shape[1] // fine
@@ -481,7 +476,7 @@
     later = lax.optimization_barrier((place, packed[0]))[0]
     packed += [pack(voltages, later, h, fine) for h in range(1, chunks)]
     moved = [sent(packed[0], [])]
-    moved.append(sent(packed[1], [moved[0][1]] if FIRST else []))
+    moved.append(sent(packed[1], []))
     received = []
     for h in range(chunks):
         if h >= 2:
@@ -490,10 +485,9 @@
             moved[0][0], packed = lax.optimization_barrier((moved[0][0], packed))
         mine = spectra(moved[h], place, taps, tables, frames, dests, chan)
         if h + 2 < chunks:
-            moved.append(sent(packed[h + 2], [mine] if WAIT else []))
+            moved.append(sent(packed[h + 2], [mine]))
         if h + 1 < chunks:
-            k = TIES[h]
-            mine, moved[h + 1][1:k] = lax.optimization_barrier((mine, moved[h + 1][1:k]))
+            mine, moved[h + 1][1:] = lax.optimization_barrier((mine, moved[h + 1][1:]))
         if received:
             mine, received[-1] = lax.optimization_barrier((mine, received[-1]))
         received.append(lax.all_to_all(mine, ("tm", "inp"), split_axis=0, concat_axis=0, tiled=True))

time: 262 us -> 262 us (level)
  no operation moved by 1% of the time
where the time goes in v5:
time: 262 us; the launch traced here: 261 us
  waiting for transfers between devices  124 us (47%)
  Pallas kernels  88.4 us (34%)
  starting transfers between devices  36.3 us (14%)
  local copies, waits for them, and re-layouts  12.6 us (5%)
    ppermute x12, waiting for transfers between devices, sent(): lax.ppermute(pieces[k], 'tm', [(t, t ^ k) for t in range(n_time)])  70.5 us
    all_to_all x4, waiting for transfers between devices, per_device(): lax.all_to_all(mine, ('tm', 'inp'), split_axis=0, concat_axis=0, tiled=True)  53.1 us
    pallas_call x4, Pallas kernels, spectra(): pl.pallas_call(functools.partial(spectra_kernel, dims), grid_spec=pltpu.P...  48 us
    pallas_call x2, Pallas kernels, gram(): pl.pallas_call(functools.partial(gram_kernel, (here, chunks, cores, scale...  19.8 us
    all_to_all x4, starting transfers between devices, per_device(): lax.all_to_all(mine, ('tm', 'inp'), split_axis=0, concat_axis=0, tiled=True)  18.2 us
    ppermute x12, starting transfers between devices, sent(): lax.ppermute(pieces[k], 'tm', [(t, t ^ k) for t in range(n_time)])  18.1 us
    pallas_call x4, Pallas kernels, pack(): pl.pallas_call(functools.partial(pack_kernel, chunk), in_specs=[pl.BlockS...  12.4 us
    unnamed x32, local copies, waits for them, and re-layouts  11.7 us
  transfers between devices with their start and end apart: 16, of which 8 were waited for; matrix products, arithmetic and copies ran while one was open for 0% of the time, Pallas kernels for 29%

profile of v5, /device:TPU:0, one launch (start us, length us, event | category | flops | bytes accessed | tf_op | source)
XLA Modules:
  0.0 261.4 jit_solution(8041125679344624004)
XLA Ops:
  3.6 2.9 %collective-permute-start = (bf16[2048,128]{1,0:T(8,128)(2,1)S(1)}, bf16[2048,128]{1,0:T(8,128)(2,1)S(1)}, u32[]{:S(2)}, u32[]{:S(2)}) collective-permute-start(bf16[2048,128]{1,0:T(8,128)(2,1)S(1)} %get-tuple-element.62), channel_id=1, source_target_pairs={{0,2},{2,0},{4,6},{6,4},{8,10},{10,8},{12,14},{14,12},{16,18},{18,... | collective-permute-start | bytes 1572872 | tf_op jit(solution)/shard_map/ppermute | solution.py:472
  8.1 3.9 %pack.5 = (bf16[2048,128]{1,0:T(8,128)(2,1)S(1)}, bf16[2048,128]{1,0:T(8,128)(2,1)}, bf16[2048,128]{1,0:T(8,128)(2,1)}, bf16[2048,128]{1,0:T(8,128)(2,1)S(1)}) custom-call(s32[1]{0:T(128)} %bitcast.place, bf16[2,4,2,512,512]{4,3,2,1,0:T(8,128)(2,1)} %bitcast.26), custom_call_target="tpu_custom_call" | custom-call | tf_op jit(solution)/shard_map/pack/pallas_call | solution.py:87
  16.3 3.1 %collective-permute-done = bf16[2048,128]{1,0:T(8,128)(2,1)S(1)} collective-permute-done((bf16[2048,128]{1,0:T(8,128)(2,1)S(1)}, bf16[2048,128]{1,0:T(8,128)(2,1)S(1)}, u32[]{:S(2)}, u32[]{:S(2)}) %collective-permute-start) | collective-permute-done | bytes 524320 | tf_op jit(solution)/shard_map/ppermute | solution.py:472
  19.3 3.0 %collective-permute-start.5 = (bf16[2048,128]{1,0:T(8,128)(2,1)S(1)}, bf16[2048,128]{1,0:T(8,128)(2,1)}, u32[]{:S(2)}, u32[]{:S(2)}) collective-permute-start(bf16[2048,128]{1,0:T(8,128)(2,1)S(1)} %get-tuple-element.69), channel_id=1, source_target_pairs={{0,6},{2,4},{4,2},{6,0},{8,14},{10,12},{12,10},{14,8},{16,22},{18,... | collective-permute-start | bytes 1572872 | tf_op jit(solution)/shard_map/ppermute | solution.py:472
  26.0 2.9 %pack.6 = (bf16[2048,128]{1,0:T(8,128)(2,1)S(1)}, bf16[2048,128]{1,0:T(8,128)(2,1)S(1)}, bf16[2048,128]{1,0:T(8,128)(2,1)S(1)}, bf16[2048,128]{1,0:T(8,128)(2,1)S(1)}) custom-call(s32[1]{0:T(128)} %bitcast.place, bf16[2,4,2,512,512]{4,3,2,1,0:T(8,128)(2,1)} %bitcast.28), custom_call_target="tpu_custom_call" | custom-call | tf_op jit(solution)/shard_map/pack/pallas_call | solution.py:87
  33.0 12.0 %spectra.4 = bf16[32,224,128]{2,1,0:T(8,128)(2,1)} custom-call(s32[1]{0:T(128)} %bitcast.place, bf16[4,2,256,128]{3,2,1,0:T(8,128)(2,1)} %bitcast.24, bf16[4,2,256,128]{3,2,1,0:T(8,128)(2,1)} %bitcast.29, bf16[4,2,256,128]{3,2,1,0:T(8,128)(2,1)} %bitcast.4.refs_2_, bf16[4,2,256,128]{3,2,1,0:T(8,128)(2,1)} %bitcast.5.refs_3_, f32[2,256,24]{2,1,0:T(8,128)} %copy.8.refs_4_, ...), custom_call_target="tpu_custom_call" | custom-call | tf_op jit(solution)/shard_map/spectra/pallas_call | solution.py:219
  45.1 8.7 %collective-permute-done.4 = bf16[2048,128]{1,0:T(8,128)(2,1)} collective-permute-done((bf16[2048,128]{1,0:T(8,128)(2,1)}, bf16[2048,128]{1,0:T(8,128)(2,1)}, u32[]{:S(2)}, u32[]{:S(2)}) %collective-permute-start.4) | collective-permute-done | bytes 524320 | tf_op jit(solution)/shard_map/ppermute | solution.py:472
  53.8 4.9 %all-to-all-start = ((bf16[32,224,128]{2,1,0:T(8,128)(2,1)}), bf16[32,224,128]{2,1,0:T(8,128)(2,1)S(1)}, u32[]{:S(2)}, u32[]{:S(2)}) async-start(bf16[32,224,128]{2,1,0:T(8,128)(2,1)} %spectra.4), calls=%async_computation | async-start | bytes 3670016 | tf_op jit(solution)/shard_map/all_to_all | solution.py:493
  62.3 12.0 %spectra.5 = bf16[32,224,128]{2,1,0:T(8,128)(2,1)} custom-call(s32[1]{0:T(128)} %bitcast.place, bf16[4,2,256,128]{3,2,1,0:T(8,128)(2,1)} %bitcast.23, bf16[4,2,256,128]{3,2,1,0:T(8,128)(2,1)} %bitcast.9.refs_1_, bf16[4,2,256,128]{3,2,1,0:T(8,128)(2,1)} %bitcast.10.refs_2_, bf16[4,2,256,128]{3,2,1,0:T(8,128)(2,1)} %bitcast.11.refs_3_, ...), custom_call_target="tpu_custom_call" | custom-call | tf_op jit(solution)/shard_map/spectra/pallas_call | solution.py:219
  74.3 16.2 %collective-permute-done.6 = bf16[2048,128]{1,0:T(8,128)(2,1)S(1)} collective-permute-done((bf16[2048,128]{1,0:T(8,128)(2,1)}, bf16[2048,128]{1,0:T(8,128)(2,1)S(1)}, u32[]{:S(2)}, u32[]{:S(2)}) %collective-permute-start.6) | collective-permute-done | bytes 524320 | tf_op jit(solution)/shard_map/ppermute | solution.py:472
  92.1 13.3 %collective-permute-done.8 = bf16[2048,128]{1,0:T(8,128)(2,1)} collective-permute-done((bf16[2048,128]{1,0:T(8,128)(2,1)}, bf16[2048,128]{1,0:T(8,128)(2,1)}, u32[]{:S(2)}, u32[]{:S(2)}) %collective-permute-start.8) | collective-permute-done | bytes 524320 | tf_op jit(solution)/shard_map/ppermute | solution.py:472
  105.4 4.6 %all-to-all-start.1 = ((bf16[32,224,128]{2,1,0:T(8,128)(2,1)}), bf16[32,224,128]{2,1,0:T(8,128)(2,1)}, u32[]{:S(2)}, u32[]{:S(2)}) async-start(bf16[32,224,128]{2,1,0:T(8,128)(2,1)} %spectra.5), calls=%async_computation.1 | async-start | bytes 3670016 | tf_op jit(solution)/shard_map/all_to_all | solution.py:493
  113.6 12.0 %spectra.6 = bf16[32,224,128]{2,1,0:T(8,128)(2,1)} custom-call(s32[1]{0:T(128)} %bitcast.place, bf16[4,2,256,128]{3,2,1,0:T(8,128)(2,1)} %bitcast.22, bf16[4,2,256,128]{3,2,1,0:T(8,128)(2,1)} %bitcast.30, bf16[4,2,256,128]{3,2,1,0:T(8,128)(2,1)} %bitcast.31, bf16[4,2,256,128]{3,2,1,0:T(8,128)(2,1)} %bitcast.15.refs_3_, f32[2,256,24]{2,1,0:T(8,128)} %copy.8.refs_4_, ...), custom_call_target="tpu_custom_call" | custom-call | tf_op jit(solution)/shard_map/spectra/pallas_call | solution.py:219
  125.6 15.9 %collective-permute-done.9 = bf16[2048,128]{1,0:T(8,128)(2,1)S(1)} collective-permute-done((bf16[2048,128]{1,0:T(8,128)(2,1)S(1)}, bf16[2048,128]{1,0:T(8,128)(2,1)S(1)}, u32[]{:S(2)}, u32[]{:S(2)}) %collective-permute-start.9) | collective-permute-done | bytes 524320 | tf_op jit(solution)/shard_map/ppermute | solution.py:472
  143.1 13.3 %collective-permute-done.11 = bf16[2048,128]{1,0:T(8,128)(2,1)} collective-permute-done((bf16[2048,128]{1,0:T(8,128)(2,1)S(1)}, bf16[2048,128]{1,0:T(8,128)(2,1)}, u32[]{:S(2)}, u32[]{:S(2)}) %collective-permute-start.11) | collective-permute-done | bytes 524320 | tf_op jit(solution)/shard_map/ppermute | solution.py:472
  156.4 4.5 %all-to-all-start.2 = ((bf16[32,224,128]{2,1,0:T(8,128)(2,1)}), bf16[32,224,128]{2,1,0:T(8,128)(2,1)}, u32[]{:S(2)}, u32[]{:S(2)}) async-start(bf16[32,224,128]{2,1,0:T(8,128)(2,1)} %spectra.6), calls=%async_computation.2 | async-start | bytes 3670016 | tf_op jit(solution)/shard_map/all_to_all | solution.py:493
  160.9 12.0 %spectra.7 = bf16[32,224,128]{2,1,0:T(8,128)(2,1)} custom-call(s32[1]{0:T(128)} %bitcast.place, bf16[4,2,256,128]{3,2,1,0:T(8,128)(2,1)} %bitcast.21, bf16[4,2,256,128]{3,2,1,0:T(8,128)(2,1)} %bitcast.32, bf16[4,2,256,128]{3,2,1,0:T(8,128)(2,1)} %bitcast.33, bf16[4,2,256,128]{3,2,1,0:T(8,128)(2,1)} %bitcast.19.refs_3_, f32[2,256,24]{2,1,0:T(8,128)} %copy.8.refs_4_, ...), custom_call_target="tpu_custom_call" | custom-call | tf_op jit(solution)/shard_map/spectra/pallas_call | solution.py:219
  172.9 31.2 %all-to-all-done.2.source = bf16[32,224,128]{2,1,0:T(8,128)(2,1)} async-done(((bf16[32,224,128]{2,1,0:T(8,128)(2,1)}), bf16[32,224,128]{2,1,0:T(8,128)(2,1)}, u32[]{:S(2)}, u32[]{:S(2)}) %all-to-all-start.2) | async-done | bytes 1835040 | tf_op jit(solution)/shard_map/all_to_all | solution.py:493
  204.1 4.1 %all-to-all-start.3 = ((bf16[32,224,128]{2,1,0:T(8,128)(2,1)}), bf16[32,224,128]{2,1,0:T(8,128)(2,1)}, u32[]{:S(2)}, u32[]{:S(2)}) async-start(bf16[32,224,128]{2,1,0:T(8,128)(2,1)} %spectra.7), calls=%async_computation.3 | async-start | bytes 3670016 | tf_op jit(solution)/shard_map/all_to_all | solution.py:493
  211.1 3.2 %sort.4.refs_1_ = bf16[16,128,256]{2,1,0:T(8,128)(2,1)S(1)} custom-call(bf16[32,224,128]{2,1,0:T(8,128)(2,1)} %all-to-all-done.1.source), custom_call_target="tpu_custom_call" | custom-call | tf_op jit(solution)/shard_map/sort/pallas_call | solution.py:288
  215.3 3.2 %sort.5.refs_2_ = bf16[16,128,256]{2,1,0:T(8,128)(2,1)S(1)} custom-call(bf16[32,224,128]{2,1,0:T(8,128)(2,1)} %all-to-all-done.2.source), custom_call_target="tpu_custom_call" | custom-call | tf_op jit(solution)/shard_map/sort/pallas_call | solution.py:288
  219.5 10.0 %gram_first.1.refs_4_ = bf16[16,1024,1024]{2,1,0:T(8,128)(2,1)} custom-call(bf16[16,128,256]{2,1,0:T(8,128)(2,1)} %copy-done, bf16[16,128,256]{2,1,0:T(8,128)(2,1)} %copy-done.1, bf16[16,128,256]{2,1,0:T(8,128)(2,1)} %copy-done.2), custom_call_target="tpu_custom_call" | custom-call | tf_op jit(solution)/shard_map/gram_first/pallas_call | solution.py:434
  229.5 21.9 %all-to-all-done.3.refs_3_ = bf16[32,224,128]{2,1,0:T(8,128)(2,1)} async-done(((bf16[32,224,128]{2,1,0:T(8,128)(2,1)}), bf16[32,224,128]{2,1,0:T(8,128)(2,1)}, u32[]{:S(2)}, u32[]{:S(2)}) %all-to-all-start.3) | async-done | bytes 1835040 | tf_op jit(solution)/shard_map/all_to_all | solution.py:493
  251.4 9.8 %gram_last.1 = bf16[16,1024,1024]{2,1,0:T(8,128)(2,1)} custom-call(bf16[16,128,256]{2,1,0:T(8,128)(2,1)} %copy-done, bf16[16,128,256]{2,1,0:T(8,128)(2,1)} %copy-done.1, bf16[16,128,256]{2,1,0:T(8,128)(2,1)} %copy-done.2, bf16[32,224,128]{2,1,0:T(8,128)(2,1)} %all-to-all-done.3.refs_3_, ...), custom_call_target="tpu_custom_call", output_to_operand_aliasing={{}: (4, {})} | custom-call | tf_op jit(solution)/shard_map/gram_last/pallas_call | solution.py:434
  (57 shorter events, 32.2 us)
Async XLA Ops:
  3.6 15.7 %collective-permute-start = (bf16[2048,128]{1,0:T(8,128)(2,1)S(1)}, bf16[2048,128]{1,0:T(8,128)(2,1)S(1)}, u32[]{:S(2)}, u32[]{:S(2)}) collective-permute-start(bf16[2048,128]{1,0:T(8,128)(2,1)S(1)} %get-tuple-element.62), channel_id=1, source_target_pairs={{0,2},{2,0},{4,6},{6,4},{8,10},{10,8},{12,14},{14,12},{16,18},{18,... | collective-permute-start | bytes 1572872 | tf_op jit(solution)/shard_map/ppermute | solution.py:472
  6.6 26.5 %collective-permute-start.1 = (bf16[2048,128]{1,0:T(8,128)(2,1)S(1)}, bf16[2048,128]{1,0:T(8,128)(2,1)}, u32[]{:S(2)}, u32[]{:S(2)}) collective-permute-start(bf16[2048,128]{1,0:T(8,128)(2,1)S(1)} %get-tuple-element.63), channel_id=1, source_target_pairs={{0,4},{2,6},{4,0},{6,2},{8,12},{10,14},{12,8},{14,10},{16,20},{18,... | collective-permute-start | bytes 1572872 | tf_op jit(solution)/shard_map/ppermute | solution.py:472
  8.1 24.9 %collective-permute-start.2 = (bf16[2048,128]{1,0:T(8,128)(2,1)S(1)}, bf16[2048,128]{1,0:T(8,128)(2,1)}, u32[]{:S(2)}, u32[]{:S(2)}) collective-permute-start(bf16[2048,128]{1,0:T(8,128)(2,1)S(1)} %get-tuple-element.64), channel_id=1, source_target_pairs={{0,6},{2,4},{4,2},{6,0},{8,14},{10,12},{12,10},{14,8},{16,22},{18,... | collective-permute-start | bytes 1572872 | tf_op jit(solution)/shard_map/ppermute | solution.py:472
  12.0 0.8 copy-start.5
  12.8 32.3 %collective-permute-start.3 = (bf16[2048,128]{1,0:T(8,128)(2,1)}, bf16[2048,128]{1,0:T(8,128)(2,1)}, u32[]{:S(2)}, u32[]{:S(2)}) collective-permute-start(bf16[2048,128]{1,0:T(8,128)(2,1)} %get-tuple-element.67), channel_id=1, source_target_pairs={{0,2},{2,0},{4,6},{6,4},{8,10},{10,8},{12,14},{14,12},{16,18},{18,... | collective-permute-start | bytes 1572872 | tf_op jit(solution)/shard_map/ppermute | solution.py:472
  14.7 39.0 %collective-permute-start.4 = (bf16[2048,128]{1,0:T(8,128)(2,1)}, bf16[2048,128]{1,0:T(8,128)(2,1)}, u32[]{:S(2)}, u32[]{:S(2)}) collective-permute-start(bf16[2048,128]{1,0:T(8,128)(2,1)} %get-tuple-element.68), channel_id=1, source_target_pairs={{0,4},{2,6},{4,0},{6,2},{8,12},{10,14},{12,8},{14,10},{16,20},{18,... | collective-permute-start | bytes 1572872 | tf_op jit(solution)/shard_map/ppermute | solution.py:472
  19.3 3.0 %copy-start.10 = (bf16[2048,128]{1,0:T(8,128)(2,1)}, bf16[2048,128]{1,0:T(8,128)(2,1)S(1)}, u32[]{:S(2)}) copy-start(bf16[2048,128]{1,0:T(8,128)(2,1)S(1)} %collective-permute-done) | copy-start | bytes 1572868
  19.3 34.4 %collective-permute-start.5 = (bf16[2048,128]{1,0:T(8,128)(2,1)S(1)}, bf16[2048,128]{1,0:T(8,128)(2,1)}, u32[]{:S(2)}, u32[]{:S(2)}) collective-permute-start(bf16[2048,128]{1,0:T(8,128)(2,1)S(1)} %get-tuple-element.69), channel_id=1, source_target_pairs={{0,6},{2,4},{4,2},{6,0},{8,14},{10,12},{12,10},{14,8},{16,22},{18,... | collective-permute-start | bytes 1572872 | tf_op jit(solution)/shard_map/ppermute | solution.py:472
  25.2 0.8 copy-start.3
  26.0 6.1 %copy-start.15 = (s32[12,1024]{1,0:T(8,128)S(1)}, s32[12,1024]{1,0:T(8,128)}, u32[]{:S(2)}) copy-start(s32[12,1024]{1,0:T(8,128)} %param.5) | copy-start | bytes 147460
  53.8 51.6 %all-to-all-start = ((bf16[32,224,128]{2,1,0:T(8,128)(2,1)}), bf16[32,224,128]{2,1,0:T(8,128)(2,1)S(1)}, u32[]{:S(2)}, u32[]{:S(2)}) async-start(bf16[32,224,128]{2,1,0:T(8,128)(2,1)} %spectra.4), calls=%async_computation | async-start | bytes 3670016 | tf_op jit(solution)/shard_map/all_to_all | solution.py:493
  58.7 31.8 %collective-permute-start.6 = (bf16[2048,128]{1,0:T(8,128)(2,1)}, bf16[2048,128]{1,0:T(8,128)(2,1)S(1)}, u32[]{:S(2)}, u32[]{:S(2)}) collective-permute-start(bf16[2048,128]{1,0:T(8,128)(2,1)} %copy-done.9), channel_id=1, source_target_pairs={{0,2},{2,0},{4,6},{6,4},{8,10},{10,8},{12,14},{14,12},{16,18},{18,... | collective-permute-start | bytes 1572872 | tf_op jit(solution)/shard_map/ppermute | solution.py:472
  60.5 29.9 %collective-permute-start.7 = (bf16[2048,128]{1,0:T(8,128)(2,1)}, bf16[2048,128]{1,0:T(8,128)(2,1)S(1)}, u32[]{:S(2)}, u32[]{:S(2)}) collective-permute-start(bf16[2048,128]{1,0:T(8,128)(2,1)} %copy-done.8), channel_id=1, source_target_pairs={{0,4},{2,6},{4,0},{6,2},{8,12},{10,14},{12,8},{14,10},{16,20},{18,... | collective-permute-start | bytes 1572872 | tf_op jit(solution)/shard_map/ppermute | solution.py:472
  62.0 43.4 %collective-permute-start.8 = (bf16[2048,128]{1,0:T(8,128)(2,1)}, bf16[2048,128]{1,0:T(8,128)(2,1)}, u32[]{:S(2)}, u32[]{:S(2)}) collective-permute-start(bf16[2048,128]{1,0:T(8,128)(2,1)} %copy-done.7), channel_id=1, source_target_pairs={{0,6},{2,4},{4,2},{6,0},{8,14},{10,12},{12,10},{14,8},{16,22},{18,... | collective-permute-start | bytes 1572872 | tf_op jit(solution)/shard_map/ppermute | solution.py:472
  90.5 0.8 copy-start.11
  105.4 51.0 %all-to-all-start.1 = ((bf16[32,224,128]{2,1,0:T(8,128)(2,1)}), bf16[32,224,128]{2,1,0:T(8,128)(2,1)}, u32[]{:S(2)}, u32[]{:S(2)}) async-start(bf16[32,224,128]{2,1,0:T(8,128)(2,1)} %spectra.5), calls=%async_computation.1 | async-start | bytes 3670016 | tf_op jit(solution)/shard_map/all_to_all | solution.py:493
  110.0 31.5 %collective-permute-start.9 = (bf16[2048,128]{1,0:T(8,128)(2,1)S(1)}, bf16[2048,128]{1,0:T(8,128)(2,1)S(1)}, u32[]{:S(2)}, u32[]{:S(2)}) collective-permute-start(bf16[2048,128]{1,0:T(8,128)(2,1)S(1)} %get-tuple-element.103), channel_id=1, source_target_pairs={{0,2},{2,0},{4,6},{6,4},{8,10},{10,8},{12,14},{14,12},{16,18},{18,... | collective-permute-start | bytes 1572872 | tf_op jit(solution)/shard_map/ppermute | solution.py:472
  111.6 29.9 %collective-permute-start.10 = (bf16[2048,128]{1,0:T(8,128)(2,1)S(1)}, bf16[2048,128]{1,0:T(8,128)(2,1)S(1)}, u32[]{:S(2)}, u32[]{:S(2)}) collective-permute-start(bf16[2048,128]{1,0:T(8,128)(2,1)S(1)} %get-tuple-element.104), channel_id=1, source_target_pairs={{0,4},{2,6},{4,0},{6,2},{8,12},{10,14},{12,8},{14,10},{16,20},{18,... | collective-permute-start | bytes 1572872 | tf_op jit(solution)/shard_map/ppermute | solution.py:472
  113.1 43.3 %collective-permute-start.11 = (bf16[2048,128]{1,0:T(8,128)(2,1)S(1)}, bf16[2048,128]{1,0:T(8,128)(2,1)}, u32[]{:S(2)}, u32[]{:S(2)}) collective-permute-start(bf16[2048,128]{1,0:T(8,128)(2,1)S(1)} %get-tuple-element.105), channel_id=1, source_target_pairs={{0,6},{2,4},{4,2},{6,0},{8,14},{10,12},{12,10},{14,8},{16,22},{18,... | collective-permute-start | bytes 1572872 | tf_op jit(solution)/shard_map/ppermute | solution.py:472
  156.4 47.7 %all-to-all-start.2 = ((bf16[32,224,128]{2,1,0:T(8,128)(2,1)}), bf16[32,224,128]{2,1,0:T(8,128)(2,1)}, u32[]{:S(2)}, u32[]{:S(2)}) async-start(bf16[32,224,128]{2,1,0:T(8,128)(2,1)} %spectra.6), calls=%async_computation.2 | async-start | bytes 3670016 | tf_op jit(solution)/shard_map/all_to_all | solution.py:493
  204.1 47.4 %all-to-all-start.3 = ((bf16[32,224,128]{2,1,0:T(8,128)(2,1)}), bf16[32,224,128]{2,1,0:T(8,128)(2,1)}, u32[]{:S(2)}, u32[]{:S(2)}) async-start(bf16[32,224,128]{2,1,0:T(8,128)(2,1)} %spectra.7), calls=%async_computation.3 | async-start | bytes 3670016 | tf_op jit(solution)/shard_map/all_to_all | solution.py:493
  210.0 1.1 copy-start
  214.3 1.0 copy-start.1
  218.5 1.0 copy-start.2
  (8 other events, 6.3 us)

commit v6 on v5

--- a/solution.py
+++ b/solution.py
@@ -306,7 +306,6 @@
     width = here * LANES
     at, steps = pl.program_id(0), pl.num_programs(0)
     slot = at % 2
-    exact = math.frexp(scale)[0] == 0.5
 
     def copies(step, channels=None):
         half = step % 2
@@ -362,11 +361,11 @@
 
     def left(e, lo, hi):
         value = stacked[e, :, lo:hi].T
-        return value * jnp.bfloat16(scale) if exact else value
+        return value
 
     def product(rows, value):
         value = jnp.dot(rows, value, preferred_element_type=jnp.float32)
-        return value if exact else value * scale
+        return value if scale == 1.0 else value * scale
 
     def narrow(value):
         return value.astype(jnp.bfloat16)
@@ -462,15 +461,19 @@
     chan = KEEP // dests
     own = PEERS * frames
     place = jnp.bitwise_and(lax.axis_index("tm"), PEERS - 1).astype(jnp.int32)[None]
-    tables = [jnp.asarray(table.astype(jnp.bfloat16)) for table in dft_tables(fine, KEEP)]
-
     planes, scale = n_time // PEERS, 1.0 / (n_time * frames)
+    root = math.sqrt(scale)
+    if math.frexp(root)[0] != 0.5:
+        root = 1.0
+    scale /= root * root
+    tables = [jnp.asarray((table * root).astype(jnp.bfloat16)) for table in dft_tables(fine, KEEP)]
+
 
     def sent(pieces, after):
         if after:
             pieces = lax.optimization_barrier((pieces, after))[0]
-        others = [lax.ppermute(pieces[k], "tm", [(t, t ^ k) for t in range(n_time)]) for k in range(1, PEERS)]
-        return [pieces[0], *others]
+        others = {k: lax.ppermute(pieces[k], "tm", [(t, t ^ k) for t in range(n_time)]) for k in range(PEERS - 1, 0, -1)}
+        return [pieces[0], *(others[k] for k in range(1, PEERS))]
 
     packed = [pack(voltages, place, 0, fine)]
     later = lax.optimization_barrier((place, packed[0]))[0]

time: 262 us -> 262 us (level)
  no operation moved by 1% of the time
where the time goes in v6:
time: 262 us; the launch traced here: 261 us
  waiting for transfers between devices  124 us (47%)
  Pallas kernels  88.4 us (34%)
  starting transfers between devices  36.3 us (14%)
  local copies, waits for them, and re-layouts  12.6 us (5%)
    ppermute x12, waiting for transfers between devices, sent(): lax.ppermute(pieces[k], 'tm', [(t, t ^ k) for t in range(n_time)])  70.5 us
    all_to_all x4, waiting for transfers between devices, per_device(): lax.all_to_all(mine, ('tm', 'inp'), split_axis=0, concat_axis=0, tiled=True)  53.1 us
    pallas_call x4, Pallas kernels, spectra(): pl.pallas_call(functools.partial(spectra_kernel, dims), grid_spec=pltpu.P...  48 us
    pallas_call x2, Pallas kernels, gram(): pl.pallas_call(functools.partial(gram_kernel, (here, chunks, cores, scale...  19.8 us
    all_to_all x4, starting transfers between devices, per_device(): lax.all_to_all(mine, ('tm', 'inp'), split_axis=0, concat_axis=0, tiled=True)  18.2 us
    ppermute x12, starting transfers between devices, sent(): lax.ppermute(pieces[k], 'tm', [(t, t ^ k) for t in range(n_time)])  18.1 us
    pallas_call x4, Pallas kernels, pack(): pl.pallas_call(functools.partial(pack_kernel, chunk), in_specs=[pl.BlockS...  12.4 us
    unnamed x32, local copies, waits for them, and re-layouts  11.7 us
  transfers between devices with their start and end apart: 16, of which 8 were waited for; matrix products, arithmetic and copies ran while one was open for 0% of the time, Pallas kernels for 29%

profile of v6, /device:TPU:0, one launch (start us, length us, event | category | flops | bytes accessed | tf_op | source)
XLA Modules:
  0.0 261.4 jit_solution(2410399096882152658)
XLA Ops:
  3.6 2.9 %collective-permute-start = (bf16[2048,128]{1,0:T(8,128)(2,1)S(1)}, bf16[2048,128]{1,0:T(8,128)(2,1)S(1)}, u32[]{:S(2)}, u32[]{:S(2)}) collective-permute-start(bf16[2048,128]{1,0:T(8,128)(2,1)S(1)} %get-tuple-element.62), channel_id=1, source_target_pairs={{0,2},{2,0},{4,6},{6,4},{8,10},{10,8},{12,14},{14,12},{16,18},{18,... | collective-permute-start | bytes 1572872 | tf_op jit(solution)/shard_map/ppermute | solution.py:475
  8.1 3.9 %pack.5 = (bf16[2048,128]{1,0:T(8,128)(2,1)S(1)}, bf16[2048,128]{1,0:T(8,128)(2,1)}, bf16[2048,128]{1,0:T(8,128)(2,1)}, bf16[2048,128]{1,0:T(8,128)(2,1)S(1)}) custom-call(s32[1]{0:T(128)} %bitcast.place, bf16[2,4,2,512,512]{4,3,2,1,0:T(8,128)(2,1)} %bitcast.26), custom_call_target="tpu_custom_call" | custom-call | tf_op jit(solution)/shard_map/pack/pallas_call | solution.py:87
  16.3 3.1 %collective-permute-done = bf16[2048,128]{1,0:T(8,128)(2,1)S(1)} collective-permute-done((bf16[2048,128]{1,0:T(8,128)(2,1)S(1)}, bf16[2048,128]{1,0:T(8,128)(2,1)S(1)}, u32[]{:S(2)}, u32[]{:S(2)}) %collective-permute-start) | collective-permute-done | bytes 524320 | tf_op jit(solution)/shard_map/ppermute | solution.py:475
  19.3 3.0 %collective-permute-start.5 = (bf16[2048,128]{1,0:T(8,128)(2,1)S(1)}, bf16[2048,128]{1,0:T(8,128)(2,1)}, u32[]{:S(2)}, u32[]{:S(2)}) collective-permute-start(bf16[2048,128]{1,0:T(8,128)(2,1)S(1)} %get-tuple-element.69), channel_id=1, source_target_pairs={{0,6},{2,4},{4,2},{6,0},{8,14},{10,12},{12,10},{14,8},{16,22},{18,... | collective-permute-start | bytes 1572872 | tf_op jit(solution)/shard_map/ppermute | solution.py:475
  26.0 2.9 %pack.6 = (bf16[2048,128]{1,0:T(8,128)(2,1)S(1)}, bf16[2048,128]{1,0:T(8,128)(2,1)S(1)}, bf16[2048,128]{1,0:T(8,128)(2,1)S(1)}, bf16[2048,128]{1,0:T(8,128)(2,1)S(1)}) custom-call(s32[1]{0:T(128)} %bitcast.place, bf16[2,4,2,512,512]{4,3,2,1,0:T(8,128)(2,1)} %bitcast.28), custom_call_target="tpu_custom_call" | custom-call | tf_op jit(solution)/shard_map/pack/pallas_call | solution.py:87
  33.0 12.0 %spectra.4 = bf16[32,224,128]{2,1,0:T(8,128)(2,1)} custom-call(s32[1]{0:T(128)} %bitcast.place, bf16[4,2,256,128]{3,2,1,0:T(8,128)(2,1)} %bitcast.24, bf16[4,2,256,128]{3,2,1,0:T(8,128)(2,1)} %bitcast.29, bf16[4,2,256,128]{3,2,1,0:T(8,128)(2,1)} %bitcast.4.refs_2_, bf16[4,2,256,128]{3,2,1,0:T(8,128)(2,1)} %bitcast.5.refs_3_, f32[2,256,24]{2,1,0:T(8,128)} %copy.8.refs_4_, ...), custom_call_target="tpu_custom_call" | custom-call | tf_op jit(solution)/shard_map/spectra/pallas_call | solution.py:219
  45.1 8.7 %collective-permute-done.4 = bf16[2048,128]{1,0:T(8,128)(2,1)} collective-permute-done((bf16[2048,128]{1,0:T(8,128)(2,1)}, bf16[2048,128]{1,0:T(8,128)(2,1)}, u32[]{:S(2)}, u32[]{:S(2)}) %collective-permute-start.4) | collective-permute-done | bytes 524320 | tf_op jit(solution)/shard_map/ppermute | solution.py:475
  53.8 4.9 %all-to-all-start = ((bf16[32,224,128]{2,1,0:T(8,128)(2,1)}), bf16[32,224,128]{2,1,0:T(8,128)(2,1)S(1)}, u32[]{:S(2)}, u32[]{:S(2)}) async-start(bf16[32,224,128]{2,1,0:T(8,128)(2,1)} %spectra.4), calls=%async_computation | async-start | bytes 3670016 | tf_op jit(solution)/shard_map/all_to_all | solution.py:496
  62.3 12.0 %spectra.5 = bf16[32,224,128]{2,1,0:T(8,128)(2,1)} custom-call(s32[1]{0:T(128)} %bitcast.place, bf16[4,2,256,128]{3,2,1,0:T(8,128)(2,1)} %bitcast.23, bf16[4,2,256,128]{3,2,1,0:T(8,128)(2,1)} %bitcast.9.refs_1_, bf16[4,2,256,128]{3,2,1,0:T(8,128)(2,1)} %bitcast.10.refs_2_, bf16[4,2,256,128]{3,2,1,0:T(8,128)(2,1)} %bitcast.11.refs_3_, ...), custom_call_target="tpu_custom_call" | custom-call | tf_op jit(solution)/shard_map/spectra/pallas_call | solution.py:219
  74.3 16.2 %collective-permute-done.6 = bf16[2048,128]{1,0:T(8,128)(2,1)S(1)} collective-permute-done((bf16[2048,128]{1,0:T(8,128)(2,1)}, bf16[2048,128]{1,0:T(8,128)(2,1)S(1)}, u32[]{:S(2)}, u32[]{:S(2)}) %collective-permute-start.6) | collective-permute-done | bytes 524320 | tf_op jit(solution)/shard_map/ppermute | solution.py:475
  92.1 13.3 %collective-permute-done.8 = bf16[2048,128]{1,0:T(8,128)(2,1)} collective-permute-done((bf16[2048,128]{1,0:T(8,128)(2,1)}, bf16[2048,128]{1,0:T(8,128)(2,1)}, u32[]{:S(2)}, u32[]{:S(2)}) %collective-permute-start.8) | collective-permute-done | bytes 524320 | tf_op jit(solution)/shard_map/ppermute | solution.py:475
  105.4 4.6 %all-to-all-start.1 = ((bf16[32,224,128]{2,1,0:T(8,128)(2,1)}), bf16[32,224,128]{2,1,0:T(8,128)(2,1)}, u32[]{:S(2)}, u32[]{:S(2)}) async-start(bf16[32,224,128]{2,1,0:T(8,128)(2,1)} %spectra.5), calls=%async_computation.1 | async-start | bytes 3670016 | tf_op jit(solution)/shard_map/all_to_all | solution.py:496
  113.6 12.0 %spectra.6 = bf16[32,224,128]{2,1,0:T(8,128)(2,1)} custom-call(s32[1]{0:T(128)} %bitcast.place, bf16[4,2,256,128]{3,2,1,0:T(8,128)(2,1)} %bitcast.22, bf16[4,2,256,128]{3,2,1,0:T(8,128)(2,1)} %bitcast.30, bf16[4,2,256,128]{3,2,1,0:T(8,128)(2,1)} %bitcast.31, bf16[4,2,256,128]{3,2,1,0:T(8,128)(2,1)} %bitcast.15.refs_3_, f32[2,256,24]{2,1,0:T(8,128)} %copy.8.refs_4_, ...), custom_call_target="tpu_custom_call" | custom-call | tf_op jit(solution)/shard_map/spectra/pallas_call | solution.py:219
  125.6 15.9 %collective-permute-done.9 = bf16[2048,128]{1,0:T(8,128)(2,1)S(1)} collective-permute-done((bf16[2048,128]{1,0:T(8,128)(2,1)S(1)}, bf16[2048,128]{1,0:T(8,128)(2,1)S(1)}, u32[]{:S(2)}, u32[]{:S(2)}) %collective-permute-start.9) | collective-permute-done | bytes 524320 | tf_op jit(solution)/shard_map/ppermute | solution.py:475
  143.1 13.3 %collective-permute-done.11 = bf16[2048,128]{1,0:T(8,128)(2,1)} collective-permute-done((bf16[2048,128]{1,0:T(8,128)(2,1)S(1)}, bf16[2048,128]{1,0:T(8,128)(2,1)}, u32[]{:S(2)}, u32[]{:S(2)}) %collective-permute-start.11) | collective-permute-done | bytes 524320 | tf_op jit(solution)/shard_map/ppermute | solution.py:475
  156.4 4.5 %all-to-all-start.2 = ((bf16[32,224,128]{2,1,0:T(8,128)(2,1)}), bf16[32,224,128]{2,1,0:T(8,128)(2,1)}, u32[]{:S(2)}, u32[]{:S(2)}) async-start(bf16[32,224,128]{2,1,0:T(8,128)(2,1)} %spectra.6), calls=%async_computation.2 | async-start | bytes 3670016 | tf_op jit(solution)/shard_map/all_to_all | solution.py:496
  160.9 12.0 %spectra.7 = bf16[32,224,128]{2,1,0:T(8,128)(2,1)} custom-call(s32[1]{0:T(128)} %bitcast.place, bf16[4,2,256,128]{3,2,1,0:T(8,128)(2,1)} %bitcast.21, bf16[4,2,256,128]{3,2,1,0:T(8,128)(2,1)} %bitcast.32, bf16[4,2,256,128]{3,2,1,0:T(8,128)(2,1)} %bitcast.33, bf16[4,2,256,128]{3,2,1,0:T(8,128)(2,1)} %bitcast.19.refs_3_, f32[2,256,24]{2,1,0:T(8,128)} %copy.8.refs_4_, ...), custom_call_target="tpu_custom_call" | custom-call | tf_op jit(solution)/shard_map/spectra/pallas_call | solution.py:219
  172.9 31.2 %all-to-all-done.2.source = bf16[32,224,128]{2,1,0:T(8,128)(2,1)} async-done(((bf16[32,224,128]{2,1,0:T(8,128)(2,1)}), bf16[32,224,128]{2,1,0:T(8,128)(2,1)}, u32[]{:S(2)}, u32[]{:S(2)}) %all-to-all-start.2) | async-done | bytes 1835040 | tf_op jit(solution)/shard_map/all_to_all | solution.py:496
  204.1 4.1 %all-to-all-start.3 = ((bf16[32,224,128]{2,1,0:T(8,128)(2,1)}), bf16[32,224,128]{2,1,0:T(8,128)(2,1)}, u32[]{:S(2)}, u32[]{:S(2)}) async-start(bf16[32,224,128]{2,1,0:T(8,128)(2,1)} %spectra.7), calls=%async_computation.3 | async-start | bytes 3670016 | tf_op jit(solution)/shard_map/all_to_all | solution.py:496
  211.1 3.2 %sort.4.refs_1_ = bf16[16,128,256]{2,1,0:T(8,128)(2,1)S(1)} custom-call(bf16[32,224,128]{2,1,0:T(8,128)(2,1)} %all-to-all-done.1.source), custom_call_target="tpu_custom_call" | custom-call | tf_op jit(solution)/shard_map/sort/pallas_call | solution.py:288
  215.3 3.2 %sort.5.refs_2_ = bf16[16,128,256]{2,1,0:T(8,128)(2,1)S(1)} custom-call(bf16[32,224,128]{2,1,0:T(8,128)(2,1)} %all-to-all-done.2.source), custom_call_target="tpu_custom_call" | custom-call | tf_op jit(solution)/shard_map/sort/pallas_call | solution.py:288
  219.5 10.0 %gram_first.1.refs_4_ = bf16[16,1024,1024]{2,1,0:T(8,128)(2,1)} custom-call(bf16[16,128,256]{2,1,0:T(8,128)(2,1)} %copy-done, bf16[16,128,256]{2,1,0:T(8,128)(2,1)} %copy-done.1, bf16[16,128,256]{2,1,0:T(8,128)(2,1)} %copy-done.2), custom_call_target="tpu_custom_call" | custom-call | tf_op jit(solution)/shard_map/gram_first/pallas_call | solution.py:433
  229.5 21.9 %all-to-all-done.3.refs_3_ = bf16[32,224,128]{2,1,0:T(8,128)(2,1)} async-done(((bf16[32,224,128]{2,1,0:T(8,128)(2,1)}), bf16[32,224,128]{2,1,0:T(8,128)(2,1)}, u32[]{:S(2)}, u32[]{:S(2)}) %all-to-all-start.3) | async-done | bytes 1835040 | tf_op jit(solution)/shard_map/all_to_all | solution.py:496
  251.4 9.8 %gram_last.1 = bf16[16,1024,1024]{2,1,0:T(8,128)(2,1)} custom-call(bf16[16,128,256]{2,1,0:T(8,128)(2,1)} %copy-done, bf16[16,128,256]{2,1,0:T(8,128)(2,1)} %copy-done.1, bf16[16,128,256]{2,1,0:T(8,128)(2,1)} %copy-done.2, bf16[32,224,128]{2,1,0:T(8,128)(2,1)} %all-to-all-done.3.refs_3_, ...), custom_call_target="tpu_custom_call", output_to_operand_aliasing={{}: (4, {})} | custom-call | tf_op jit(solution)/shard_map/gram_last/pallas_call | solution.py:433
  (57 shorter events, 32.2 us)
Async XLA Ops:
  3.6 15.7 %collective-permute-start = (bf16[2048,128]{1,0:T(8,128)(2,1)S(1)}, bf16[2048,128]{1,0:T(8,128)(2,1)S(1)}, u32[]{:S(2)}, u32[]{:S(2)}) collective-permute-start(bf16[2048,128]{1,0:T(8,128)(2,1)S(1)} %get-tuple-element.62), channel_id=1, source_target_pairs={{0,2},{2,0},{4,6},{6,4},{8,10},{10,8},{12,14},{14,12},{16,18},{18,... | collective-permute-start | bytes 1572872 | tf_op jit(solution)/shard_map/ppermute | solution.py:475
  6.6 26.5 %collective-permute-start.1 = (bf16[2048,128]{1,0:T(8,128)(2,1)S(1)}, bf16[2048,128]{1,0:T(8,128)(2,1)}, u32[]{:S(2)}, u32[]{:S(2)}) collective-permute-start(bf16[2048,128]{1,0:T(8,128)(2,1)S(1)} %get-tuple-element.63), channel_id=1, source_target_pairs={{0,4},{2,6},{4,0},{6,2},{8,12},{10,14},{12,8},{14,10},{16,20},{18,... | collective-permute-start | bytes 1572872 | tf_op jit(solution)/shard_map/ppermute | solution.py:475
  8.1 24.9 %collective-permute-start.2 = (bf16[2048,128]{1,0:T(8,128)(2,1)S(1)}, bf16[2048,128]{1,0:T(8,128)(2,1)}, u32[]{:S(2)}, u32[]{:S(2)}) collective-permute-start(bf16[2048,128]{1,0:T(8,128)(2,1)S(1)} %get-tuple-element.64), channel_id=1, source_target_pairs={{0,6},{2,4},{4,2},{6,0},{8,14},{10,12},{12,10},{14,8},{16,22},{18,... | collective-permute-start | bytes 1572872 | tf_op jit(solution)/shard_map/ppermute | solution.py:475
  12.0 0.8 copy-start.5
  12.8 32.3 %collective-permute-start.3 = (bf16[2048,128]{1,0:T(8,128)(2,1)}, bf16[2048,128]{1,0:T(8,128)(2,1)}, u32[]{:S(2)}, u32[]{:S(2)}) collective-permute-start(bf16[2048,128]{1,0:T(8,128)(2,1)} %get-tuple-element.67), channel_id=1, source_target_pairs={{0,2},{2,0},{4,6},{6,4},{8,10},{10,8},{12,14},{14,12},{16,18},{18,... | collective-permute-start | bytes 1572872 | tf_op jit(solution)/shard_map/ppermute | solution.py:475
  14.7 39.0 %collective-permute-start.4 = (bf16[2048,128]{1,0:T(8,128)(2,1)}, bf16[2048,128]{1,0:T(8,128)(2,1)}, u32[]{:S(2)}, u32[]{:S(2)}) collective-permute-start(bf16[2048,128]{1,0:T(8,128)(2,1)} %get-tuple-element.68), channel_id=1, source_target_pairs={{0,4},{2,6},{4,0},{6,2},{8,12},{10,14},{12,8},{14,10},{16,20},{18,... | collective-permute-start | bytes 1572872 | tf_op jit(solution)/shard_map/ppermute | solution.py:475
  19.3 3.0 %copy-start.10 = (bf16[2048,128]{1,0:T(8,128)(2,1)}, bf16[2048,128]{1,0:T(8,128)(2,1)S(1)}, u32[]{:S(2)}) copy-start(bf16[2048,128]{1,0:T(8,128)(2,1)S(1)} %collective-permute-done) | copy-start | bytes 1572868
  19.3 34.4 %collective-permute-start.5 = (bf16[2048,128]{1,0:T(8,128)(2,1)S(1)}, bf16[2048,128]{1,0:T(8,128)(2,1)}, u32[]{:S(2)}, u32[]{:S(2)}) collective-permute-start(bf16[2048,128]{1,0:T(8,128)(2,1)S(1)} %get-tuple-element.69), channel_id=1, source_target_pairs={{0,6},{2,4},{4,2},{6,0},{8,14},{10,12},{12,10},{14,8},{16,22},{18,... | collective-permute-start | bytes 1572872 | tf_op jit(solution)/shard_map/ppermute | solution.py:475
  25.2 0.8 copy-start.3
  26.0 6.1 %copy-start.15 = (s32[12,1024]{1,0:T(8,128)S(1)}, s32[12,1024]{1,0:T(8,128)}, u32[]{:S(2)}) copy-start(s32[12,1024]{1,0:T(8,128)} %param.5) | copy-start | bytes 147460
  53.8 51.6 %all-to-all-start = ((bf16[32,224,128]{2,1,0:T(8,128)(2,1)}), bf16[32,224,128]{2,1,0:T(8,128)(2,1)S(1)}, u32[]{:S(2)}, u32[]{:S(2)}) async-start(bf16[32,224,128]{2,1,0:T(8,128)(2,1)} %spectra.4), calls=%async_computation | async-start | bytes 3670016 | tf_op jit(solution)/shard_map/all_to_all | solution.py:496
  58.7 31.8 %collective-permute-start.6 = (bf16[2048,128]{1,0:T(8,128)(2,1)}, bf16[2048,128]{1,0:T(8,128)(2,1)S(1)}, u32[]{:S(2)}, u32[]{:S(2)}) collective-permute-start(bf16[2048,128]{1,0:T(8,128)(2,1)} %copy-done.9), channel_id=1, source_target_pairs={{0,2},{2,0},{4,6},{6,4},{8,10},{10,8},{12,14},{14,12},{16,18},{18,... | collective-permute-start | bytes 1572872 | tf_op jit(solution)/shard_map/ppermute | solution.py:475
  60.5 29.9 %collective-permute-start.7 = (bf16[2048,128]{1,0:T(8,128)(2,1)}, bf16[2048,128]{1,0:T(8,128)(2,1)S(1)}, u32[]{:S(2)}, u32[]{:S(2)}) collective-permute-start(bf16[2048,128]{1,0:T(8,128)(2,1)} %copy-done.8), channel_id=1, source_target_pairs={{0,4},{2,6},{4,0},{6,2},{8,12},{10,14},{12,8},{14,10},{16,20},{18,... | collective-permute-start | bytes 1572872 | tf_op jit(solution)/shard_map/ppermute | solution.py:475
  62.0 43.4 %collective-permute-start.8 = (bf16[2048,128]{1,0:T(8,128)(2,1)}, bf16[2048,128]{1,0:T(8,128)(2,1)}, u32[]{:S(2)}, u32[]{:S(2)}) collective-permute-start(bf16[2048,128]{1,0:T(8,128)(2,1)} %copy-done.7), channel_id=1, source_target_pairs={{0,6},{2,4},{4,2},{6,0},{8,14},{10,12},{12,10},{14,8},{16,22},{18,... | collective-permute-start | bytes 1572872 | tf_op jit(solution)/shard_map/ppermute | solution.py:475
  90.5 0.8 copy-start.11
  105.4 51.0 %all-to-all-start.1 = ((bf16[32,224,128]{2,1,0:T(8,128)(2,1)}), bf16[32,224,128]{2,1,0:T(8,128)(2,1)}, u32[]{:S(2)}, u32[]{:S(2)}) async-start(bf16[32,224,128]{2,1,0:T(8,128)(2,1)} %spectra.5), calls=%async_computation.1 | async-start | bytes 3670016 | tf_op jit(solution)/shard_map/all_to_all | solution.py:496
  110.0 31.5 %collective-permute-start.9 = (bf16[2048,128]{1,0:T(8,128)(2,1)S(1)}, bf16[2048,128]{1,0:T(8,128)(2,1)S(1)}, u32[]{:S(2)}, u32[]{:S(2)}) collective-permute-start(bf16[2048,128]{1,0:T(8,128)(2,1)S(1)} %get-tuple-element.103), channel_id=1, source_target_pairs={{0,2},{2,0},{4,6},{6,4},{8,10},{10,8},{12,14},{14,12},{16,18},{18,... | collective-permute-start | bytes 1572872 | tf_op jit(solution)/shard_map/ppermute | solution.py:475
  111.6 29.9 %collective-permute-start.10 = (bf16[2048,128]{1,0:T(8,128)(2,1)S(1)}, bf16[2048,128]{1,0:T(8,128)(2,1)S(1)}, u32[]{:S(2)}, u32[]{:S(2)}) collective-permute-start(bf16[2048,128]{1,0:T(8,128)(2,1)S(1)} %get-tuple-element.104), channel_id=1, source_target_pairs={{0,4},{2,6},{4,0},{6,2},{8,12},{10,14},{12,8},{14,10},{16,20},{18,... | collective-permute-start | bytes 1572872 | tf_op jit(solution)/shard_map/ppermute | solution.py:475
  113.1 43.3 %collective-permute-start.11 = (bf16[2048,128]{1,0:T(8,128)(2,1)S(1)}, bf16[2048,128]{1,0:T(8,128)(2,1)}, u32[]{:S(2)}, u32[]{:S(2)}) collective-permute-start(bf16[2048,128]{1,0:T(8,128)(2,1)S(1)} %get-tuple-element.105), channel_id=1, source_target_pairs={{0,6},{2,4},{4,2},{6,0},{8,14},{10,12},{12,10},{14,8},{16,22},{18,... | collective-permute-start | bytes 1572872 | tf_op jit(solution)/shard_map/ppermute | solution.py:475
  156.4 47.7 %all-to-all-start.2 = ((bf16[32,224,128]{2,1,0:T(8,128)(2,1)}), bf16[32,224,128]{2,1,0:T(8,128)(2,1)}, u32[]{:S(2)}, u32[]{:S(2)}) async-start(bf16[32,224,128]{2,1,0:T(8,128)(2,1)} %spectra.6), calls=%async_computation.2 | async-start | bytes 3670016 | tf_op jit(solution)/shard_map/all_to_all | solution.py:496
  204.1 47.4 %all-to-all-start.3 = ((bf16[32,224,128]{2,1,0:T(8,128)(2,1)}), bf16[32,224,128]{2,1,0:T(8,128)(2,1)}, u32[]{:S(2)}, u32[]{:S(2)}) async-start(bf16[32,224,128]{2,1,0:T(8,128)(2,1)} %spectra.7), calls=%async_computation.3 | async-start | bytes 3670016 | tf_op jit(solution)/shard_map/all_to_all | solution.py:496
  210.0 1.1 copy-start
  214.3 1.0 copy-start.1
  218.5 1.0 copy-start.2
  (8 other events, 6.3 us)
